TPU v7x, 32 devices: a whole 2x2x4 slice. The times are simulated.
32 devices in a mesh: sample: 4 (over z), expert: 8 (over y, x, core).
Axes of the slice: x: 2, y: 2, z: 4, core: 2. Of those that a mesh axis runs over, the one named last changes fastest.
Arguments:
- queries: bfloat16 [64, 4, 8192], P('expert', 'sample'), may hold values from -8 to 8
- prompt_kv: bfloat16 [64, 256, 1024], P('expert', 'sample'), may hold values from -8 to 8
- gen_kv: bfloat16 [64, 4, 32, 1024], P('expert', 'sample'), may hold values from -4 to 4
- gen_lengths: int32 [64, 4], P('expert', 'sample'), may hold values from 1 to 32, 64 in all within a row
- out_proj: bfloat16 [8192, 4096], P(None, 'sample'), may hold values from -1 to 1
- residual: bfloat16 [64, 4, 4096], P('expert', None, 'sample'), may hold values from -160 to 160
- norm_gain: float32 [4096], P('sample'), may hold values from 0.1 to 1.9
- w_gate_up: bfloat16 [24, 4096, 3072], P('expert', 'sample'), may hold values from -0.09375 to 0.09375
- w_down: bfloat16 [24, 1536, 4096], P('expert', None, 'sample'), may hold values from -0.15625 to 0.15625
- routes: int32 [64, 4, 8], P('expert'), may hold values from 0 to 23, all different within a row; in each aligned block of 32 rows (0 to 31, 32 to 63, ..., all dimensions but the last counted through in order) at most 13 rows name the same one
- route_probs: float32 [64, 4, 8], P('expert'), may hold values from 0.1 to 1
Outputs:
- mixed: bfloat16 [64, 4, 4096], P('expert', None, 'sample')
- expert_out: bfloat16 [64, 4, 4096], P('expert', None, 'sample')
Inputs may be any that keep to these rules, and one draw needn't show every extreme that they name: `gen_lengths`: in each prompt, at least one sample has 32 generated tokens. `routes`: each row names 8 different experts. Among the 32 rows of the prompts of one index of expert, no expert is named by more than 13 rows, a bound that some block reaches.
All inputs are finite; a program needn't handle non-finite values. No bound on the sum of `gen_lengths` on one device may be relied on, other than what follows from the above.
Results may differ from a plain program's by a relative error of at most 0.028.
Values may be sent and summed in bfloat16 or wider, within the bound.
No kernel may reach another device: no remote copies, remote signals or barrier semaphores. Data moves between devices by JAX's collectives and lax.ppermute only.
A program may use at most 128 MiB of HBM per device.

v0:
```python
import jax
import jax.numpy as jnp
from jax import lax
from jax.sharding import PartitionSpec as P

D = 4096
FF = 1536
QHEADS = 64
KVHEADS = 4
HDIM = 128
TOPK = 8
EXP_COL = 3


NEGATIVE = -1e30
EPSILON = 1e-06


def absorb(carried, scores, value_rows):
    highest = jnp.maximum(carried[0], jnp.max(scores, axis=-1))
    rescale = jnp.exp(carried[0] - highest)
    weights = jnp.exp(scores - highest[..., None])
    weight_sum = carried[1] * rescale + jnp.sum(weights, axis=-1)
    numerator = carried[2] * rescale[..., None] + jnp.einsum(
        "brhgn,bnhd->brhgd",
        weights,
        value_rows.astype(jnp.float32),
        precision=lax.Precision.HIGHEST,
    )
    return (highest, weight_sum, numerator)


def split_cache(cache):
    kv_width = KVHEADS * HDIM
    prompts_here = cache.shape[0]
    length = cache.shape[1]
    key_rows = cache[:, :, :kv_width].reshape(prompts_here, length, KVHEADS, HDIM)
    value_rows = cache[:, :, kv_width:].reshape(prompts_here, length, KVHEADS, HDIM)
    return (key_rows, value_rows)


def score_rows(query, key_rows):
    return jnp.einsum(
        "brhgd,bnhd->brhgn", query, key_rows, preferred_element_type=jnp.float32
    ) * HDIM ** (-0.5)


def empty_state(shape):
    return (
        jnp.full(shape, NEGATIVE, jnp.float32),
        jnp.zeros(shape, jnp.float32),
        jnp.zeros(shape + (HDIM,), jnp.float32),
    )


def on_device(
    queries,
    prompt_kv,
    gen_kv,
    gen_lengths,
    out_proj,
    residual,
    norm_gain,
    w_gate_up,
    w_down,
    routes,
    route_probs,
):
    prompts_here = queries.shape[0]
    groups = QHEADS // KVHEADS
    samples = lax.axis_size("sample")
    width = residual.shape[2]
    own_query = queries.reshape(prompts_here, 1, KVHEADS, groups, HDIM)
    gen_keys, gen_values = split_cache(gen_kv[:, 0])
    positions = jnp.arange(gen_kv.shape[2], dtype=jnp.int32)
    valid = (positions[None, :] < gen_lengths)[:, None, None, None, :]
    gen_scores = jnp.where(valid, score_rows(own_query, gen_keys), NEGATIVE)
    own_state = absorb(empty_state((prompts_here, 1, KVHEADS, groups)), gen_scores, gen_values)
    key_rows, value_rows = split_cache(lax.all_gather(prompt_kv, "sample", axis=1, tiled=True))
    merged = absorb(own_state, score_rows(own_query, key_rows), value_rows)
    attended = (
        (merged[2] / merged[1][..., None])
        .astype(jnp.bfloat16)
        .reshape(prompts_here, 1, QHEADS * HDIM)
    )
    projected = jnp.einsum(
        "bnq,qd->bnd",
        lax.all_gather(attended, "sample", axis=1, tiled=True),
        out_proj,
        preferred_element_type=jnp.float32,
    )
    mixed = projected.astype(jnp.bfloat16)
    stream = residual.astype(jnp.float32) + projected
    squares = lax.psum(jnp.sum(stream * stream, axis=-1), "sample")
    factor = lax.rsqrt(squares / D + EPSILON)
    row_count = prompts_here * samples
    normed = (stream * factor[..., None] * norm_gain).astype(jnp.bfloat16).reshape(row_count, width)
    owners = lax.axis_size("expert")
    experts_all = EXP_COL * owners
    capacity = 5 * prompts_here * samples * TOPK // (4 * experts_all)
    expert_ids = routes.reshape(row_count, TOPK)
    route_weight = route_probs.reshape(row_count, TOPK)
    expert_hits = jnp.sum(
        (expert_ids[:, :, None] == jnp.arange(experts_all, dtype=jnp.int32)[None, None, :]).astype(
            jnp.int32
        ),
        axis=1,
    )
    before = jnp.cumsum(expert_hits, axis=0) - expert_hits
    arrival = jnp.take_along_axis(before, expert_ids, axis=1)
    slot_index = (expert_ids * capacity + arrival).reshape(-1)
    outgoing = (
        jnp.zeros((experts_all * capacity, width), jnp.bfloat16)
        .at[slot_index]
        .set(jnp.repeat(normed, TOPK, axis=0))
    )
    outgoing = outgoing.reshape(owners, EXP_COL, capacity, width)
    partial_sums = jnp.einsum(
        "sjcd,jdf->sjcf",
        lax.all_to_all(outgoing, "expert", split_axis=0, concat_axis=0, tiled=True),
        w_gate_up,
        preferred_element_type=jnp.float32,
    )
    gate_up = lax.psum(partial_sums.astype(jnp.bfloat16), "sample").astype(jnp.float32)
    activated = (jax.nn.silu(gate_up[..., :FF]) * gate_up[..., FF:]).astype(jnp.bfloat16)
    finished = jnp.einsum(
        "sjcf,jfd->sjcd", activated, w_down, preferred_element_type=jnp.float32
    ).astype(jnp.bfloat16)
    returned = lax.all_to_all(finished, "expert", split_axis=0, concat_axis=0, tiled=True)
    picked = jnp.take(returned.reshape(experts_all * capacity, width), slot_index, axis=0).reshape(
        row_count, TOPK, width
    )
    combined = jnp.sum(picked.astype(jnp.float32) * route_weight[:, :, None], axis=1)
    expert_out = combined.astype(jnp.bfloat16).reshape(prompts_here, samples, width)
    return (mixed, expert_out)


def solution(mesh):
    placed = (
        P("expert", "sample", None),
        P("expert", "sample", None),
        P("expert", "sample", None, None),
        P("expert", "sample"),
        P(None, "sample"),
        P("expert", None, "sample"),
        P("sample"),
        P("expert", "sample", None),
        P("expert", None, "sample"),
        P("expert", None, None),
        P("expert", None, None),
    )
    return jax.shard_map(
        on_device,
        mesh=mesh,
        in_specs=placed,
        out_specs=(P("expert", None, "sample"), P("expert", None, "sample")),
        check_vma=False,
    )
```

profile of v0, /device:TPU:0, one launch (start us, length us, event | category | flops | bytes accessed | tf_op | source)
XLA Modules:
  0.0 297.4 jit_solution(7748349599917151613)
XLA Ops:
  7.2 0.0 copy-start.2
  7.2 0.0 all-gather.2.cloned.1.call-start
  7.2 2.8 copy.46
  10.0 0.0 all-gather.2.cloned.1.call-update
  10.0 0.0 all-reduce.2.cloned.1.call-start
  10.1 0.0 copy-done.2
  10.1 0.1 reshape.295
  10.2 0.1 copy.52
  10.3 0.1 copy.53
  10.4 0.1 reduce_window_sum.11
  10.4 0.1 reshape.308
  10.5 0.0 copy-start.6
  10.5 0.0 copy-start
  10.5 0.0 copy-start.3
  10.6 1.9 gather_fusion.1
  12.5 0.0 copy-done.6
  12.5 0.1 iota_compare_fusion.1
  12.6 0.0 copy-done
  12.6 0.1 slice_bitcast_fusion.1
  12.7 0.0 copy-done.3
  12.7 0.3 fusion.55
  13.0 80.6 %all-gather.2.cloned.1.call-done = bf16[8,256,1024]{2,0,1:T(8,128)(2,1)} async-done(((bf16[8,64,1024]{2,0,1:T(8,128)(2,1)}), bf16[8,256,1024]{2,0,1:T(8,128)(2,1)}) %all-gather.2.cloned.1.call-update) | async-done | bytes 4194320 | tf_op jit(solution)/shard_map/all_gather | solution.py:79
  93.6 4.5 %fusion.54 = (bf16[8,256,512]{2,0,1:T(8,128)(2,1)}, bf16[8,256,512]{2,0,1:T(8,128)(2,1)}) fusion(bf16[8,256,1024]{2,0,1:T(8,128)(2,1)} %all-gather.2.cloned.1.call-done), kind=kLoop, calls=%fused_computation.78 | loop fusion | bytes 8388608 | tf_op jit(solution)/shard_map/slice | solution.py:38
  98.1 3.0 %copy.64 = bf16[8,256,512]{1,2,0:T(8,128)(2,1)S(1)} copy(bf16[8,256,512]{2,0,1:T(8,128)(2,1)} %get-tuple-element.13) | data formatting | bytes 4194304
  101.1 0.5 fusion.56
  101.6 3.0 %copy.65 = bf16[8,256,512]{1,2,0:T(8,128)(2,1)S(1)} copy(bf16[8,256,512]{2,0,1:T(8,128)(2,1)} %get-tuple-element.12) | data formatting | bytes 4194304
  104.6 0.3 fusion.44
  104.9 0.3 fusion.35
  105.2 0.0 copy-start.1
  105.2 0.4 fusion.25
  105.6 1.8 fusion.30
  107.4 0.1 reshape.292
  107.5 16.1 %all_gather.7 = bf16[8,4,8192]{2,0,1:T(8,128)(2,1)S(1)} all-gather(bf16[8,1,8192]{2,0,1:T(8,128)(2,1)S(1)} %reshape.292), channel_id=1, replica_groups=mesh['sample'=4,'expert'=8] {'sample'}, dimensions={1}, use_global_device_ids=true | all-gather | bytes 655360 | tf_op jit(solution)/shard_map/all_gather | solution.py:88
  123.6 0.0 copy-done.1
  123.6 0.0 copy-start.5
  123.6 8.8 %multiply_reduce_fusion.1 = (f32[8,4]{0,1:T(4,128)S(1)}, f32[8,4,1024]{2,0,1:T(8,128)S(1)}) fusion(bf16[8,4,1024]{2,1,0:T(4,128)(2,1)S(1)} %copy-done.1, bf16[8,4,8192]{2,0,1:T(8,128)(2,1)S(1)} %all_gather.7, bf16[8192,1024]{1,0:T(8,128)(2,1)} %param.15), kind=kOutput, calls=%fused_computation.51 | convolution fusion | flops 537001984 | bytes 17498240 | tf_op jit(solution)/shard_map/bnq,qd->bnd/dot_general | solution.py:86
  132.4 8.4 %psum.14 = f32[8,4]{0,1:T(4,128)S(1)} all-reduce(f32[8,4]{0,1:T(4,128)S(1)} %get-tuple-element.25), channel_id=1, replica_groups=mesh['sample'=4,'expert'=8] {'sample'}, use_global_device_ids=true, to_apply=%region_7.8 | all-reduce | flops 32 | bytes 256 | tf_op jit(solution)/shard_map/psum | solution.py:94
  140.8 0.0 copy-done.5
  140.8 0.1 multiply_convert_fusion
  140.9 0.1 copy.56
  140.9 1.8 scatter_custom_fusion
  142.8 0.2 reshape.298
  143.0 16.1 %all_to_all.10 = bf16[8,3,13,1024]{3,2,1,0:T(8,128)(2,1)S(1)} all-to-all(bf16[8,3,13,1024]{3,2,1,0:T(8,128)(2,1)S(1)} %reshape.298), channel_id=1, replica_groups=mesh['sample'=4,'expert'=8] {'expert'}, dimensions={0} | all-to-all | bytes 1277952 | tf_op jit(solution)/shard_map/all_to_all | solution.py:120
  159.1 10.4 %fusion.9 = bf16[8,3,13,3072]{3,2,0,1:T(8,128)(2,1)} fusion(bf16[3,1024,3072]{2,1,0:T(8,128)(2,1)} %param.18, bf16[8,3,13,1024]{3,2,1,0:T(8,128)(2,1)S(1)} %all_to_all.10), kind=kOutput, calls=%fused_computation.10 | convolution fusion | flops 1963892736 | bytes 21430272 | tf_op jit(solution)/shard_map/sjcd,jdf->sjcf/dot_general | solution.py:118
  169.5 0.0 all-reduce.2.cloned.1.call-update
  169.6 93.3 %all-reduce.2.cloned.1.call-done = bf16[8,3,13,3072]{3,2,0,1:T(8,128)(2,1)} async-done(((bf16[8,3,13,3072]{3,2,0,1:T(8,128)(2,1)}), bf16[8,3,13,3072]{3,2,0,1:T(8,128)(2,1)}) %all-reduce.2.cloned.1.call-update) | async-done | bytes 1916944 | tf_op jit(solution)/shard_map/psum | solution.py:124
  262.9 2.2 convert_element_type.49
  265.1 5.7 %fusion.16 = bf16[8,3,13,1024]{3,2,0,1:T(8,128)(2,1)S(1)} fusion(bf16[3,1536,1024]{2,1,0:T(8,128)(2,1)} %param.19, f32[8,3,13,3072]{3,2,0,1:T(8,128)S(1)} %convert_element_type.49), kind=kOutput, calls=%fused_computation.14 | convolution fusion | flops 984662016 | bytes 13910016 | tf_op jit(solution)/shard_map/sjcf,jfd->sjcd/dot_general | solution.py:126
  270.8 0.9 copy.58
  271.8 3.7 %all-to-all-start.1 = ((bf16[8,3,13,1024]{3,2,1,0:T(8,128)(2,1)}), bf16[8,3,13,1024]{3,2,1,0:T(8,128)(2,1)S(1)}, u32[]{:S(2)}, u32[]{:S(2)}) async-start(bf16[8,3,13,1024]{3,2,1,0:T(8,128)(2,1)} %copy.58), calls=%async_computation.1 | async-start | bytes 1572864 | tf_op jit(solution)/shard_map/all_to_all | solution.py:129
  275.4 0.1 reshape.311
  275.5 0.7 copy.59
  276.2 11.8 %all-to-all-done.1 = bf16[8,3,13,1024]{3,2,1,0:T(8,128)(2,1)S(1)} async-done(((bf16[8,3,13,1024]{3,2,1,0:T(8,128)(2,1)}), bf16[8,3,13,1024]{3,2,1,0:T(8,128)(2,1)S(1)}, u32[]{:S(2)}, u32[]{:S(2)}) %all-to-all-start.1) | async-done | bytes 639008 | tf_op jit(solution)/shard_map/all_to_all | solution.py:129
  288.0 0.2 reshape.299
  288.2 0.0 copy-start.4
  288.3 1.2 gather_fusion
  289.4 0.0 copy-done.4
  289.4 0.4 multiply_reduce_fusion
  289.9 0.7 convert_element_type.55
  (10 shorter events, 0.2 us)
Async XLA Ops:
  7.2 2.9 copy-start.2
  7.2 86.5 %all-gather.2.cloned.1.call-start = ((), (), s32[]{:S(2)}) async-start(), calls=%async_computation.2 | async-start | bytes 5242880 | tf_op jit(solution)/shard_map/all_gather | solution.py:79
  10.0 252.9 %all-reduce.2.cloned.1.call-start = ((), (), s32[]{:S(2)}) async-start(), calls=%async_computation.3 | async-start | bytes 4718592 | tf_op jit(solution)/shard_map/psum | solution.py:124
  10.5 2.0 copy-start.6
  10.5 2.1 copy-start
  10.5 2.1 copy-start.3
  105.2 18.4 %copy-start.1 = (bf16[8,4,1024]{2,1,0:T(4,128)(2,1)S(1)}, bf16[8,4,1024]{2,1,0:T(4,128)(2,1)}, u32[]{:S(2)}) copy-start(bf16[8,4,1024]{2,1,0:T(4,128)(2,1)} %param.16) | copy-start | bytes 196612
  123.6 17.1 %copy-start.5 = (f32[1024]{0:T(1024)S(1)}, f32[1024]{0:T(1024)}, u32[]{:S(2)}) copy-start(f32[1024]{0:T(1024)} %param.17) | copy-start | bytes 12292
  271.8 16.3 %all-to-all-start.1 = ((bf16[8,3,13,1024]{3,2,1,0:T(8,128)(2,1)}), bf16[8,3,13,1024]{3,2,1,0:T(8,128)(2,1)S(1)}, u32[]{:S(2)}, u32[]{:S(2)}) async-start(bf16[8,3,13,1024]{3,2,1,0:T(8,128)(2,1)} %copy.58), calls=%async_computation.1 | async-start | bytes 1572864 | tf_op jit(solution)/shard_map/all_to_all | solution.py:129
  288.2 1.2 copy-start.4
Sparse Core Ops, SparseCore 0:
  10.1 83.4 all-gather.1
  169.7 93.1 all-reduce.1
where the time goes:
time: 298 us; the launch traced here: 297 us
  waiting for transfers between devices  186 us (62%)
  blocking collectives  40.6 us (14%)
  matrix products  27.9 us (9%)
  local copies, waits for them, and re-layouts  21.5 us (7%)
  between operations  14.3 us (5%)
  starting transfers between devices  3.73 us (1%)
  other arithmetic  3.58 us (1%)
    psum x1, waiting for transfers between devices, on_device(): lax.psum(partial_sums.astype(jnp.bfloat16), 'sample').astype(jnp.float32)  93.3 us
    all_gather x1, waiting for transfers between devices, on_device(): lax.all_gather(prompt_kv, 'sample', axis=1, tiled=True)  80.6 us
    all_gather x1, blocking collectives, on_device(): lax.all_gather(attended, 'sample', axis=1, tiled=True)  16.1 us
    all_to_all x1, blocking collectives, on_device(): lax.all_to_all(outgoing, 'expert', split_axis=0, concat_axis=0, tiled=True)  16.1 us
    all_to_all x1, waiting for transfers between devices, on_device(): lax.all_to_all(finished, 'expert', split_axis=0, concat_axis=0, tiled=True)  11.8 us
    dot_general x1, matrix products, on_device(): jnp.einsum('sjcd,jdf->sjcf', lax.all_to_all(outgoing, 'expert', split_axi...  10.4 us
    unnamed x19, local copies, waits for them, and re-layouts  9.54 us
    dot_general x1, matrix products, on_device(): jnp.einsum('bnq,qd->bnd', lax.all_gather(attended, 'sample', axis=1, tile...  8.76 us
  transfers between devices with their start and end apart: 3, of which 3 were waited for; matrix products, arithmetic and copies ran while one was open for 1% of the time, Pallas kernels for 0%

commit v1 on v0

v1 whole, which is shorter than its diff:
```python
import functools

import jax
import jax.numpy as jnp
from jax import lax
from jax.experimental import pallas as pl
from jax.experimental.pallas import tpu as pltpu
from jax.sharding import PartitionSpec as P

KVHEADS = 4
HDIM = 128
TOPK = 8
NEGATIVE = -1e30
EPSILON = 1e-06
MIB = 1 << 20


def send(array, axis, size, shift):
    return lax.ppermute(array, axis, [(i, (i + shift) % size) for i in range(size)])


def swap(array, axis, size, bits):
    return lax.ppermute(array, axis, [(i, i ^ bits) for i in range(size)])


def block_scores(keys, query, tokens, groups, bound):
    scores = lax.dot_general(
        keys, query, (((1,), (1,)), ((), ())), preferred_element_type=jnp.float32
    ) * (HDIM**-0.5)
    row = lax.broadcasted_iota(jnp.int32, scores.shape, 0)
    lane = lax.broadcasted_iota(jnp.int32, scores.shape, 1)
    keep = row // tokens == (lane // groups) % KVHEADS
    if bound is not None:
        keep = keep & (row % tokens < bound)
    return jnp.where(keep, scores, NEGATIVE)


def stacked_heads(rows, first):
    return jnp.concatenate(
        [rows[:, (first + h) * HDIM : (first + h + 1) * HDIM] for h in range(KVHEADS)], axis=0
    )


def softmax_part(scores, values):
    highest = jnp.max(scores, axis=0, keepdims=True)
    weights = jnp.exp(scores - highest)
    total = jnp.sum(weights, axis=0, keepdims=True)
    numerator = lax.dot_general(
        weights.astype(jnp.bfloat16),
        values,
        (((0,), (0,)), ((), ())),
        preferred_element_type=jnp.float32,
    )
    return highest, total, numerator


def prompt_kernel(samples, *refs):
    query_refs, cache_ref = refs[:samples], refs[samples]
    out_refs, stat_ref = refs[samples + 1 : 2 * samples + 1], refs[2 * samples + 1]
    prompts, tokens, _ = cache_ref.shape
    heads = query_refs[0].shape[1]
    for p in range(prompts):
        rows = cache_ref[p]
        keys, values = stacked_heads(rows, 0), stacked_heads(rows, KVHEADS)
        for pair in range(samples // 2):
            query = jnp.concatenate([query_refs[2 * pair][p], query_refs[2 * pair + 1][p]], axis=0)
            scores = block_scores(keys, query, tokens, heads // KVHEADS, None)
            highest, total, numerator = softmax_part(scores, values)
            out_refs[2 * pair][p] = numerator[:heads].astype(jnp.bfloat16)
            out_refs[2 * pair + 1][p] = numerator[heads:].astype(jnp.bfloat16)
            stat_ref[pair, 0, p : p + 1, :] = highest
            stat_ref[pair, 1, p : p + 1, :] = total


def gen_kernel(length_ref, query_ref, cache_ref, out_ref, stat_ref):
    prompts, tokens, _ = cache_ref.shape
    heads = query_ref.shape[1]
    for p in range(prompts):
        rows = cache_ref[p]
        keys, values = stacked_heads(rows, 0), stacked_heads(rows, KVHEADS)
        scores = block_scores(keys, query_ref[p], tokens, heads // KVHEADS, length_ref[p])
        highest, total, numerator = softmax_part(scores, values)
        out_ref[p] = numerator
        stat_ref[0, p : p + 1, :] = highest
        stat_ref[1, p : p + 1, :] = total


VMEM_SPEC = pl.BlockSpec(memory_space=pltpu.VMEM)
SMEM_SPEC = pl.BlockSpec(memory_space=pltpu.SMEM)


def prompt_part(queries, cache):
    samples = len(queries)
    shape = queries[0].shape
    results = pl.pallas_call(
        functools.partial(prompt_kernel, samples),
        out_shape=[jax.ShapeDtypeStruct(shape, jnp.bfloat16)] * samples
        + [jax.ShapeDtypeStruct((samples // 2, 2, shape[0], 2 * shape[1]), jnp.float32)],
        in_specs=[VMEM_SPEC] * (samples + 1),
        out_specs=[VMEM_SPEC] * (samples + 1),
        compiler_params=pltpu.CompilerParams(vmem_limit_bytes=32 * MIB),
        cost_estimate=pl.CostEstimate(
            flops=1000 * 1000 * 1000, bytes_accessed=4 * MIB, transcendentals=500 * 1000
        ),
    )(*queries, cache)
    stats = results[samples]
    heads = shape[1]
    return results[:samples], [
        stats[k // 2, :, :, (k % 2) * heads : (k % 2 + 1) * heads] for k in range(samples)
    ]


def gen_part(query, cache, lengths):
    shape = query.shape
    return pl.pallas_call(
        gen_kernel,
        out_shape=[
            jax.ShapeDtypeStruct(shape, jnp.float32),
            jax.ShapeDtypeStruct((2, shape[0], shape[1]), jnp.float32),
        ],
        in_specs=[SMEM_SPEC, VMEM_SPEC, VMEM_SPEC],
        out_specs=[VMEM_SPEC, VMEM_SPEC],
        compiler_params=pltpu.CompilerParams(vmem_limit_bytes=32 * MIB),
        cost_estimate=pl.CostEstimate(
            flops=100 * 1000 * 1000, bytes_accessed=2 * MIB, transcendentals=100 * 1000
        ),
    )(lengths, query, cache)


def project_kernel(samples, features, place_ref, *refs):
    attended_refs = refs[:samples]
    weight_ref, residual_ref, gain_ref, mixed_ref, row_ref, total_ref, order_ref = refs[samples:]
    step = pl.program_id(0)
    prompts = attended_refs[0].shape[0]

    @pl.when(step == 0)
    def _():
        total_ref[...] = jnp.zeros_like(total_ref)

    stacked = jnp.concatenate([r[...] for r in attended_refs], axis=0)
    total_ref[...] += jnp.dot(stacked, weight_ref[...], preferred_element_type=jnp.float32)

    @pl.when(step == pl.num_programs(0) - 1)
    def _():
        for k in range(samples):
            s = lax.rem(place_ref[0] - k + samples, samples)
            order_ref[pl.ds(pl.multiple_of(s * prompts, prompts), prompts), :] = total_ref[
                k * prompts : (k + 1) * prompts, :
            ]
        projected = order_ref[...]
        mixed_ref[...] = projected.astype(jnp.bfloat16)
        stream = residual_ref[...].astype(jnp.float32) + projected
        square = jnp.sum(stream * stream, axis=1, keepdims=True)
        high = square.astype(jnp.bfloat16).astype(jnp.float32)
        low = square - high
        row_ref[:, :features] = (stream * gain_ref[...]).astype(jnp.bfloat16)
        lane = lax.broadcasted_iota(jnp.int32, (square.shape[0], HDIM), 1)
        row_ref[:, features:] = jnp.where(
            lane == 0, high, jnp.where(lane == 1, low, 0.0)
        ).astype(jnp.bfloat16)


def project(attended, out_proj, residual, gain, place):
    samples = len(attended)
    prompts, inner = attended[0].shape
    width = out_proj.shape[1]
    rows = samples * prompts
    depth = 1024
    whole = lambda shape: pl.BlockSpec(shape, lambda i, place: (0, 0))
    return pl.pallas_call(
        functools.partial(project_kernel, samples, width),
        out_shape=[
            jax.ShapeDtypeStruct((rows, width), jnp.bfloat16),
            jax.ShapeDtypeStruct((rows, width + HDIM), jnp.bfloat16),
        ],
        grid_spec=pltpu.PrefetchScalarGridSpec(
            num_scalar_prefetch=1,
            grid=(inner // depth,),
            in_specs=[pl.BlockSpec((prompts, depth), lambda i, place: (0, i))] * samples
            + [
                pl.BlockSpec((depth, width), lambda i, place: (i, 0)),
                whole((rows, width)),
                whole((1, width)),
            ],
            out_specs=[whole((rows, width)), whole((rows, width + HDIM))],
            scratch_shapes=[
                pltpu.VMEM((rows, width), jnp.float32),
                pltpu.VMEM((rows, width), jnp.float32),
            ],
        ),
        compiler_params=pltpu.CompilerParams(vmem_limit_bytes=32 * MIB),
        cost_estimate=pl.CostEstimate(
            flops=2 * rows * inner * width, bytes_accessed=2 * inner * width, transcendentals=0
        ),
    )(place, *attended, out_proj, residual, gain)


def gate_kernel(features, place_ref, pick_ref, near_ref, far_ref, gate_ref, up_ref, *rest):
    out_refs, chosen_ref = rest[:-1], rest[-1]
    step = pl.program_id(0)
    half = near_ref.shape[0]

    @pl.when(step == 0)
    def _():
        pick = pick_ref[...]
        chosen = jnp.dot(
            pick[:, :half], near_ref[:, :features], preferred_element_type=jnp.float32
        ) + jnp.dot(pick[:, half:], far_ref[:, :features], preferred_element_type=jnp.float32)
        chosen_ref[...] = chosen.astype(jnp.bfloat16)

    chosen = chosen_ref[...]
    part = gate_ref.shape[1]
    gate = jnp.dot(chosen, gate_ref[...], preferred_element_type=jnp.float32)
    up = jnp.dot(chosen, up_ref[...], preferred_element_type=jnp.float32)
    for k, out_ref in enumerate(out_refs):

        @pl.when(step == (k - 1) % len(out_refs))
        def _():
            out_ref[:, :part] = gate.astype(jnp.bfloat16)
            out_ref[:, part:] = up.astype(jnp.bfloat16)


def gate_up_parts(pick, near, far, weights, expert, place, samples):
    slots, rows = pick.shape
    _, features, wide = weights.shape
    hidden = wide // 2
    part = hidden // samples
    if part % HDIM:
        chosen = jnp.dot(
            pick,
            jnp.concatenate([near, far], axis=0)[:, :features],
            preferred_element_type=jnp.float32,
        ).astype(jnp.bfloat16)
        shares = jnp.dot(chosen, weights[expert], preferred_element_type=jnp.float32)
        shares = shares.astype(jnp.bfloat16).reshape(slots, 2, samples, part)
        shares = jnp.roll(shares, -place[0], axis=2)
        return [shares[:, :, k].reshape(slots, 2 * part) for k in range(samples)]
    whole = lambda shape: pl.BlockSpec(shape, lambda i, place: (0, 0))
    column = lambda i, place: lax.rem(place[0] + i + 1, samples)
    return pl.pallas_call(
        functools.partial(gate_kernel, features),
        out_shape=[jax.ShapeDtypeStruct((slots, 2 * part), jnp.bfloat16)] * samples,
        grid_spec=pltpu.PrefetchScalarGridSpec(
            num_scalar_prefetch=1,
            grid=(samples,),
            in_specs=[
                whole(pick.shape),
                whole(near.shape),
                whole(far.shape),
                pl.BlockSpec(
                    (None, features, part), lambda i, place: (expert, 0, column(i, place))
                ),
                pl.BlockSpec(
                    (None, features, part), lambda i, place: (expert, 0, samples + column(i, place))
                ),
            ],
            out_specs=[whole((slots, 2 * part))] * samples,
            scratch_shapes=[pltpu.VMEM((slots, features), jnp.bfloat16)],
        ),
        compiler_params=pltpu.CompilerParams(vmem_limit_bytes=32 * MIB),
        cost_estimate=pl.CostEstimate(
            flops=2 * slots * features * wide, bytes_accessed=2 * features * wide, transcendentals=0
        ),
    )(place, pick, near, far, weights, weights)


def down_kernel(place_ref, *refs):
    samples = len(refs) - 3
    act_refs, (weight_ref, out_ref, total_ref) = refs[:samples], refs[samples:]
    step = pl.program_id(0)
    for k, act_ref in enumerate(act_refs):

        @pl.when(step == k)
        def _():
            share = jnp.dot(act_ref[...], weight_ref[...], preferred_element_type=jnp.float32)
            if k == 0:
                total_ref[...] = share
            elif k < samples - 1:
                total_ref[...] += share
            else:
                out_ref[...] = (total_ref[...] + share).astype(jnp.bfloat16)


def down_rows(acts, weights, expert, place):
    samples = len(acts)
    slots, part = acts[0].shape
    _, hidden, width = weights.shape
    if part % HDIM:
        joined = jnp.stack(acts, axis=1)[:, ::-1]
        joined = jnp.roll(joined, place[0] + 1, axis=1).reshape(slots, hidden)
        return jnp.dot(joined, weights[expert], preferred_element_type=jnp.float32).astype(
            jnp.bfloat16
        )
    whole = lambda shape: pl.BlockSpec(shape, lambda i, place: (0, 0))
    return pl.pallas_call(
        down_kernel,
        out_shape=jax.ShapeDtypeStruct((slots, width), jnp.bfloat16),
        grid_spec=pltpu.PrefetchScalarGridSpec(
            num_scalar_prefetch=1,
            grid=(samples,),
            in_specs=[whole((slots, part))] * samples
            + [
                pl.BlockSpec(
                    (None, part, width),
                    lambda i, place: (expert, lax.rem(place[0] - i + samples, samples), 0),
                )
            ],
            out_specs=whole((slots, width)),
            scratch_shapes=[pltpu.VMEM((slots, width), jnp.float32)],
        ),
        compiler_params=pltpu.CompilerParams(vmem_limit_bytes=32 * MIB),
        cost_estimate=pl.CostEstimate(
            flops=2 * slots * hidden * width, bytes_accessed=2 * hidden * width, transcendentals=0
        ),
    )(place, *acts, weights)


def gather_experts(array, owners):
    near = jnp.concatenate(
        [array] + [swap(array, "expert", owners, b) for b in range(2, owners, 2)], axis=0
    )
    return near, swap(near, "expert", owners, 1)


def on_device(
    queries,
    prompt_kv,
    gen_kv,
    gen_lengths,
    out_proj,
    residual,
    norm_gain,
    w_gate_up,
    w_down,
    routes,
    route_probs,
):
    samples, owners = lax.axis_size("sample"), lax.axis_size("expert")
    place = lax.axis_index("sample").astype(jnp.int32).reshape(1)
    prompts = queries.shape[0]
    heads = queries.shape[2] // HDIM
    width = residual.shape[2]
    rows = prompts * samples
    per_owner = w_gate_up.shape[0]
    hidden = w_down.shape[1]
    part = hidden // samples

    query = queries.reshape(prompts, heads, HDIM)
    all_queries = [query] + [send(query, "sample", samples, k) for k in range(1, samples)]

    by_sample = lambda a: jnp.swapaxes(a, 0, 1).reshape(rows, TOPK)
    table = jnp.concatenate(
        [by_sample(routes).astype(jnp.float32), by_sample(route_probs)], axis=1
    )
    table = jnp.concatenate(gather_experts(table, owners), axis=0)
    capacity = 5 * rows * TOPK // (4 * per_owner * owners)
    slots = owners * capacity
    first = lax.axis_index("expert") * per_owner
    mine = (first + jnp.arange(per_owner, dtype=jnp.int32)).astype(jnp.float32)
    match = table[None, :, :TOPK] == mine[:, None, None]
    hit = jnp.any(match, axis=2)
    weight = jnp.sum(jnp.where(match, table[None, :, TOPK:], 0.0), axis=2)
    hit_blocks = hit.reshape(per_owner, owners, rows)
    earlier = (jnp.arange(rows)[:, None] < jnp.arange(rows)[None, :]).astype(jnp.bfloat16)
    rank = jnp.einsum(
        "jbr,rq->jbq",
        hit_blocks.astype(jnp.bfloat16),
        earlier,
        preferred_element_type=jnp.float32,
    ).astype(jnp.int32)
    slot = rank + capacity * jnp.arange(owners, dtype=jnp.int32)[None, :, None]
    slot = jnp.where(hit_blocks, slot, -1).reshape(per_owner, owners * rows)
    chosen = slot[:, None, :] == jnp.arange(slots, dtype=jnp.int32)[None, :, None]
    pick = chosen.astype(jnp.bfloat16)
    slot_weight = jnp.sum(jnp.where(chosen, weight[:, None, :], 0.0), axis=2)

    gen_out, gen_stat = gen_part(query, gen_kv[:, 0], gen_lengths[:, 0])
    parts, stats = prompt_part(all_queries, prompt_kv)
    outs, marks = [gen_out, parts[0]], [gen_stat, stats[0]]
    for k in range(1, samples):
        outs.append(send(parts[k], "sample", samples, -k))
        marks.append(send(stats[k], "sample", samples, -k))
    highest = functools.reduce(jnp.maximum, [m[0] for m in marks])
    scales = [jnp.exp(m[0] - highest) for m in marks]
    total = sum(c * m[1] for c, m in zip(scales, marks))
    attended = sum(
        o.astype(jnp.float32) * (c / total)[:, :, None] for o, c in zip(outs, scales)
    )
    attended = attended.astype(jnp.bfloat16).reshape(prompts, heads * HDIM)
    attended = [attended] + [send(attended, "sample", samples, k) for k in range(1, samples)]
    mixed, row_block = project(
        attended,
        out_proj,
        jnp.swapaxes(residual, 0, 1).reshape(rows, width),
        norm_gain.reshape(1, width),
        place,
    )
    mixed = jnp.swapaxes(mixed.reshape(samples, prompts, width), 0, 1)

    near, far = gather_experts(row_block, owners)
    square = jnp.concatenate([near[:, width : width + 2], far[:, width : width + 2]], axis=0)
    square = jnp.sum(square.astype(jnp.float32), axis=1)
    square = square + sum(send(square, "sample", samples, k) for k in range(1, samples))
    factor = lax.rsqrt(square / (width * samples) + EPSILON)
    slot_factor = jnp.sum(jnp.where(chosen, factor[None, None, :], 0.0), axis=2)

    finished = []
    for j in range(per_owner):
        shares = gate_up_parts(pick[j], near, far, w_gate_up, j, place, samples)
        gate_up = shares[0].astype(jnp.float32)
        for k in range(1, samples):
            gate_up = gate_up + send(shares[k], "sample", samples, k).astype(jnp.float32)
        gate_up = gate_up * slot_factor[j][:, None]
        act = jax.nn.silu(gate_up[:, :part]) * gate_up[:, part:] * slot_weight[j][:, None]
        act = act.astype(jnp.bfloat16)
        acts = [act] + [send(act, "sample", samples, k) for k in range(1, samples)]
        finished.append(down_rows(acts, w_down, j, place))
    returned = sum(
        lax.dot_general(
            pick[j], finished[j], (((0,), (0,)), ((), ())), preferred_element_type=jnp.float32
        )
        for j in range(per_owner)
    )
    returned = returned.reshape(2, owners // 2, rows, width)
    arrived = swap(returned[1].astype(jnp.bfloat16), "expert", owners, 1)
    paired = returned[0] + arrived.astype(jnp.float32)
    outgoing = paired.astype(jnp.bfloat16)
    combined = paired[0]
    for b in range(1, owners // 2):
        combined = combined + swap(outgoing[b], "expert", owners, 2 * b).astype(jnp.float32)
    expert_out = combined.astype(jnp.bfloat16).reshape(samples, prompts, width)
    return mixed, jnp.swapaxes(expert_out, 0, 1)


def solution(mesh):
    placed = (
        P("expert", "sample", None),
        P("expert", "sample", None),
        P("expert", "sample", None, None),
        P("expert", "sample"),
        P(None, "sample"),
        P("expert", None, "sample"),
        P("sample"),
        P("expert", "sample", None),
        P("expert", None, "sample"),
        P("expert", None, None),
        P("expert", None, None),
    )
    return jax.shard_map(
        on_device,
        mesh=mesh,
        in_specs=placed,
        out_specs=(P("expert", None, "sample"), P("expert", None, "sample")),
        check_vma=False,
    )
```

time: 298 us -> 175 us (0.59)
  waiting for transfers between devices: 186 us -> 47 us
  starting transfers between devices: 3.73 us -> 76.5 us
  blocking collectives: 40.6 us -> 0 us
  matrix products: 27.9 us -> 1.12 us
  Pallas kernels: 0 us -> 19.2 us
  between operations: 14.3 us -> 1.09 us
  local copies, waits for them, and re-layouts: 21.5 us -> 27.1 us
    psum x1 -> x0, waiting for transfers between devices: 93.3 us -> none  [on_device(): lax.psum(partial_sums.astype(jnp.bfloat16), 'sample').astype(jnp.float32)]
    all_gather x1 -> x0, waiting for transfers between devices: 80.6 us -> none  [on_device(): lax.all_gather(prompt_kv, 'sample', axis=1, tiled=True)]
    ppermute x0 -> x45, starting transfers between devices: none -> 76.5 us  [the longest x33 64.7 us: send(): lax.ppermute(array, axis, [(i, (i + shift) % size) for i in range(size)])]
    ppermute x0 -> x45, waiting for transfers between devices: none -> 47 us  [the longest x33 37 us: send(): lax.ppermute(array, axis, [(i, (i + shift) % size) for i in range(size)])]
    dot_general x7 -> x4, matrix products: 27.9 us -> 1.12 us  [the longest x3 1.04 us: on_device(): lax.dot_general(pick[j], finished[j], (((0,), (0,)), ((), ())), preferred...]
    pallas_call x0 -> x9, Pallas kernels: none -> 19.2 us  [the longest x3 9.06 us: gate_up_parts(): pl.pallas_call(functools.partial(gate_kernel, features), out_shape=[jax.S...]
    all_gather x1 -> x0, blocking collectives: 16.1 us -> none  [on_device(): lax.all_gather(attended, 'sample', axis=1, tiled=True)]
    all_to_all x1 -> x0, blocking collectives: 16.1 us -> none  [on_device(): lax.all_to_all(outgoing, 'expert', split_axis=0, concat_axis=0, tiled=True)]
  transfers between devices with their start and end apart: 3 -> 45, of which waited for: 3 -> 16; matrix products, arithmetic and copies ran while one was open for 1% -> 3% of each run, Pallas kernels for 0% -> 7%
where the time goes in v1:
time: 175 us; the launch traced here: 174 us
  starting transfers between devices  76.5 us (44%)
  waiting for transfers between devices  47 us (27%)
  local copies, waits for them, and re-layouts  27.1 us (15%)
  Pallas kernels  19.2 us (11%)
  other arithmetic  2.39 us (1%)
    ppermute x33, starting transfers between devices, send(): lax.ppermute(array, axis, [(i, (i + shift) % size) for i in range(size)])  64.7 us
    ppermute x33, waiting for transfers between devices, send(): lax.ppermute(array, axis, [(i, (i + shift) % size) for i in range(size)])  37 us
    unnamed x27, local copies, waits for them, and re-layouts  23.9 us
    ppermute x12, starting transfers between devices, swap(): return lax.ppermute(array, axis, [(i, i ^ bits) for i in range(size)])  11.8 us
    ppermute x12, waiting for transfers between devices, swap(): return lax.ppermute(array, axis, [(i, i ^ bits) for i in range(size)])  10 us
    pallas_call x3, Pallas kernels, gate_up_parts(): pl.pallas_call(functools.partial(gate_kernel, features), out_shape=[jax.S...  9.06 us
    pallas_call x3, Pallas kernels, down_rows(): pl.pallas_call(down_kernel, out_shape=jax.ShapeDtypeStruct((slots, width)...  3.93 us
    pallas_call x1, Pallas kernels, project(): pl.pallas_call(functools.partial(project_kernel, samples, width), out_sha...  3.91 us
  transfers between devices with their start and end apart: 45, of which 16 were waited for; matrix products, arithmetic and copies ran while one was open for 3% of the time, Pallas kernels for 7%

profile of v1, /device:TPU:0, one launch (start us, length us, event | category | flops | bytes accessed | tf_op | source)
XLA Modules:
  0.0 174.5 jit_solution(2931569803012770076)
XLA Ops:
  0.6 0.7 convert_bitcast_fusion
  1.5 0.8 copy.34
  2.4 3.9 %collective-permute-start.14 = (f32[32,16]{0,1:T(8,128)S(1)}, f32[32,16]{0,1:T(8,128)S(1)}, u32[]{:S(2)}, u32[]{:S(2)}) collective-permute-start(f32[32,16]{0,1:T(8,128)S(1)} %constant_dynamic-update-slice_fusion), channel_id=1, source_target_pairs={{0,6},{1,7},{2,4},{3,5},{4,2},{5,3},{6,0},{7,1},{8,14},{9,15},{10,... | collective-permute-start | bytes 6152 | tf_op jit(solution)/shard_map/ppermute | solution.py:23
  7.0 0.9 copy.45
  7.9 4.1 %collective-permute-start.2 = (bf16[8,64,128]{2,1,0:T(8,128)(2,1)S(1)}, bf16[8,64,128]{2,1,0:T(8,128)(2,1)S(1)}, u32[]{:S(2)}, u32[]{:S(2)}) collective-permute-start(bf16[8,64,128]{2,1,0:T(8,128)(2,1)S(1)} %bitcast.202), channel_id=1, source_target_pairs={{0,24},{8,0},{16,8},{24,16},{1,25},{9,1},{17,9},{25,17},{2,26},{10... | collective-permute-start | bytes 393224 | tf_op jit(solution)/shard_map/ppermute | solution.py:19
  11.9 0.9 copy.47
  12.8 1.1 collective-permute-start
  14.0 1.0 copy-done.3
  15.0 0.7 copy-done.5
  15.7 1.1 shard_map.122
  17.0 5.7 %collective-permute-done.1.refs_2_ = bf16[8,64,128]{2,1,0:T(8,128)(2,1)S(1)} collective-permute-done((bf16[8,64,128]{2,1,0:T(8,128)(2,1)S(1)}, bf16[8,64,128]{2,1,0:T(8,128)(2,1)S(1)}, u32[]{:S(2)}, u32[]{:S(2)}) %collective-permute-start.1) | collective-permute-done | bytes 131104 | tf_op jit(solution)/shard_map/ppermute | solution.py:19
  22.7 1.2 copy-done.6
  24.0 1.3 shard_map.123
  25.3 1.2 collective-permute-start.3
  26.5 0.8 collective-permute-start.5
  27.3 2.2 %collective-permute-start.4 = (f32[2,8,64]{2,1,0:T(8,128)S(1)}, f32[2,8,64]{2,1,0:T(8,128)S(1)}, u32[]{:S(2)}, u32[]{:S(2)}) collective-permute-start(f32[2,8,64]{2,1,0:T(8,128)S(1)} %get-tuple-element.67), channel_id=1, source_target_pairs={{0,16},{8,24},{16,0},{24,8},{1,17},{9,25},{17,1},{25,9},{2,18},{10... | collective-permute-start | bytes 12296 | tf_op jit(solution)/shard_map/ppermute | solution.py:19
  29.8 1.0 collective-permute-start.6
  30.7 1.9 %collective-permute-start.7 = (bf16[8,64,128]{2,1,0:T(8,128)(2,1)S(1)}, bf16[8,64,128]{2,1,0:T(8,128)(2,1)S(1)}, u32[]{:S(2)}, u32[]{:S(2)}) collective-permute-start(bf16[8,64,128]{2,1,0:T(8,128)(2,1)S(1)} %get-tuple-element.28), channel_id=1, source_target_pairs={{0,16},{8,24},{16,0},{24,8},{1,17},{9,25},{17,1},{25,9},{2,18},{10... | collective-permute-start | bytes 393224 | tf_op jit(solution)/shard_map/ppermute | solution.py:19
  32.7 3.2 %collective-permute-done.6 = bf16[8,64,128]{2,1,0:T(8,128)(2,1)S(1)} collective-permute-done((bf16[8,64,128]{2,1,0:T(8,128)(2,1)S(1)}, bf16[8,64,128]{2,1,0:T(8,128)(2,1)S(1)}, u32[]{:S(2)}, u32[]{:S(2)}) %collective-permute-start.6) | collective-permute-done | bytes 131104 | tf_op jit(solution)/shard_map/ppermute | solution.py:19
  35.9 6.6 %collective-permute-done.7 = bf16[8,64,128]{2,1,0:T(8,128)(2,1)S(1)} collective-permute-done((bf16[8,64,128]{2,1,0:T(8,128)(2,1)S(1)}, bf16[8,64,128]{2,1,0:T(8,128)(2,1)S(1)}, u32[]{:S(2)}, u32[]{:S(2)}) %collective-permute-start.7) | collective-permute-done | bytes 131104 | tf_op jit(solution)/shard_map/ppermute | solution.py:19
  43.1 1.6 collective-permute-start.10
  44.8 1.9 %collective-permute-start.9 = (bf16[8,8192]{1,0:T(8,128)(2,1)S(1)}, bf16[8,8192]{1,0:T(8,128)(2,1)S(1)}, u32[]{:S(2)}, u32[]{:S(2)}) collective-permute-start(bf16[8,8192]{1,0:T(8,128)(2,1)S(1)} %bitcast.199), channel_id=1, source_target_pairs={{0,8},{8,16},{16,24},{24,0},{1,9},{9,17},{17,25},{25,1},{2,10},{10... | collective-permute-start | bytes 393224 | tf_op jit(solution)/shard_map/ppermute | solution.py:19
  46.8 1.8 %collective-permute-done.11.refs_3_ = bf16[8,8192]{1,0:T(8,128)(2,1)S(1)} collective-permute-done((bf16[8,8192]{1,0:T(8,128)(2,1)S(1)}, bf16[8,8192]{1,0:T(8,128)(2,1)S(1)}, u32[]{:S(2)}, u32[]{:S(2)}) %collective-permute-start.11) | collective-permute-done | bytes 131104 | tf_op jit(solution)/shard_map/ppermute | solution.py:19
  48.5 8.0 %collective-permute-done.10.refs_2_ = bf16[8,8192]{1,0:T(8,128)(2,1)S(1)} collective-permute-done((bf16[8,8192]{1,0:T(8,128)(2,1)S(1)}, bf16[8,8192]{1,0:T(8,128)(2,1)S(1)}, u32[]{:S(2)}, u32[]{:S(2)}) %collective-permute-start.10) | collective-permute-done | bytes 131104 | tf_op jit(solution)/shard_map/ppermute | solution.py:19
  56.5 5.8 %copy-done.2 = bf16[8192,1024]{1,0:T(8,128)(2,1)S(1)} copy-done((bf16[8192,1024]{1,0:T(8,128)(2,1)S(1)}, bf16[8192,1024]{1,0:T(8,128)(2,1)}, u32[]{:S(2)}) %copy-start.2) | copy-done | bytes 16777240
  62.3 0.7 copy-done.4
  63.0 3.9 %shard_map.124 = (bf16[32,1024]{1,0:T(8,128)(2,1)S(1)}, bf16[32,1152]{1,0:T(8,128)(2,1)S(1)}) custom-call(s32[1]{0:T(128)} %bitcast.place_ref, bf16[8,8192]{1,0:T(8,128)(2,1)S(1)} %bitcast.200, bf16[8,8192]{1,0:T(8,128)(2,1)S(1)} %collective-permute-done.9.refs_1_, bf16[8,8192]{1,0:T(8,128)(2,1)S(1)} %collective-permute-done.10.refs_2_, ...), custom_call_target="tpu_custom_call" | custom-call | flops 536870912 | bytes 16777216 | tf_op jit(solution)/shard_map/pallas_call | solution.py:170
  66.9 2.5 %collective-permute-start.18 = (bf16[32,1152]{1,0:T(8,128)(2,1)S(1)}, bf16[32,1152]{1,0:T(8,128)(2,1)S(1)}, u32[]{:S(2)}, u32[]{:S(2)}) collective-permute-start(bf16[32,1152]{1,0:T(8,128)(2,1)S(1)} %get-tuple-element.31), channel_id=1, source_target_pairs={{0,6},{1,7},{2,4},{3,5},{4,2},{5,3},{6,0},{7,1},{8,14},{9,15},{10,... | collective-permute-start | bytes 221192 | tf_op jit(solution)/shard_map/ppermute | solution.py:23
  69.9 0.5 collective-permute-start.16
  70.4 3.8 %collective-permute-done.16 = bf16[32,1152]{1,0:T(8,128)(2,1)S(1)} collective-permute-done((bf16[32,1152]{1,0:T(8,128)(2,1)S(1)}, bf16[32,1152]{1,0:T(8,128)(2,1)S(1)}, u32[]{:S(2)}, u32[]{:S(2)}) %collective-permute-start.16) | collective-permute-done | bytes 73760 | tf_op jit(solution)/shard_map/ppermute | solution.py:23
  74.6 1.4 collective-permute-done.19.far_ref
  76.1 1.0 collective-permute-start.24
  77.1 1.9 %collective-permute-start.23 = (f32[256]{0:T(256)S(1)}, f32[256]{0:T(256)S(1)}, u32[]{:S(2)}, u32[]{:S(2)}) collective-permute-start(f32[256]{0:T(256)S(1)} %convert_reduce_fusion), channel_id=1, source_target_pairs={{0,8},{8,16},{16,24},{24,0},{1,9},{9,17},{17,25},{25,1},{2,10},{10... | collective-permute-start | bytes 3080 | tf_op jit(solution)/shard_map/ppermute | solution.py:19
  79.1 6.4 %copy-done = bf16[3,1024,3072]{2,1,0:T(8,128)(2,1)S(1)} copy-done((bf16[3,1024,3072]{2,1,0:T(8,128)(2,1)S(1)}, bf16[3,1024,3072]{2,1,0:T(8,128)(2,1)}, u32[]{:S(2)}) %copy-start) | copy-done | bytes 18874392
  85.5 3.0 %shard_map.129 = (bf16[104,768]{1,0:T(8,128)(2,1)S(1)}, bf16[104,768]{1,0:T(8,128)(2,1)S(1)}, bf16[104,768]{1,0:T(8,128)(2,1)S(1)}, bf16[104,768]{1,0:T(8,128)(2,1)S(1)}) custom-call(s32[1]{0:T(128)} %bitcast.place_ref, bf16[104,256]{1,0:T(8,128)(2,1)S(1)} %get-tuple-element.61.pick_ref, bf16[128,1152]{1,0:T(8,128)(2,1)S(1)} %constant_dynamic-update-slice_fusion.2.near_ref, ...), custom_call_target="tpu_custom_call" | custom-call | flops 654311424 | bytes 6291456 | tf_op jit(solution)/shard_map/pallas_call | solution.py:240
  88.5 0.7 collective-permute-start.35
  89.1 1.8 %collective-permute-start.36 = (bf16[104,768]{1,0:T(8,128)(2,1)S(1)}, bf16[104,768]{1,0:T(8,128)(2,1)S(1)}, u32[]{:S(2)}, u32[]{:S(2)}) collective-permute-start(bf16[104,768]{1,0:T(8,128)(2,1)S(1)} %get-tuple-element.42), channel_id=1, source_target_pairs={{0,16},{8,24},{16,0},{24,8},{1,17},{9,25},{17,1},{25,9},{2,18},{10... | collective-permute-start | bytes 479240 | tf_op jit(solution)/shard_map/ppermute | solution.py:19
  91.0 6.4 %copy-done.1 = bf16[3,1024,3072]{2,1,0:T(8,128)(2,1)S(1)} copy-done((bf16[3,1024,3072]{2,1,0:T(8,128)(2,1)S(1)}, bf16[3,1024,3072]{2,1,0:T(8,128)(2,1)}, u32[]{:S(2)}) %copy-start.1) | copy-done | bytes 18874392
  97.3 3.0 %shard_map.127 = (bf16[104,768]{1,0:T(8,128)(2,1)S(1)}, bf16[104,768]{1,0:T(8,128)(2,1)S(1)}, bf16[104,768]{1,0:T(8,128)(2,1)S(1)}, bf16[104,768]{1,0:T(8,128)(2,1)S(1)}) custom-call(s32[1]{0:T(128)} %bitcast.place_ref, bf16[104,256]{1,0:T(8,128)(2,1)S(1)} %get-tuple-element.62.pick_ref, bf16[128,1152]{1,0:T(8,128)(2,1)S(1)} %constant_dynamic-update-slice_fusion.2.near_ref, ...), custom_call_target="tpu_custom_call" | custom-call | flops 654311424 | bytes 6291456 | tf_op jit(solution)/shard_map/pallas_call | solution.py:240
  100.4 3.0 %shard_map.125 = (bf16[104,768]{1,0:T(8,128)(2,1)S(1)}, bf16[104,768]{1,0:T(8,128)(2,1)S(1)}, bf16[104,768]{1,0:T(8,128)(2,1)S(1)}, bf16[104,768]{1,0:T(8,128)(2,1)S(1)}) custom-call(s32[1]{0:T(128)} %bitcast.place_ref, bf16[104,256]{1,0:T(8,128)(2,1)S(1)} %get-tuple-element.60.pick_ref, bf16[128,1152]{1,0:T(8,128)(2,1)S(1)} %constant_dynamic-update-slice_fusion.2.near_ref, ...), custom_call_target="tpu_custom_call" | custom-call | flops 654311424 | bytes 6291456 | tf_op jit(solution)/shard_map/pallas_call | solution.py:240
  103.4 2.5 %collective-permute-start.37 = (bf16[104,768]{1,0:T(8,128)(2,1)S(1)}, bf16[104,768]{1,0:T(8,128)(2,1)S(1)}, u32[]{:S(2)}, u32[]{:S(2)}) collective-permute-start(bf16[104,768]{1,0:T(8,128)(2,1)S(1)} %get-tuple-element.43), channel_id=1, source_target_pairs={{0,24},{8,0},{16,8},{24,16},{1,25},{9,1},{17,9},{25,17},{2,26},{10... | collective-permute-start | bytes 479240 | tf_op jit(solution)/shard_map/ppermute | solution.py:19
  106.0 1.0 collective-permute-start.30
  107.2 2.9 %collective-permute-start.31 = (bf16[104,768]{1,0:T(8,128)(2,1)S(1)}, bf16[104,768]{1,0:T(8,128)(2,1)S(1)}, u32[]{:S(2)}, u32[]{:S(2)}) collective-permute-start(bf16[104,768]{1,0:T(8,128)(2,1)S(1)} %get-tuple-element.39), channel_id=1, source_target_pairs={{0,24},{8,0},{16,8},{24,16},{1,25},{9,1},{17,9},{25,17},{2,26},{10... | collective-permute-start | bytes 479240 | tf_op jit(solution)/shard_map/ppermute | solution.py:19
  110.1 0.6 collective-permute-start.20
  110.7 1.1 collective-permute-done.37
  111.8 6.9 %collective-permute-start.21 = (bf16[104,768]{1,0:T(8,128)(2,1)S(1)}, bf16[104,768]{1,0:T(8,128)(2,1)S(1)}, u32[]{:S(2)}, u32[]{:S(2)}) collective-permute-start(bf16[104,768]{1,0:T(8,128)(2,1)S(1)} %get-tuple-element.34), channel_id=1, source_target_pairs={{0,16},{8,24},{16,0},{24,8},{1,17},{9,25},{17,1},{25,9},{2,18},{10... | collective-permute-start | bytes 479240 | tf_op jit(solution)/shard_map/ppermute | solution.py:19
  118.9 3.9 %collective-permute-start.22 = (bf16[104,768]{1,0:T(8,128)(2,1)S(1)}, bf16[104,768]{1,0:T(8,128)(2,1)S(1)}, u32[]{:S(2)}, u32[]{:S(2)}) collective-permute-start(bf16[104,768]{1,0:T(8,128)(2,1)S(1)} %get-tuple-element.35), channel_id=1, source_target_pairs={{0,24},{8,0},{16,8},{24,16},{1,25},{9,1},{17,9},{25,17},{2,26},{10... | collective-permute-start | bytes 479240 | tf_op jit(solution)/shard_map/ppermute | solution.py:19
  122.9 6.0 %collective-permute-done.30 = bf16[104,768]{1,0:T(8,128)(2,1)S(1)} collective-permute-done((bf16[104,768]{1,0:T(8,128)(2,1)S(1)}, bf16[104,768]{1,0:T(8,128)(2,1)S(1)}, u32[]{:S(2)}, u32[]{:S(2)}) %collective-permute-start.30) | collective-permute-done | bytes 159776 | tf_op jit(solution)/shard_map/ppermute | solution.py:19
  128.9 7.4 %collective-permute-start.40 = (bf16[104,384]{1,0:T(8,128)(2,1)S(1)}, bf16[104,384]{1,0:T(8,128)(2,1)S(1)}, u32[]{:S(2)}, u32[]{:S(2)}) collective-permute-start(bf16[104,384]{1,0:T(8,128)(2,1)S(1)} %fusion.5.refs_0_), channel_id=1, source_target_pairs={{0,24},{8,0},{16,8},{24,16},{1,25},{9,1},{17,9},{25,17},{2,26},{10... | collective-permute-start | bytes 239624 | tf_op jit(solution)/shard_map/ppermute | solution.py:19
  136.6 2.9 %collective-permute-start.33 = (bf16[104,384]{1,0:T(8,128)(2,1)S(1)}, bf16[104,384]{1,0:T(8,128)(2,1)S(1)}, u32[]{:S(2)}, u32[]{:S(2)}) collective-permute-start(bf16[104,384]{1,0:T(8,128)(2,1)S(1)} %fusion.7.refs_0_), channel_id=1, source_target_pairs={{0,16},{8,24},{16,0},{24,8},{1,17},{9,25},{17,1},{25,9},{2,18},{10... | collective-permute-start | bytes 239624 | tf_op jit(solution)/shard_map/ppermute | solution.py:19
  139.5 8.5 %collective-permute-start.32 = (bf16[104,384]{1,0:T(8,128)(2,1)S(1)}, bf16[104,384]{1,0:T(8,128)(2,1)S(1)}, u32[]{:S(2)}, u32[]{:S(2)}) collective-permute-start(bf16[104,384]{1,0:T(8,128)(2,1)S(1)} %fusion.7.refs_0_), channel_id=1, source_target_pairs={{0,8},{8,16},{16,24},{24,0},{1,9},{9,17},{17,25},{25,1},{2,10},{10... | collective-permute-start | bytes 239624 | tf_op jit(solution)/shard_map/ppermute | solution.py:19
  148.3 4.7 %collective-permute-start.28 = (bf16[104,384]{1,0:T(8,128)(2,1)S(1)}, bf16[104,384]{1,0:T(8,128)(2,1)S(1)}, u32[]{:S(2)}, u32[]{:S(2)}) collective-permute-start(bf16[104,384]{1,0:T(8,128)(2,1)S(1)} %fusion.9.refs_0_), channel_id=1, source_target_pairs={{0,24},{8,0},{16,8},{24,16},{1,25},{9,1},{17,9},{25,17},{2,26},{10... | collective-permute-start | bytes 239624 | tf_op jit(solution)/shard_map/ppermute | solution.py:19
  153.0 1.6 collective-permute-start.27
  154.6 1.3 shard_map.128
  156.5 1.3 shard_map.130
  158.7 4.0 %collective-permute-done.26.refs_1_ = bf16[104,384]{1,0:T(8,128)(2,1)S(1)} collective-permute-done((bf16[104,384]{1,0:T(8,128)(2,1)S(1)}, bf16[104,384]{1,0:T(8,128)(2,1)S(1)}, u32[]{:S(2)}, u32[]{:S(2)}) %collective-permute-start.26) | collective-permute-done | bytes 79904 | tf_op jit(solution)/shard_map/ppermute | solution.py:19
  162.7 1.3 shard_map.126
  164.6 1.5 collective-permute-done.41
  166.1 0.7 collective-permute-start.42
  166.9 2.3 %collective-permute-start.44 = (bf16[32,1024]{1,0:T(8,128)(2,1)S(1)}, bf16[32,1024]{1,0:T(8,128)(2,1)S(1)}, u32[]{:S(2)}, u32[]{:S(2)}) collective-permute-start(bf16[32,1024]{1,0:T(8,128)(2,1)S(1)} %get-tuple-element.58), channel_id=1, source_target_pairs={{0,6},{1,7},{2,4},{3,5},{4,2},{5,3},{6,0},{7,1},{8,14},{9,15},{10,... | collective-permute-start | bytes 196616 | tf_op jit(solution)/shard_map/ppermute | solution.py:23
  169.7 0.7 copy.46
  170.9 1.9 %collective-permute-done.44 = bf16[32,1024]{1,0:T(8,128)(2,1)S(1)} collective-permute-done((bf16[32,1024]{1,0:T(8,128)(2,1)S(1)}, bf16[32,1024]{1,0:T(8,128)(2,1)S(1)}, u32[]{:S(2)}, u32[]{:S(2)}) %collective-permute-start.44) | collective-permute-done | bytes 65568 | tf_op jit(solution)/shard_map/ppermute | solution.py:23
  172.8 0.9 collective-permute-done.43
  173.8 0.7 copy.37
  (110 shorter events, 7.4 us)
Async XLA Ops:
  2.4 10.4 %collective-permute-start.14 = (f32[32,16]{0,1:T(8,128)S(1)}, f32[32,16]{0,1:T(8,128)S(1)}, u32[]{:S(2)}, u32[]{:S(2)}) collective-permute-start(f32[32,16]{0,1:T(8,128)S(1)} %constant_dynamic-update-slice_fusion), channel_id=1, source_target_pairs={{0,6},{1,7},{2,4},{3,5},{4,2},{5,3},{6,0},{7,1},{8,14},{9,15},{10,... | collective-permute-start | bytes 6152 | tf_op jit(solution)/shard_map/ppermute | solution.py:23
  6.3 7.6 %collective-permute-start.13 = (f32[32,16]{0,1:T(8,128)S(1)}, f32[32,16]{0,1:T(8,128)S(1)}, u32[]{:S(2)}, u32[]{:S(2)}) collective-permute-start(f32[32,16]{0,1:T(8,128)S(1)} %constant_dynamic-update-slice_fusion), channel_id=1, source_target_pairs={{0,4},{1,5},{2,6},{3,7},{4,0},{5,1},{6,2},{7,3},{8,12},{9,13},{10,... | collective-permute-start | bytes 6152 | tf_op jit(solution)/shard_map/ppermute | solution.py:23
  6.8 7.1 %collective-permute-start.12 = (f32[32,16]{0,1:T(8,128)S(1)}, f32[32,16]{0,1:T(8,128)S(1)}, u32[]{:S(2)}, u32[]{:S(2)}) collective-permute-start(f32[32,16]{0,1:T(8,128)S(1)} %constant_dynamic-update-slice_fusion), channel_id=1, source_target_pairs={{0,2},{1,3},{2,0},{3,1},{4,6},{5,7},{6,4},{7,5},{8,10},{9,11},{10,... | collective-permute-start | bytes 6152 | tf_op jit(solution)/shard_map/ppermute | solution.py:23
  7.9 9.2 %collective-permute-start.2 = (bf16[8,64,128]{2,1,0:T(8,128)(2,1)S(1)}, bf16[8,64,128]{2,1,0:T(8,128)(2,1)S(1)}, u32[]{:S(2)}, u32[]{:S(2)}) collective-permute-start(bf16[8,64,128]{2,1,0:T(8,128)(2,1)S(1)} %bitcast.202), channel_id=1, source_target_pairs={{0,24},{8,0},{16,8},{24,16},{1,25},{9,1},{17,9},{25,17},{2,26},{10... | collective-permute-start | bytes 393224 | tf_op jit(solution)/shard_map/ppermute | solution.py:19
  11.9 10.8 %collective-permute-start.1 = (bf16[8,64,128]{2,1,0:T(8,128)(2,1)S(1)}, bf16[8,64,128]{2,1,0:T(8,128)(2,1)S(1)}, u32[]{:S(2)}, u32[]{:S(2)}) collective-permute-start(bf16[8,64,128]{2,1,0:T(8,128)(2,1)S(1)} %bitcast.203), channel_id=1, source_target_pairs={{0,16},{8,24},{16,0},{24,8},{1,17},{9,25},{17,1},{25,9},{2,18},{10... | collective-permute-start | bytes 393224 | tf_op jit(solution)/shard_map/ppermute | solution.py:19
  12.8 9.9 %collective-permute-start = (bf16[8,64,128]{2,1,0:T(8,128)(2,1)S(1)}, bf16[8,64,128]{2,1,0:T(8,128)(2,1)S(1)}, u32[]{:S(2)}, u32[]{:S(2)}) collective-permute-start(bf16[8,64,128]{2,1,0:T(8,128)(2,1)S(1)} %bitcast.204), channel_id=1, source_target_pairs={{0,8},{8,16},{16,24},{24,0},{1,9},{9,17},{17,25},{25,1},{2,10},{10... | collective-permute-start | bytes 393224 | tf_op jit(solution)/shard_map/ppermute | solution.py:19
  14.0 2.8 %collective-permute-start.15 = (f32[128,16]{0,1:T(8,128)S(1)}, f32[128,16]{0,1:T(8,128)S(1)}, u32[]{:S(2)}, u32[]{:S(2)}) collective-permute-start(f32[128,16]{0,1:T(8,128)S(1)} %pad_maximum_fusion), channel_id=1, source_target_pairs={{0,1},{1,0},{2,3},{3,2},{4,5},{5,4},{6,7},{7,6},{8,9},{9,8},{10,11... | collective-permute-start | bytes 24584 | tf_op jit(solution)/shard_map/ppermute | solution.py:23
  14.0 1.0 copy-start.3
  15.0 0.7 copy-start.5
  22.7 1.2 copy-start.6
  25.3 7.3 %collective-permute-start.3 = (f32[2,8,64]{2,1,0:T(8,128)S(1)}, f32[2,8,64]{2,1,0:T(8,128)S(1)}, u32[]{:S(2)}, u32[]{:S(2)}) collective-permute-start(f32[2,8,64]{2,1,0:T(8,128)S(1)} %get-tuple-element.65), channel_id=1, source_target_pairs={{0,24},{8,0},{16,8},{24,16},{1,25},{9,1},{17,9},{25,17},{2,26},{10... | collective-permute-start | bytes 12296 | tf_op jit(solution)/shard_map/ppermute | solution.py:19
  26.5 6.1 %collective-permute-start.5 = (f32[2,8,64]{2,1,0:T(8,128)S(1)}, f32[2,8,64]{2,1,0:T(8,128)S(1)}, u32[]{:S(2)}, u32[]{:S(2)}) collective-permute-start(f32[2,8,64]{2,1,0:T(8,128)S(1)} %get-tuple-element.66), channel_id=1, source_target_pairs={{0,8},{8,16},{16,24},{24,0},{1,9},{9,17},{17,25},{25,1},{2,10},{10... | collective-permute-start | bytes 12296 | tf_op jit(solution)/shard_map/ppermute | solution.py:19
  27.3 5.3 %collective-permute-start.4 = (f32[2,8,64]{2,1,0:T(8,128)S(1)}, f32[2,8,64]{2,1,0:T(8,128)S(1)}, u32[]{:S(2)}, u32[]{:S(2)}) collective-permute-start(f32[2,8,64]{2,1,0:T(8,128)S(1)} %get-tuple-element.67), channel_id=1, source_target_pairs={{0,16},{8,24},{16,0},{24,8},{1,17},{9,25},{17,1},{25,9},{2,18},{10... | collective-permute-start | bytes 12296 | tf_op jit(solution)/shard_map/ppermute | solution.py:19
  29.8 6.1 %collective-permute-start.6 = (bf16[8,64,128]{2,1,0:T(8,128)(2,1)S(1)}, bf16[8,64,128]{2,1,0:T(8,128)(2,1)S(1)}, u32[]{:S(2)}, u32[]{:S(2)}) collective-permute-start(bf16[8,64,128]{2,1,0:T(8,128)(2,1)S(1)} %get-tuple-element.27), channel_id=1, source_target_pairs={{0,24},{8,0},{16,8},{24,16},{1,25},{9,1},{17,9},{25,17},{2,26},{10... | collective-permute-start | bytes 393224 | tf_op jit(solution)/shard_map/ppermute | solution.py:19
  30.7 11.7 %collective-permute-start.7 = (bf16[8,64,128]{2,1,0:T(8,128)(2,1)S(1)}, bf16[8,64,128]{2,1,0:T(8,128)(2,1)S(1)}, u32[]{:S(2)}, u32[]{:S(2)}) collective-permute-start(bf16[8,64,128]{2,1,0:T(8,128)(2,1)S(1)} %get-tuple-element.28), channel_id=1, source_target_pairs={{0,16},{8,24},{16,0},{24,8},{1,17},{9,25},{17,1},{25,9},{2,18},{10... | collective-permute-start | bytes 393224 | tf_op jit(solution)/shard_map/ppermute | solution.py:19
  32.6 9.9 %collective-permute-start.8 = (bf16[8,64,128]{2,1,0:T(8,128)(2,1)S(1)}, bf16[8,64,128]{2,1,0:T(8,128)(2,1)S(1)}, u32[]{:S(2)}, u32[]{:S(2)}) collective-permute-start(bf16[8,64,128]{2,1,0:T(8,128)(2,1)S(1)} %get-tuple-element.29), channel_id=1, source_target_pairs={{0,8},{8,16},{16,24},{24,0},{1,9},{9,17},{17,25},{25,1},{2,10},{10... | collective-permute-start | bytes 393224 | tf_op jit(solution)/shard_map/ppermute | solution.py:19
  43.0 5.6 %collective-permute-start.11 = (bf16[8,8192]{1,0:T(8,128)(2,1)S(1)}, bf16[8,8192]{1,0:T(8,128)(2,1)S(1)}, u32[]{:S(2)}, u32[]{:S(2)}) collective-permute-start(bf16[8,8192]{1,0:T(8,128)(2,1)S(1)} %bitcast.197), channel_id=1, source_target_pairs={{0,24},{8,0},{16,8},{24,16},{1,25},{9,1},{17,9},{25,17},{2,26},{10... | collective-permute-start | bytes 393224 | tf_op jit(solution)/shard_map/ppermute | solution.py:19
  43.1 13.4 %collective-permute-start.10 = (bf16[8,8192]{1,0:T(8,128)(2,1)S(1)}, bf16[8,8192]{1,0:T(8,128)(2,1)S(1)}, u32[]{:S(2)}, u32[]{:S(2)}) collective-permute-start(bf16[8,8192]{1,0:T(8,128)(2,1)S(1)} %bitcast.198), channel_id=1, source_target_pairs={{0,16},{8,24},{16,0},{24,8},{1,17},{9,25},{17,1},{25,9},{2,18},{10... | collective-permute-start | bytes 393224 | tf_op jit(solution)/shard_map/ppermute | solution.py:19
  44.8 11.7 %collective-permute-start.9 = (bf16[8,8192]{1,0:T(8,128)(2,1)S(1)}, bf16[8,8192]{1,0:T(8,128)(2,1)S(1)}, u32[]{:S(2)}, u32[]{:S(2)}) collective-permute-start(bf16[8,8192]{1,0:T(8,128)(2,1)S(1)} %bitcast.199), channel_id=1, source_target_pairs={{0,8},{8,16},{16,24},{24,0},{1,9},{9,17},{17,25},{25,1},{2,10},{10... | collective-permute-start | bytes 393224 | tf_op jit(solution)/shard_map/ppermute | solution.py:19
  56.5 5.8 %copy-start.2 = (bf16[8192,1024]{1,0:T(8,128)(2,1)S(1)}, bf16[8192,1024]{1,0:T(8,128)(2,1)}, u32[]{:S(2)}) copy-start(bf16[8192,1024]{1,0:T(8,128)(2,1)} %refs_4_.6) | copy-start | bytes 50331652
  62.3 0.7 copy-start.4
  66.9 7.4 %collective-permute-start.18 = (bf16[32,1152]{1,0:T(8,128)(2,1)S(1)}, bf16[32,1152]{1,0:T(8,128)(2,1)S(1)}, u32[]{:S(2)}, u32[]{:S(2)}) collective-permute-start(bf16[32,1152]{1,0:T(8,128)(2,1)S(1)} %get-tuple-element.31), channel_id=1, source_target_pairs={{0,6},{1,7},{2,4},{3,5},{4,2},{5,3},{6,0},{7,1},{8,14},{9,15},{10,... | collective-permute-start | bytes 221192 | tf_op jit(solution)/shard_map/ppermute | solution.py:23
  69.4 4.9 %collective-permute-start.17 = (bf16[32,1152]{1,0:T(8,128)(2,1)S(1)}, bf16[32,1152]{1,0:T(8,128)(2,1)S(1)}, u32[]{:S(2)}, u32[]{:S(2)}) collective-permute-start(bf16[32,1152]{1,0:T(8,128)(2,1)S(1)} %get-tuple-element.31), channel_id=1, source_target_pairs={{0,4},{1,5},{2,6},{3,7},{4,0},{5,1},{6,2},{7,3},{8,12},{9,13},{10,... | collective-permute-start | bytes 221192 | tf_op jit(solution)/shard_map/ppermute | solution.py:23
  69.9 4.4 %collective-permute-start.16 = (bf16[32,1152]{1,0:T(8,128)(2,1)S(1)}, bf16[32,1152]{1,0:T(8,128)(2,1)S(1)}, u32[]{:S(2)}, u32[]{:S(2)}) collective-permute-start(bf16[32,1152]{1,0:T(8,128)(2,1)S(1)} %get-tuple-element.31), channel_id=1, source_target_pairs={{0,2},{1,3},{2,0},{3,1},{4,6},{5,7},{6,4},{7,5},{8,10},{9,11},{10,... | collective-permute-start | bytes 221192 | tf_op jit(solution)/shard_map/ppermute | solution.py:23
  74.3 1.6 collective-permute-start.19
  76.1 27.3 %collective-permute-start.25 = (f32[256]{0:T(256)S(1)}, f32[256]{0:T(256)S(1)}, u32[]{:S(2)}, u32[]{:S(2)}) collective-permute-start(f32[256]{0:T(256)S(1)} %convert_reduce_fusion), channel_id=1, source_target_pairs={{0,24},{8,0},{16,8},{24,16},{1,25},{9,1},{17,9},{25,17},{2,26},{10... | collective-permute-start | bytes 3080 | tf_op jit(solution)/shard_map/ppermute | solution.py:19
  76.1 29.8 %collective-permute-start.24 = (f32[256]{0:T(256)S(1)}, f32[256]{0:T(256)S(1)}, u32[]{:S(2)}, u32[]{:S(2)}) collective-permute-start(f32[256]{0:T(256)S(1)} %convert_reduce_fusion), channel_id=1, source_target_pairs={{0,16},{8,24},{16,0},{24,8},{1,17},{9,25},{17,1},{25,9},{2,18},{10... | collective-permute-start | bytes 3080 | tf_op jit(solution)/shard_map/ppermute | solution.py:19
  77.1 28.8 %collective-permute-start.23 = (f32[256]{0:T(256)S(1)}, f32[256]{0:T(256)S(1)}, u32[]{:S(2)}, u32[]{:S(2)}) collective-permute-start(f32[256]{0:T(256)S(1)} %convert_reduce_fusion), channel_id=1, source_target_pairs={{0,8},{8,16},{16,24},{24,0},{1,9},{9,17},{17,25},{25,1},{2,10},{10... | collective-permute-start | bytes 3080 | tf_op jit(solution)/shard_map/ppermute | solution.py:19
  79.1 6.4 %copy-start = (bf16[3,1024,3072]{2,1,0:T(8,128)(2,1)S(1)}, bf16[3,1024,3072]{2,1,0:T(8,128)(2,1)}, u32[]{:S(2)}) copy-start(bf16[3,1024,3072]{2,1,0:T(8,128)(2,1)} %up_ref.5) | copy-start | bytes 56623108
  88.5 18.7 %collective-permute-start.35 = (bf16[104,768]{1,0:T(8,128)(2,1)S(1)}, bf16[104,768]{1,0:T(8,128)(2,1)S(1)}, u32[]{:S(2)}, u32[]{:S(2)}) collective-permute-start(bf16[104,768]{1,0:T(8,128)(2,1)S(1)} %get-tuple-element.41), channel_id=1, source_target_pairs={{0,8},{8,16},{16,24},{24,0},{1,9},{9,17},{17,25},{25,1},{2,10},{10... | collective-permute-start | bytes 479240 | tf_op jit(solution)/shard_map/ppermute | solution.py:19
  89.1 21.0 %collective-permute-start.36 = (bf16[104,768]{1,0:T(8,128)(2,1)S(1)}, bf16[104,768]{1,0:T(8,128)(2,1)S(1)}, u32[]{:S(2)}, u32[]{:S(2)}) collective-permute-start(bf16[104,768]{1,0:T(8,128)(2,1)S(1)} %get-tuple-element.42), channel_id=1, source_target_pairs={{0,16},{8,24},{16,0},{24,8},{1,17},{9,25},{17,1},{25,9},{2,18},{10... | collective-permute-start | bytes 479240 | tf_op jit(solution)/shard_map/ppermute | solution.py:19
  91.0 6.4 %copy-start.1 = (bf16[3,1024,3072]{2,1,0:T(8,128)(2,1)S(1)}, bf16[3,1024,3072]{2,1,0:T(8,128)(2,1)}, u32[]{:S(2)}) copy-start(bf16[3,1024,3072]{2,1,0:T(8,128)(2,1)} %up_ref.5) | copy-start | bytes 56623108
  97.3 57.2 %slice-start = ((s8[9437184]{0:T(1024)(128)(4,1)}), s8[4194304]{0:T(1024)(128)(4,1)S(1)}, s32[]{:S(2)}) async-start(s8[9437184]{0:T(1024)(128)(4,1)} %bitcast.195), calls=%async_computation | async-start | bytes 8388608
  97.3 57.2 %slice-start.1 = ((s8[9437184]{0:T(1024)(128)(4,1)}), s8[4194304]{0:T(1024)(128)(4,1)S(1)}, s32[]{:S(2)}) async-start(s8[9437184]{0:T(1024)(128)(4,1)} %bitcast.195), calls=%async_computation.1 | async-start | bytes 8388608
  100.4 54.2 %slice-start.2 = ((s8[9437184]{0:T(1024)(128)(4,1)}), s8[1048576]{0:T(1024)(128)(4,1)S(1)}, s32[]{:S(2)}) async-start(s8[9437184]{0:T(1024)(128)(4,1)} %bitcast.195), calls=%async_computation.2 | async-start | bytes 2097152
  103.4 8.4 %collective-permute-start.37 = (bf16[104,768]{1,0:T(8,128)(2,1)S(1)}, bf16[104,768]{1,0:T(8,128)(2,1)S(1)}, u32[]{:S(2)}, u32[]{:S(2)}) collective-permute-start(bf16[104,768]{1,0:T(8,128)(2,1)S(1)} %get-tuple-element.43), channel_id=1, source_target_pairs={{0,24},{8,0},{16,8},{24,16},{1,25},{9,1},{17,9},{25,17},{2,26},{10... | collective-permute-start | bytes 479240 | tf_op jit(solution)/shard_map/ppermute | solution.py:19
  106.0 13.0 %collective-permute-start.29 = (bf16[104,768]{1,0:T(8,128)(2,1)S(1)}, bf16[104,768]{1,0:T(8,128)(2,1)S(1)}, u32[]{:S(2)}, u32[]{:S(2)}) collective-permute-start(bf16[104,768]{1,0:T(8,128)(2,1)S(1)} %get-tuple-element.37), channel_id=1, source_target_pairs={{0,8},{8,16},{16,24},{24,0},{1,9},{9,17},{17,25},{25,1},{2,10},{10... | collective-permute-start | bytes 479240 | tf_op jit(solution)/shard_map/ppermute | solution.py:19
  106.0 22.9 %collective-permute-start.30 = (bf16[104,768]{1,0:T(8,128)(2,1)S(1)}, bf16[104,768]{1,0:T(8,128)(2,1)S(1)}, u32[]{:S(2)}, u32[]{:S(2)}) collective-permute-start(bf16[104,768]{1,0:T(8,128)(2,1)S(1)} %get-tuple-element.38), channel_id=1, source_target_pairs={{0,16},{8,24},{16,0},{24,8},{1,17},{9,25},{17,1},{25,9},{2,18},{10... | collective-permute-start | bytes 479240 | tf_op jit(solution)/shard_map/ppermute | solution.py:19
  107.2 29.0 %collective-permute-start.31 = (bf16[104,768]{1,0:T(8,128)(2,1)S(1)}, bf16[104,768]{1,0:T(8,128)(2,1)S(1)}, u32[]{:S(2)}, u32[]{:S(2)}) collective-permute-start(bf16[104,768]{1,0:T(8,128)(2,1)S(1)} %get-tuple-element.39), channel_id=1, source_target_pairs={{0,24},{8,0},{16,8},{24,16},{1,25},{9,1},{17,9},{25,17},{2,26},{10... | collective-permute-start | bytes 479240 | tf_op jit(solution)/shard_map/ppermute | solution.py:19
  110.1 26.3 %collective-permute-start.20 = (bf16[104,768]{1,0:T(8,128)(2,1)S(1)}, bf16[104,768]{1,0:T(8,128)(2,1)S(1)}, u32[]{:S(2)}, u32[]{:S(2)}) collective-permute-start(bf16[104,768]{1,0:T(8,128)(2,1)S(1)} %get-tuple-element.33), channel_id=1, source_target_pairs={{0,8},{8,16},{16,24},{24,0},{1,9},{9,17},{17,25},{25,1},{2,10},{10... | collective-permute-start | bytes 479240 | tf_op jit(solution)/shard_map/ppermute | solution.py:19
  111.8 24.7 %collective-permute-start.21 = (bf16[104,768]{1,0:T(8,128)(2,1)S(1)}, bf16[104,768]{1,0:T(8,128)(2,1)S(1)}, u32[]{:S(2)}, u32[]{:S(2)}) collective-permute-start(bf16[104,768]{1,0:T(8,128)(2,1)S(1)} %get-tuple-element.34), channel_id=1, source_target_pairs={{0,16},{8,24},{16,0},{24,8},{1,17},{9,25},{17,1},{25,9},{2,18},{10... | collective-permute-start | bytes 479240 | tf_op jit(solution)/shard_map/ppermute | solution.py:19
  118.9 20.6 %collective-permute-start.22 = (bf16[104,768]{1,0:T(8,128)(2,1)S(1)}, bf16[104,768]{1,0:T(8,128)(2,1)S(1)}, u32[]{:S(2)}, u32[]{:S(2)}) collective-permute-start(bf16[104,768]{1,0:T(8,128)(2,1)S(1)} %get-tuple-element.35), channel_id=1, source_target_pairs={{0,24},{8,0},{16,8},{24,16},{1,25},{9,1},{17,9},{25,17},{2,26},{10... | collective-permute-start | bytes 479240 | tf_op jit(solution)/shard_map/ppermute | solution.py:19
  128.9 27.4 %collective-permute-start.40 = (bf16[104,384]{1,0:T(8,128)(2,1)S(1)}, bf16[104,384]{1,0:T(8,128)(2,1)S(1)}, u32[]{:S(2)}, u32[]{:S(2)}) collective-permute-start(bf16[104,384]{1,0:T(8,128)(2,1)S(1)} %fusion.5.refs_0_), channel_id=1, source_target_pairs={{0,24},{8,0},{16,8},{24,16},{1,25},{9,1},{17,9},{25,17},{2,26},{10... | collective-permute-start | bytes 239624 | tf_op jit(solution)/shard_map/ppermute | solution.py:19
  136.2 20.3 %collective-permute-start.39 = (bf16[104,384]{1,0:T(8,128)(2,1)S(1)}, bf16[104,384]{1,0:T(8,128)(2,1)S(1)}, u32[]{:S(2)}, u32[]{:S(2)}) collective-permute-start(bf16[104,384]{1,0:T(8,128)(2,1)S(1)} %fusion.5.refs_0_), channel_id=1, source_target_pairs={{0,16},{8,24},{16,0},{24,8},{1,17},{9,25},{17,1},{25,9},{2,18},{10... | collective-permute-start | bytes 239624 | tf_op jit(solution)/shard_map/ppermute | solution.py:19
  136.4 11.8 %collective-permute-start.34 = (bf16[104,384]{1,0:T(8,128)(2,1)S(1)}, bf16[104,384]{1,0:T(8,128)(2,1)S(1)}, u32[]{:S(2)}, u32[]{:S(2)}) collective-permute-start(bf16[104,384]{1,0:T(8,128)(2,1)S(1)} %fusion.7.refs_0_), channel_id=1, source_target_pairs={{0,24},{8,0},{16,8},{24,16},{1,25},{9,1},{17,9},{25,17},{2,26},{10... | collective-permute-start | bytes 239624 | tf_op jit(solution)/shard_map/ppermute | solution.py:19
  136.6 11.7 %collective-permute-start.33 = (bf16[104,384]{1,0:T(8,128)(2,1)S(1)}, bf16[104,384]{1,0:T(8,128)(2,1)S(1)}, u32[]{:S(2)}, u32[]{:S(2)}) collective-permute-start(bf16[104,384]{1,0:T(8,128)(2,1)S(1)} %fusion.7.refs_0_), channel_id=1, source_target_pairs={{0,16},{8,24},{16,0},{24,8},{1,17},{9,25},{17,1},{25,9},{2,18},{10... | collective-permute-start | bytes 239624 | tf_op jit(solution)/shard_map/ppermute | solution.py:19
  139.5 13.5 %collective-permute-start.32 = (bf16[104,384]{1,0:T(8,128)(2,1)S(1)}, bf16[104,384]{1,0:T(8,128)(2,1)S(1)}, u32[]{:S(2)}, u32[]{:S(2)}) collective-permute-start(bf16[104,384]{1,0:T(8,128)(2,1)S(1)} %fusion.7.refs_0_), channel_id=1, source_target_pairs={{0,8},{8,16},{16,24},{24,0},{1,9},{9,17},{17,25},{25,1},{2,10},{10... | collective-permute-start | bytes 239624 | tf_op jit(solution)/shard_map/ppermute | solution.py:19
  148.2 8.3 %collective-permute-start.38 = (bf16[104,384]{1,0:T(8,128)(2,1)S(1)}, bf16[104,384]{1,0:T(8,128)(2,1)S(1)}, u32[]{:S(2)}, u32[]{:S(2)}) collective-permute-start(bf16[104,384]{1,0:T(8,128)(2,1)S(1)} %fusion.5.refs_0_), channel_id=1, source_target_pairs={{0,8},{8,16},{16,24},{24,0},{1,9},{9,17},{17,25},{25,1},{2,10},{10... | collective-permute-start | bytes 239624 | tf_op jit(solution)/shard_map/ppermute | solution.py:19
  148.3 9.9 %collective-permute-start.28 = (bf16[104,384]{1,0:T(8,128)(2,1)S(1)}, bf16[104,384]{1,0:T(8,128)(2,1)S(1)}, u32[]{:S(2)}, u32[]{:S(2)}) collective-permute-start(bf16[104,384]{1,0:T(8,128)(2,1)S(1)} %fusion.9.refs_0_), channel_id=1, source_target_pairs={{0,24},{8,0},{16,8},{24,16},{1,25},{9,1},{17,9},{25,17},{2,26},{10... | collective-permute-start | bytes 239624 | tf_op jit(solution)/shard_map/ppermute | solution.py:19
  153.0 5.7 %collective-permute-start.27 = (bf16[104,384]{1,0:T(8,128)(2,1)S(1)}, bf16[104,384]{1,0:T(8,128)(2,1)S(1)}, u32[]{:S(2)}, u32[]{:S(2)}) collective-permute-start(bf16[104,384]{1,0:T(8,128)(2,1)S(1)} %fusion.9.refs_0_), channel_id=1, source_target_pairs={{0,16},{8,24},{16,0},{24,8},{1,17},{9,25},{17,1},{25,9},{2,18},{10... | collective-permute-start | bytes 239624 | tf_op jit(solution)/shard_map/ppermute | solution.py:19
  156.3 6.5 %collective-permute-start.26 = (bf16[104,384]{1,0:T(8,128)(2,1)S(1)}, bf16[104,384]{1,0:T(8,128)(2,1)S(1)}, u32[]{:S(2)}, u32[]{:S(2)}) collective-permute-start(bf16[104,384]{1,0:T(8,128)(2,1)S(1)} %fusion.9.refs_0_), channel_id=1, source_target_pairs={{0,8},{8,16},{16,24},{24,0},{1,9},{9,17},{17,25},{25,1},{2,10},{10... | collective-permute-start | bytes 239624 | tf_op jit(solution)/shard_map/ppermute | solution.py:19
  164.4 1.6 collective-permute-start.41
  166.1 4.7 %collective-permute-start.42 = (bf16[32,1024]{1,0:T(8,128)(2,1)S(1)}, bf16[32,1024]{1,0:T(8,128)(2,1)S(1)}, u32[]{:S(2)}, u32[]{:S(2)}) collective-permute-start(bf16[32,1024]{1,0:T(8,128)(2,1)S(1)} %get-tuple-element.57), channel_id=1, source_target_pairs={{0,2},{1,3},{2,0},{3,1},{4,6},{5,7},{6,4},{7,5},{8,10},{9,11},{10,... | collective-permute-start | bytes 196616 | tf_op jit(solution)/shard_map/ppermute | solution.py:23
  166.9 6.0 %collective-permute-start.44 = (bf16[32,1024]{1,0:T(8,128)(2,1)S(1)}, bf16[32,1024]{1,0:T(8,128)(2,1)S(1)}, u32[]{:S(2)}, u32[]{:S(2)}) collective-permute-start(bf16[32,1024]{1,0:T(8,128)(2,1)S(1)} %get-tuple-element.58), channel_id=1, source_target_pairs={{0,6},{1,7},{2,4},{3,5},{4,2},{5,3},{6,0},{7,1},{8,14},{9,15},{10,... | collective-permute-start | bytes 196616 | tf_op jit(solution)/shard_map/ppermute | solution.py:23
  169.2 4.5 %collective-permute-start.43 = (bf16[32,1024]{1,0:T(8,128)(2,1)S(1)}, bf16[32,1024]{1,0:T(8,128)(2,1)S(1)}, u32[]{:S(2)}, u32[]{:S(2)}) collective-permute-start(bf16[32,1024]{1,0:T(8,128)(2,1)S(1)} %get-tuple-element.59), channel_id=1, source_target_pairs={{0,4},{1,5},{2,6},{3,7},{4,0},{5,1},{6,2},{7,3},{8,12},{9,13},{10,... | collective-permute-start | bytes 196616 | tf_op jit(solution)/shard_map/ppermute | solution.py:23

commit v2 on v1

--- a/solution.py
+++ b/solution.py
@@ -13,6 +13,7 @@
 NEGATIVE = -1e30
 EPSILON = 1e-06
 MIB = 1 << 20
+SCOPED = 10 * MIB
 
 
 def send(array, axis, size, shift):
@@ -86,7 +87,12 @@
 
 
 VMEM_SPEC = pl.BlockSpec(memory_space=pltpu.VMEM)
+ANY_SPEC = pl.BlockSpec(memory_space=pl.ANY)
 SMEM_SPEC = pl.BlockSpec(memory_space=pltpu.SMEM)
+
+
+def in_hbm(array):
+    return pltpu.with_memory_space_constraint(array, pltpu.HBM)
 
 
 def prompt_part(queries, cache):
@@ -98,7 +104,7 @@
         + [jax.ShapeDtypeStruct((samples // 2, 2, shape[0], 2 * shape[1]), jnp.float32)],
         in_specs=[VMEM_SPEC] * (samples + 1),
         out_specs=[VMEM_SPEC] * (samples + 1),
-        compiler_params=pltpu.CompilerParams(vmem_limit_bytes=32 * MIB),
+        compiler_params=pltpu.CompilerParams(vmem_limit_bytes=SCOPED),
         cost_estimate=pl.CostEstimate(
             flops=1000 * 1000 * 1000, bytes_accessed=4 * MIB, transcendentals=500 * 1000
         ),
@@ -120,7 +126,7 @@
         ],
         in_specs=[SMEM_SPEC, VMEM_SPEC, VMEM_SPEC],
         out_specs=[VMEM_SPEC, VMEM_SPEC],
-        compiler_params=pltpu.CompilerParams(vmem_limit_bytes=32 * MIB),
+        compiler_params=pltpu.CompilerParams(vmem_limit_bytes=SCOPED),
         cost_estimate=pl.CostEstimate(
             flops=100 * 1000 * 1000, bytes_accessed=2 * MIB, transcendentals=100 * 1000
         ),
@@ -129,35 +135,40 @@
 
 def project_kernel(samples, features, place_ref, *refs):
     attended_refs = refs[:samples]
-    weight_ref, residual_ref, gain_ref, mixed_ref, row_ref, total_ref, order_ref = refs[samples:]
-    step = pl.program_id(0)
+    weight_ref, residual_ref, gain_ref, mixed_ref, row_ref, order_ref, held_ref, sems = refs[samples:]
     prompts = attended_refs[0].shape[0]
-
-    @pl.when(step == 0)
-    def _():
-        total_ref[...] = jnp.zeros_like(total_ref)
-
+    pieces = sems.shape[0]
+    depth = weight_ref.shape[0] // pieces
+    copies = []
+    for i in range(pieces):
+        piece = pl.ds(i * depth, depth)
+        copies.append(pltpu.make_async_copy(weight_ref.at[piece], held_ref.at[piece], sems.at[i]))
+        copies[i].start()
     stacked = jnp.concatenate([r[...] for r in attended_refs], axis=0)
-    total_ref[...] += jnp.dot(stacked, weight_ref[...], preferred_element_type=jnp.float32)
-
-    @pl.when(step == pl.num_programs(0) - 1)
-    def _():
-        for k in range(samples):
-            s = lax.rem(place_ref[0] - k + samples, samples)
-            order_ref[pl.ds(pl.multiple_of(s * prompts, prompts), prompts), :] = total_ref[
-                k * prompts : (k + 1) * prompts, :
-            ]
-        projected = order_ref[...]
-        mixed_ref[...] = projected.astype(jnp.bfloat16)
-        stream = residual_ref[...].astype(jnp.float32) + projected
-        square = jnp.sum(stream * stream, axis=1, keepdims=True)
-        high = square.astype(jnp.bfloat16).astype(jnp.float32)
-        low = square - high
-        row_ref[:, :features] = (stream * gain_ref[...]).astype(jnp.bfloat16)
-        lane = lax.broadcasted_iota(jnp.int32, (square.shape[0], HDIM), 1)
-        row_ref[:, features:] = jnp.where(
-            lane == 0, high, jnp.where(lane == 1, low, 0.0)
-        ).astype(jnp.bfloat16)
+    total = jnp.zeros(order_ref.shape, jnp.float32)
+    for i in range(pieces):
+        copies[i].wait()
+        total = total + jnp.dot(
+            stacked[:, i * depth : (i + 1) * depth],
+            held_ref[i * depth : (i + 1) * depth, :],
+            preferred_element_type=jnp.float32,
+        )
+    for k in range(samples):
+        s = lax.rem(place_ref[0] - k + samples, samples)
+        order_ref[pl.ds(pl.multiple_of(s * prompts, prompts), prompts), :] = total[
+            k * prompts : (k + 1) * prompts, :
+        ]
+    projected = order_ref[...]
+    mixed_ref[...] = projected.astype(jnp.bfloat16)
+    stream = residual_ref[...].astype(jnp.float32) + projected
+    square = jnp.sum(stream * stream, axis=1, keepdims=True)
+    high = square.astype(jnp.bfloat16).astype(jnp.float32)
+    low = square - high
+    row_ref[:, :features] = (stream * gain_ref[...]).astype(jnp.bfloat16)
+    lane = lax.broadcasted_iota(jnp.int32, (square.shape[0], HDIM), 1)
+    row_ref[:, features:] = jnp.where(lane == 0, high, jnp.where(lane == 1, low, 0.0)).astype(
+        jnp.bfloat16
+    )
 
 
 def project(attended, out_proj, residual, gain, place):
@@ -165,59 +176,53 @@
     prompts, inner = attended[0].shape
     width = out_proj.shape[1]
     rows = samples * prompts
-    depth = 1024
-    whole = lambda shape: pl.BlockSpec(shape, lambda i, place: (0, 0))
     return pl.pallas_call(
         functools.partial(project_kernel, samples, width),
         out_shape=[
             jax.ShapeDtypeStruct((rows, width), jnp.bfloat16),
             jax.ShapeDtypeStruct((rows, width + HDIM), jnp.bfloat16),
         ],
-        grid_spec=pltpu.PrefetchScalarGridSpec(
-            num_scalar_prefetch=1,
-            grid=(inner // depth,),
-            in_specs=[pl.BlockSpec((prompts, depth), lambda i, place: (0, i))] * samples
-            + [
-                pl.BlockSpec((depth, width), lambda i, place: (i, 0)),
-                whole((rows, width)),
-                whole((1, width)),
-            ],
-            out_specs=[whole((rows, width)), whole((rows, width + HDIM))],
-            scratch_shapes=[
-                pltpu.VMEM((rows, width), jnp.float32),
-                pltpu.VMEM((rows, width), jnp.float32),
-            ],
-        ),
-        compiler_params=pltpu.CompilerParams(vmem_limit_bytes=32 * MIB),
+        in_specs=[SMEM_SPEC] + [VMEM_SPEC] * samples + [ANY_SPEC] + [VMEM_SPEC] * 2,
+        out_specs=[VMEM_SPEC] * 2,
+        scratch_shapes=[
+            pltpu.VMEM((rows, width), jnp.float32),
+            pltpu.VMEM(out_proj.shape, jnp.bfloat16),
+            pltpu.SemaphoreType.DMA((8,)),
+        ],
+        compiler_params=pltpu.CompilerParams(vmem_limit_bytes=SCOPED + 2 * inner * width),
         cost_estimate=pl.CostEstimate(
             flops=2 * rows * inner * width, bytes_accessed=2 * inner * width, transcendentals=0
         ),
-    )(place, *attended, out_proj, residual, gain)
-
-
-def gate_kernel(features, place_ref, pick_ref, near_ref, far_ref, gate_ref, up_ref, *rest):
-    out_refs, chosen_ref = rest[:-1], rest[-1]
-    step = pl.program_id(0)
+    )(place, *attended, in_hbm(out_proj), residual, gain)
+
+
+def gate_kernel(features, expert, place_ref, pick_ref, near_ref, far_ref, weight_ref, *refs):
+    out_refs, held_ref, sems = refs[:-2], refs[-2], refs[-1]
     half = near_ref.shape[0]
-
-    @pl.when(step == 0)
-    def _():
-        pick = pick_ref[...]
-        chosen = jnp.dot(
-            pick[:, :half], near_ref[:, :features], preferred_element_type=jnp.float32
-        ) + jnp.dot(pick[:, half:], far_ref[:, :features], preferred_element_type=jnp.float32)
-        chosen_ref[...] = chosen.astype(jnp.bfloat16)
-
-    chosen = chosen_ref[...]
-    part = gate_ref.shape[1]
-    gate = jnp.dot(chosen, gate_ref[...], preferred_element_type=jnp.float32)
-    up = jnp.dot(chosen, up_ref[...], preferred_element_type=jnp.float32)
-    for k, out_ref in enumerate(out_refs):
-
-        @pl.when(step == (k - 1) % len(out_refs))
-        def _():
-            out_ref[:, :part] = gate.astype(jnp.bfloat16)
-            out_ref[:, part:] = up.astype(jnp.bfloat16)
+    samples = len(out_refs)
+    hidden = weight_ref.shape[2] // 2
+    part = hidden // samples
+    order = list(range(1, samples)) + [0]
+    copies = {}
+    for k in order:
+        column = lax.rem(place_ref[0] + k, samples) * part
+        for side in range(2):
+            columns = pl.ds(pl.multiple_of(side * hidden + column, HDIM), part)
+            copies[k, side] = pltpu.make_async_copy(
+                weight_ref.at[expert, :, columns], held_ref.at[k, side], sems.at[k, side]
+            )
+            copies[k, side].start()
+    pick = pick_ref[...]
+    chosen = jnp.dot(
+        pick[:, :half], near_ref[:, :features], preferred_element_type=jnp.float32
+    ) + jnp.dot(pick[:, half:], far_ref[:, :features], preferred_element_type=jnp.float32)
+    chosen = chosen.astype(jnp.bfloat16)
+    for k in order:
+        for side in range(2):
+            copies[k, side].wait()
+            out_refs[k][:, side * part : (side + 1) * part] = jnp.dot(
+                chosen, held_ref[k, side], preferred_element_type=jnp.float32
+            ).astype(jnp.bfloat16)
 
 
 def gate_up_parts(pick, near, far, weights, expert, place, samples):
@@ -235,50 +240,36 @@
         shares = shares.astype(jnp.bfloat16).reshape(slots, 2, samples, part)
         shares = jnp.roll(shares, -place[0], axis=2)
         return [shares[:, :, k].reshape(slots, 2 * part) for k in range(samples)]
-    whole = lambda shape: pl.BlockSpec(shape, lambda i, place: (0, 0))
-    column = lambda i, place: lax.rem(place[0] + i + 1, samples)
     return pl.pallas_call(
-        functools.partial(gate_kernel, features),
+        functools.partial(gate_kernel, features, expert),
         out_shape=[jax.ShapeDtypeStruct((slots, 2 * part), jnp.bfloat16)] * samples,
-        grid_spec=pltpu.PrefetchScalarGridSpec(
-            num_scalar_prefetch=1,
-            grid=(samples,),
-            in_specs=[
-                whole(pick.shape),
-                whole(near.shape),
-                whole(far.shape),
-                pl.BlockSpec(
-                    (None, features, part), lambda i, place: (expert, 0, column(i, place))
-                ),
-                pl.BlockSpec(
-                    (None, features, part), lambda i, place: (expert, 0, samples + column(i, place))
-                ),
-            ],
-            out_specs=[whole((slots, 2 * part))] * samples,
-            scratch_shapes=[pltpu.VMEM((slots, features), jnp.bfloat16)],
-        ),
-        compiler_params=pltpu.CompilerParams(vmem_limit_bytes=32 * MIB),
+        in_specs=[SMEM_SPEC] + [VMEM_SPEC] * 3 + [ANY_SPEC],
+        out_specs=[VMEM_SPEC] * samples,
+        scratch_shapes=[
+            pltpu.VMEM((samples, 2, features, part), jnp.bfloat16),
+            pltpu.SemaphoreType.DMA((samples, 2)),
+        ],
+        compiler_params=pltpu.CompilerParams(vmem_limit_bytes=SCOPED + 2 * features * wide),
         cost_estimate=pl.CostEstimate(
             flops=2 * slots * features * wide, bytes_accessed=2 * features * wide, transcendentals=0
         ),
-    )(place, pick, near, far, weights, weights)
-
-
-def down_kernel(place_ref, *refs):
-    samples = len(refs) - 3
-    act_refs, (weight_ref, out_ref, total_ref) = refs[:samples], refs[samples:]
-    step = pl.program_id(0)
+    )(place, pick, near, far, in_hbm(weights))
+
+
+def down_kernel(expert, place_ref, *refs):
+    samples = len(refs) - 2
+    act_refs, (weight_ref, out_ref) = refs[:samples], refs[samples:]
+    part = act_refs[0].shape[1]
+    total = None
     for k, act_ref in enumerate(act_refs):
-
-        @pl.when(step == k)
-        def _():
-            share = jnp.dot(act_ref[...], weight_ref[...], preferred_element_type=jnp.float32)
-            if k == 0:
-                total_ref[...] = share
-            elif k < samples - 1:
-                total_ref[...] += share
-            else:
-                out_ref[...] = (total_ref[...] + share).astype(jnp.bfloat16)
+        row = lax.rem(place_ref[0] - k + samples, samples) * part
+        share = jnp.dot(
+            act_ref[...],
+            weight_ref[expert, pl.ds(pl.multiple_of(row, HDIM), part), :],
+            preferred_element_type=jnp.float32,
+        )
+        total = share if total is None else total + share
+    out_ref[...] = total.astype(jnp.bfloat16)
 
 
 def down_rows(acts, weights, expert, place):
@@ -291,24 +282,12 @@
         return jnp.dot(joined, weights[expert], preferred_element_type=jnp.float32).astype(
             jnp.bfloat16
         )
-    whole = lambda shape: pl.BlockSpec(shape, lambda i, place: (0, 0))
     return pl.pallas_call(
-        down_kernel,
+        functools.partial(down_kernel, expert),
         out_shape=jax.ShapeDtypeStruct((slots, width), jnp.bfloat16),
-        grid_spec=pltpu.PrefetchScalarGridSpec(
-            num_scalar_prefetch=1,
-            grid=(samples,),
-            in_specs=[whole((slots, part))] * samples
-            + [
-                pl.BlockSpec(
-                    (None, part, width),
-                    lambda i, place: (expert, lax.rem(place[0] - i + samples, samples), 0),
-                )
-            ],
-            out_specs=whole((slots, width)),
-            scratch_shapes=[pltpu.VMEM((slots, width), jnp.float32)],
-        ),
-        compiler_params=pltpu.CompilerParams(vmem_limit_bytes=32 * MIB),
+        in_specs=[SMEM_SPEC] + [VMEM_SPEC] * (samples + 1),
+        out_specs=VMEM_SPEC,
+        compiler_params=pltpu.CompilerParams(vmem_limit_bytes=SCOPED),
         cost_estimate=pl.CostEstimate(
             flops=2 * slots * hidden * width, bytes_accessed=2 * hidden * width, transcendentals=0
         ),

time: 175 us -> 159 us (0.909)
  local copies, waits for them, and re-layouts: 27.1 us -> 8.6 us
  starting transfers between devices: 76.5 us -> 72.9 us
  Pallas kernels: 19.2 us -> 22.6 us
  waiting for transfers between devices: 47 us -> 50 us
    unnamed x27 -> x21, local copies, waits for them, and re-layouts: 23.9 us -> 5.36 us
    ppermute x33, starting transfers between devices: 64.7 us -> 60.6 us  [send(): lax.ppermute(array, axis, [(i, (i + shift) % size) for i in range(size)])]
    ppermute x33, waiting for transfers between devices: 37 us -> 40 us  [send(): lax.ppermute(array, axis, [(i, (i + shift) % size) for i in range(size)])]
    pallas_call x1, Pallas kernels: 3.91 us -> 6.49 us  [project(): pl.pallas_call(functools.partial(project_kernel, samples, width), out_sha...]
  transfers between devices with their start and end apart: 45 -> 45, of which waited for: 16 -> 16; matrix products, arithmetic and copies ran while one was open for 3% -> 3% of each run, Pallas kernels for 7% -> 9%
where the time goes in v2:
time: 159 us
  starting transfers between devices  72.9 us (46%)
  waiting for transfers between devices  50 us (31%)
  Pallas kernels  22.6 us (14%)
  local copies, waits for them, and re-layouts  8.6 us (5%)
  other arithmetic  2.4 us (2%)
    ppermute x33, starting transfers between devices, send(): lax.ppermute(array, axis, [(i, (i + shift) % size) for i in range(size)])  60.6 us
    ppermute x33, waiting for transfers between devices, send(): lax.ppermute(array, axis, [(i, (i + shift) % size) for i in range(size)])  40 us
    ppermute x12, starting transfers between devices, swap(): return lax.ppermute(array, axis, [(i, i ^ bits) for i in range(size)])  12.3 us
    pallas_call x3, Pallas kernels, gate_up_parts(): pl.pallas_call(functools.partial(gate_kernel, features, expert), out_shap...  11.7 us
    ppermute x12, waiting for transfers between devices, swap(): return lax.ppermute(array, axis, [(i, i ^ bits) for i in range(size)])  9.99 us
    pallas_call x1, Pallas kernels, project(): pl.pallas_call(functools.partial(project_kernel, samples, width), out_sha...  6.49 us
    unnamed x21, local copies, waits for them, and re-layouts  5.36 us
  transfers between devices with their start and end apart: 45, of which 16 were waited for; matrix products, arithmetic and copies ran while one was open for 3% of the time, Pallas kernels for 9%

profile of v2, /device:TPU:0, one launch (start us, length us, event | category | flops | bytes accessed | tf_op | source)
XLA Modules:
  0.0 158.6 jit_solution(13761898059997302567)
XLA Ops:
  0.6 0.7 convert_bitcast_fusion
  1.5 0.8 copy.34
  2.4 3.9 %collective-permute-start.14 = (f32[32,16]{0,1:T(8,128)S(1)}, f32[32,16]{0,1:T(8,128)S(1)}, u32[]{:S(2)}, u32[]{:S(2)}) collective-permute-start(f32[32,16]{0,1:T(8,128)S(1)} %constant_dynamic-update-slice_fusion), channel_id=1, source_target_pairs={{0,6},{1,7},{2,4},{3,5},{4,2},{5,3},{6,0},{7,1},{8,14},{9,15},{10,... | collective-permute-start | bytes 6152 | tf_op jit(solution)/shard_map/ppermute | solution.py:24
  7.0 0.9 copy.45
  7.9 4.1 %collective-permute-start.2 = (bf16[8,64,128]{2,1,0:T(8,128)(2,1)S(1)}, bf16[8,64,128]{2,1,0:T(8,128)(2,1)S(1)}, u32[]{:S(2)}, u32[]{:S(2)}) collective-permute-start(bf16[8,64,128]{2,1,0:T(8,128)(2,1)S(1)} %bitcast.202), channel_id=1, source_target_pairs={{0,24},{8,0},{16,8},{24,16},{1,25},{9,1},{17,9},{25,17},{2,26},{10... | collective-permute-start | bytes 393224 | tf_op jit(solution)/shard_map/ppermute | solution.py:20
  11.9 0.9 copy.47
  12.8 1.1 collective-permute-start
  14.0 1.0 copy-done
  15.0 0.7 copy-done.2
  15.7 1.1 shard_map.122
  17.0 5.7 %collective-permute-done.1.refs_2_ = bf16[8,64,128]{2,1,0:T(8,128)(2,1)S(1)} collective-permute-done((bf16[8,64,128]{2,1,0:T(8,128)(2,1)S(1)}, bf16[8,64,128]{2,1,0:T(8,128)(2,1)S(1)}, u32[]{:S(2)}, u32[]{:S(2)}) %collective-permute-start.1) | collective-permute-done | bytes 131104 | tf_op jit(solution)/shard_map/ppermute | solution.py:20
  22.7 1.2 copy-done.3
  24.0 1.3 shard_map.123
  25.3 1.2 collective-permute-start.3
  26.5 0.8 collective-permute-start.5
  27.3 2.2 %collective-permute-start.4 = (f32[2,8,64]{2,1,0:T(8,128)S(1)}, f32[2,8,64]{2,1,0:T(8,128)S(1)}, u32[]{:S(2)}, u32[]{:S(2)}) collective-permute-start(f32[2,8,64]{2,1,0:T(8,128)S(1)} %get-tuple-element.67), channel_id=1, source_target_pairs={{0,16},{8,24},{16,0},{24,8},{1,17},{9,25},{17,1},{25,9},{2,18},{10... | collective-permute-start | bytes 12296 | tf_op jit(solution)/shard_map/ppermute | solution.py:20
  29.8 1.0 collective-permute-start.6
  30.7 1.9 %collective-permute-start.7 = (bf16[8,64,128]{2,1,0:T(8,128)(2,1)S(1)}, bf16[8,64,128]{2,1,0:T(8,128)(2,1)S(1)}, u32[]{:S(2)}, u32[]{:S(2)}) collective-permute-start(bf16[8,64,128]{2,1,0:T(8,128)(2,1)S(1)} %get-tuple-element.28), channel_id=1, source_target_pairs={{0,16},{8,24},{16,0},{24,8},{1,17},{9,25},{17,1},{25,9},{2,18},{10... | collective-permute-start | bytes 393224 | tf_op jit(solution)/shard_map/ppermute | solution.py:20
  32.7 3.2 %collective-permute-done.6 = bf16[8,64,128]{2,1,0:T(8,128)(2,1)S(1)} collective-permute-done((bf16[8,64,128]{2,1,0:T(8,128)(2,1)S(1)}, bf16[8,64,128]{2,1,0:T(8,128)(2,1)S(1)}, u32[]{:S(2)}, u32[]{:S(2)}) %collective-permute-start.6) | collective-permute-done | bytes 131104 | tf_op jit(solution)/shard_map/ppermute | solution.py:20
  35.9 6.6 %collective-permute-done.7 = bf16[8,64,128]{2,1,0:T(8,128)(2,1)S(1)} collective-permute-done((bf16[8,64,128]{2,1,0:T(8,128)(2,1)S(1)}, bf16[8,64,128]{2,1,0:T(8,128)(2,1)S(1)}, u32[]{:S(2)}, u32[]{:S(2)}) %collective-permute-start.7) | collective-permute-done | bytes 131104 | tf_op jit(solution)/shard_map/ppermute | solution.py:20
  43.1 1.6 %collective-permute-start.10 = (bf16[8,8192]{1,0:T(8,128)(2,1)S(1)}, bf16[8,8192]{1,0:T(8,128)(2,1)S(1)}, u32[]{:S(2)}, u32[]{:S(2)}) collective-permute-start(bf16[8,8192]{1,0:T(8,128)(2,1)S(1)} %bitcast.198), channel_id=1, source_target_pairs={{0,16},{8,24},{16,0},{24,8},{1,17},{9,25},{17,1},{25,9},{2,18},{10... | collective-permute-start | bytes 393224 | tf_op jit(solution)/shard_map/ppermute | solution.py:20
  44.8 1.9 %collective-permute-start.9 = (bf16[8,8192]{1,0:T(8,128)(2,1)S(1)}, bf16[8,8192]{1,0:T(8,128)(2,1)S(1)}, u32[]{:S(2)}, u32[]{:S(2)}) collective-permute-start(bf16[8,8192]{1,0:T(8,128)(2,1)S(1)} %bitcast.199), channel_id=1, source_target_pairs={{0,8},{8,16},{16,24},{24,0},{1,9},{9,17},{17,25},{25,1},{2,10},{10... | collective-permute-start | bytes 393224 | tf_op jit(solution)/shard_map/ppermute | solution.py:20
  46.8 1.8 %collective-permute-done.11.refs_3_ = bf16[8,8192]{1,0:T(8,128)(2,1)S(1)} collective-permute-done((bf16[8,8192]{1,0:T(8,128)(2,1)S(1)}, bf16[8,8192]{1,0:T(8,128)(2,1)S(1)}, u32[]{:S(2)}, u32[]{:S(2)}) %collective-permute-start.11) | collective-permute-done | bytes 131104 | tf_op jit(solution)/shard_map/ppermute | solution.py:20
  48.6 8.0 %collective-permute-done.10.refs_2_ = bf16[8,8192]{1,0:T(8,128)(2,1)S(1)} collective-permute-done((bf16[8,8192]{1,0:T(8,128)(2,1)S(1)}, bf16[8,8192]{1,0:T(8,128)(2,1)S(1)}, u32[]{:S(2)}, u32[]{:S(2)}) %collective-permute-start.10) | collective-permute-done | bytes 131104 | tf_op jit(solution)/shard_map/ppermute | solution.py:20
  56.5 0.7 copy-done.1
  57.2 6.5 %shard_map.124 = (bf16[32,1024]{1,0:T(8,128)(2,1)S(1)}, bf16[32,1152]{1,0:T(8,128)(2,1)S(1)}) custom-call(s32[1]{0:T(128)} %bitcast.place_ref, bf16[8,8192]{1,0:T(8,128)(2,1)S(1)} %bitcast.200, bf16[8,8192]{1,0:T(8,128)(2,1)S(1)} %collective-permute-done.9.refs_1_, bf16[8,8192]{1,0:T(8,128)(2,1)S(1)} %collective-permute-done.10.refs_2_, ...), custom_call_target="tpu_custom_call" | custom-call | flops 536870912 | bytes 16777216 | tf_op jit(solution)/shard_map/pallas_call | solution.py:179
  63.7 2.5 %collective-permute-start.18 = (bf16[32,1152]{1,0:T(8,128)(2,1)S(1)}, bf16[32,1152]{1,0:T(8,128)(2,1)S(1)}, u32[]{:S(2)}, u32[]{:S(2)}) collective-permute-start(bf16[32,1152]{1,0:T(8,128)(2,1)S(1)} %get-tuple-element.31), channel_id=1, source_target_pairs={{0,6},{1,7},{2,4},{3,5},{4,2},{5,3},{6,0},{7,1},{8,14},{9,15},{10,... | collective-permute-start | bytes 221192 | tf_op jit(solution)/shard_map/ppermute | solution.py:24
  66.7 0.5 collective-permute-start.16
  67.3 3.8 %collective-permute-done.16 = bf16[32,1152]{1,0:T(8,128)(2,1)S(1)} collective-permute-done((bf16[32,1152]{1,0:T(8,128)(2,1)S(1)}, bf16[32,1152]{1,0:T(8,128)(2,1)S(1)}, u32[]{:S(2)}, u32[]{:S(2)}) %collective-permute-start.16) | collective-permute-done | bytes 73760 | tf_op jit(solution)/shard_map/ppermute | solution.py:24
  71.4 1.4 collective-permute-done.19.far_ref
  73.0 1.0 collective-permute-start.24
  74.0 1.9 %collective-permute-start.23 = (f32[256]{0:T(256)S(1)}, f32[256]{0:T(256)S(1)}, u32[]{:S(2)}, u32[]{:S(2)}) collective-permute-start(f32[256]{0:T(256)S(1)} %convert_reduce_fusion), channel_id=1, source_target_pairs={{0,8},{8,16},{16,24},{24,0},{1,9},{9,17},{17,25},{25,1},{2,10},{10... | collective-permute-start | bytes 3080 | tf_op jit(solution)/shard_map/ppermute | solution.py:20
  75.9 3.7 %shard_map.129 = (bf16[104,768]{1,0:T(8,128)(2,1)S(1)}, bf16[104,768]{1,0:T(8,128)(2,1)S(1)}, bf16[104,768]{1,0:T(8,128)(2,1)S(1)}, bf16[104,768]{1,0:T(8,128)(2,1)S(1)}) custom-call(s32[1]{0:T(128)} %bitcast.place_ref, bf16[104,256]{1,0:T(8,128)(2,1)S(1)} %get-tuple-element.61.pick_ref, bf16[128,1152]{1,0:T(8,128)(2,1)S(1)} %constant_dynamic-update-slice_fusion.2.near_ref, ...), custom_call_target="tpu_custom_call" | custom-call | flops 654311424 | bytes 6291456 | tf_op jit(solution)/shard_map/pallas_call | solution.py:243
  79.6 0.9 collective-permute-start.35
  80.4 1.8 %collective-permute-start.36 = (bf16[104,768]{1,0:T(8,128)(2,1)S(1)}, bf16[104,768]{1,0:T(8,128)(2,1)S(1)}, u32[]{:S(2)}, u32[]{:S(2)}) collective-permute-start(bf16[104,768]{1,0:T(8,128)(2,1)S(1)} %get-tuple-element.42), channel_id=1, source_target_pairs={{0,16},{8,24},{16,0},{24,8},{1,17},{9,25},{17,1},{25,9},{2,18},{10... | collective-permute-start | bytes 479240 | tf_op jit(solution)/shard_map/ppermute | solution.py:20
  82.2 3.8 %shard_map.127 = (bf16[104,768]{1,0:T(8,128)(2,1)S(1)}, bf16[104,768]{1,0:T(8,128)(2,1)S(1)}, bf16[104,768]{1,0:T(8,128)(2,1)S(1)}, bf16[104,768]{1,0:T(8,128)(2,1)S(1)}) custom-call(s32[1]{0:T(128)} %bitcast.place_ref, bf16[104,256]{1,0:T(8,128)(2,1)S(1)} %get-tuple-element.62.pick_ref, bf16[128,1152]{1,0:T(8,128)(2,1)S(1)} %constant_dynamic-update-slice_fusion.2.near_ref, ...), custom_call_target="tpu_custom_call" | custom-call | flops 654311424 | bytes 6291456 | tf_op jit(solution)/shard_map/pallas_call | solution.py:243
  86.1 4.3 %shard_map.125 = (bf16[104,768]{1,0:T(8,128)(2,1)S(1)}, bf16[104,768]{1,0:T(8,128)(2,1)S(1)}, bf16[104,768]{1,0:T(8,128)(2,1)S(1)}, bf16[104,768]{1,0:T(8,128)(2,1)S(1)}) custom-call(s32[1]{0:T(128)} %bitcast.place_ref, bf16[104,256]{1,0:T(8,128)(2,1)S(1)} %get-tuple-element.60.pick_ref, bf16[128,1152]{1,0:T(8,128)(2,1)S(1)} %constant_dynamic-update-slice_fusion.2.near_ref, ...), custom_call_target="tpu_custom_call" | custom-call | flops 654311424 | bytes 6291456 | tf_op jit(solution)/shard_map/pallas_call | solution.py:243
  90.4 2.5 %collective-permute-start.37 = (bf16[104,768]{1,0:T(8,128)(2,1)S(1)}, bf16[104,768]{1,0:T(8,128)(2,1)S(1)}, u32[]{:S(2)}, u32[]{:S(2)}) collective-permute-start(bf16[104,768]{1,0:T(8,128)(2,1)S(1)} %get-tuple-element.43), channel_id=1, source_target_pairs={{0,24},{8,0},{16,8},{24,16},{1,25},{9,1},{17,9},{25,17},{2,26},{10... | collective-permute-start | bytes 479240 | tf_op jit(solution)/shard_map/ppermute | solution.py:20
  92.9 1.0 collective-permute-start.30
  94.2 2.9 %collective-permute-start.31 = (bf16[104,768]{1,0:T(8,128)(2,1)S(1)}, bf16[104,768]{1,0:T(8,128)(2,1)S(1)}, u32[]{:S(2)}, u32[]{:S(2)}) collective-permute-start(bf16[104,768]{1,0:T(8,128)(2,1)S(1)} %get-tuple-element.39), channel_id=1, source_target_pairs={{0,24},{8,0},{16,8},{24,16},{1,25},{9,1},{17,9},{25,17},{2,26},{10... | collective-permute-start | bytes 479240 | tf_op jit(solution)/shard_map/ppermute | solution.py:20
  97.1 0.6 collective-permute-start.20
  97.7 4.0 %collective-permute-done.37 = bf16[104,768]{1,0:T(8,128)(2,1)S(1)} collective-permute-done((bf16[104,768]{1,0:T(8,128)(2,1)S(1)}, bf16[104,768]{1,0:T(8,128)(2,1)S(1)}, u32[]{:S(2)}, u32[]{:S(2)}) %collective-permute-start.37) | collective-permute-done | bytes 159776 | tf_op jit(solution)/shard_map/ppermute | solution.py:20
  101.6 4.3 %collective-permute-start.21 = (bf16[104,768]{1,0:T(8,128)(2,1)S(1)}, bf16[104,768]{1,0:T(8,128)(2,1)S(1)}, u32[]{:S(2)}, u32[]{:S(2)}) collective-permute-start(bf16[104,768]{1,0:T(8,128)(2,1)S(1)} %get-tuple-element.34), channel_id=1, source_target_pairs={{0,16},{8,24},{16,0},{24,8},{1,17},{9,25},{17,1},{25,9},{2,18},{10... | collective-permute-start | bytes 479240 | tf_op jit(solution)/shard_map/ppermute | solution.py:20
  106.1 3.9 %collective-permute-start.22 = (bf16[104,768]{1,0:T(8,128)(2,1)S(1)}, bf16[104,768]{1,0:T(8,128)(2,1)S(1)}, u32[]{:S(2)}, u32[]{:S(2)}) collective-permute-start(bf16[104,768]{1,0:T(8,128)(2,1)S(1)} %get-tuple-element.35), channel_id=1, source_target_pairs={{0,24},{8,0},{16,8},{24,16},{1,25},{9,1},{17,9},{25,17},{2,26},{10... | collective-permute-start | bytes 479240 | tf_op jit(solution)/shard_map/ppermute | solution.py:20
  110.1 5.9 %collective-permute-done.30 = bf16[104,768]{1,0:T(8,128)(2,1)S(1)} collective-permute-done((bf16[104,768]{1,0:T(8,128)(2,1)S(1)}, bf16[104,768]{1,0:T(8,128)(2,1)S(1)}, u32[]{:S(2)}, u32[]{:S(2)}) %collective-permute-start.30) | collective-permute-done | bytes 159776 | tf_op jit(solution)/shard_map/ppermute | solution.py:20
  116.0 6.4 %collective-permute-start.40 = (bf16[104,384]{1,0:T(8,128)(2,1)S(1)}, bf16[104,384]{1,0:T(8,128)(2,1)S(1)}, u32[]{:S(2)}, u32[]{:S(2)}) collective-permute-start(bf16[104,384]{1,0:T(8,128)(2,1)S(1)} %fusion.5.refs_0_), channel_id=1, source_target_pairs={{0,24},{8,0},{16,8},{24,16},{1,25},{9,1},{17,9},{25,17},{2,26},{10... | collective-permute-start | bytes 239624 | tf_op jit(solution)/shard_map/ppermute | solution.py:20
  122.5 0.9 collective-permute-start.34
  123.7 2.0 %collective-permute-start.33 = (bf16[104,384]{1,0:T(8,128)(2,1)S(1)}, bf16[104,384]{1,0:T(8,128)(2,1)S(1)}, u32[]{:S(2)}, u32[]{:S(2)}) collective-permute-start(bf16[104,384]{1,0:T(8,128)(2,1)S(1)} %fusion.7.refs_0_), channel_id=1, source_target_pairs={{0,16},{8,24},{16,0},{24,8},{1,17},{9,25},{17,1},{25,9},{2,18},{10... | collective-permute-start | bytes 239624 | tf_op jit(solution)/shard_map/ppermute | solution.py:20
  125.7 9.2 %collective-permute-start.32 = (bf16[104,384]{1,0:T(8,128)(2,1)S(1)}, bf16[104,384]{1,0:T(8,128)(2,1)S(1)}, u32[]{:S(2)}, u32[]{:S(2)}) collective-permute-start(bf16[104,384]{1,0:T(8,128)(2,1)S(1)} %fusion.7.refs_0_), channel_id=1, source_target_pairs={{0,8},{8,16},{16,24},{24,0},{1,9},{9,17},{17,25},{25,1},{2,10},{10... | collective-permute-start | bytes 239624 | tf_op jit(solution)/shard_map/ppermute | solution.py:20
  135.1 4.6 %collective-permute-start.28 = (bf16[104,384]{1,0:T(8,128)(2,1)S(1)}, bf16[104,384]{1,0:T(8,128)(2,1)S(1)}, u32[]{:S(2)}, u32[]{:S(2)}) collective-permute-start(bf16[104,384]{1,0:T(8,128)(2,1)S(1)} %fusion.9.refs_0_), channel_id=1, source_target_pairs={{0,24},{8,0},{16,8},{24,16},{1,25},{9,1},{17,9},{25,17},{2,26},{10... | collective-permute-start | bytes 239624 | tf_op jit(solution)/shard_map/ppermute | solution.py:20
  139.8 0.7 shard_map.128
  140.8 0.6 collective-permute-start.26
  141.4 0.7 shard_map.130
  142.5 3.0 %collective-permute-done.27.refs_2_ = bf16[104,384]{1,0:T(8,128)(2,1)S(1)} collective-permute-done((bf16[104,384]{1,0:T(8,128)(2,1)S(1)}, bf16[104,384]{1,0:T(8,128)(2,1)S(1)}, u32[]{:S(2)}, u32[]{:S(2)}) %collective-permute-start.27) | collective-permute-done | bytes 79904 | tf_op jit(solution)/shard_map/ppermute | solution.py:20
  145.5 1.6 %collective-permute-done.26.refs_1_ = bf16[104,384]{1,0:T(8,128)(2,1)S(1)} collective-permute-done((bf16[104,384]{1,0:T(8,128)(2,1)S(1)}, bf16[104,384]{1,0:T(8,128)(2,1)S(1)}, u32[]{:S(2)}, u32[]{:S(2)}) %collective-permute-start.26) | collective-permute-done | bytes 79904 | tf_op jit(solution)/shard_map/ppermute | solution.py:20
  147.1 0.7 shard_map.126
  148.3 1.5 collective-permute-done.41
  149.9 2.5 %collective-permute-start.42 = (bf16[32,1024]{1,0:T(8,128)(2,1)S(1)}, bf16[32,1024]{1,0:T(8,128)(2,1)S(1)}, u32[]{:S(2)}, u32[]{:S(2)}) collective-permute-start(bf16[32,1024]{1,0:T(8,128)(2,1)S(1)} %get-tuple-element.57), channel_id=1, source_target_pairs={{0,2},{1,3},{2,0},{3,1},{4,6},{5,7},{6,4},{7,5},{8,10},{9,11},{10,... | collective-permute-start | bytes 196616 | tf_op jit(solution)/shard_map/ppermute | solution.py:24
  152.3 0.6 collective-permute-start.44
  152.9 1.0 collective-permute-start.43
  153.9 0.7 copy.46
  154.6 0.7 collective-permute-done.42
  155.2 2.3 %collective-permute-done.44 = bf16[32,1024]{1,0:T(8,128)(2,1)S(1)} collective-permute-done((bf16[32,1024]{1,0:T(8,128)(2,1)S(1)}, bf16[32,1024]{1,0:T(8,128)(2,1)S(1)}, u32[]{:S(2)}, u32[]{:S(2)}) %collective-permute-start.44) | collective-permute-done | bytes 65568 | tf_op jit(solution)/shard_map/ppermute | solution.py:24
  157.9 0.7 copy.37
  (104 shorter events, 6.1 us)
Async XLA Ops:
  2.4 10.4 %collective-permute-start.14 = (f32[32,16]{0,1:T(8,128)S(1)}, f32[32,16]{0,1:T(8,128)S(1)}, u32[]{:S(2)}, u32[]{:S(2)}) collective-permute-start(f32[32,16]{0,1:T(8,128)S(1)} %constant_dynamic-update-slice_fusion), channel_id=1, source_target_pairs={{0,6},{1,7},{2,4},{3,5},{4,2},{5,3},{6,0},{7,1},{8,14},{9,15},{10,... | collective-permute-start | bytes 6152 | tf_op jit(solution)/shard_map/ppermute | solution.py:24
  6.3 7.6 %collective-permute-start.13 = (f32[32,16]{0,1:T(8,128)S(1)}, f32[32,16]{0,1:T(8,128)S(1)}, u32[]{:S(2)}, u32[]{:S(2)}) collective-permute-start(f32[32,16]{0,1:T(8,128)S(1)} %constant_dynamic-update-slice_fusion), channel_id=1, source_target_pairs={{0,4},{1,5},{2,6},{3,7},{4,0},{5,1},{6,2},{7,3},{8,12},{9,13},{10,... | collective-permute-start | bytes 6152 | tf_op jit(solution)/shard_map/ppermute | solution.py:24
  6.8 7.1 %collective-permute-start.12 = (f32[32,16]{0,1:T(8,128)S(1)}, f32[32,16]{0,1:T(8,128)S(1)}, u32[]{:S(2)}, u32[]{:S(2)}) collective-permute-start(f32[32,16]{0,1:T(8,128)S(1)} %constant_dynamic-update-slice_fusion), channel_id=1, source_target_pairs={{0,2},{1,3},{2,0},{3,1},{4,6},{5,7},{6,4},{7,5},{8,10},{9,11},{10,... | collective-permute-start | bytes 6152 | tf_op jit(solution)/shard_map/ppermute | solution.py:24
  7.9 9.2 %collective-permute-start.2 = (bf16[8,64,128]{2,1,0:T(8,128)(2,1)S(1)}, bf16[8,64,128]{2,1,0:T(8,128)(2,1)S(1)}, u32[]{:S(2)}, u32[]{:S(2)}) collective-permute-start(bf16[8,64,128]{2,1,0:T(8,128)(2,1)S(1)} %bitcast.202), channel_id=1, source_target_pairs={{0,24},{8,0},{16,8},{24,16},{1,25},{9,1},{17,9},{25,17},{2,26},{10... | collective-permute-start | bytes 393224 | tf_op jit(solution)/shard_map/ppermute | solution.py:20
  11.9 10.8 %collective-permute-start.1 = (bf16[8,64,128]{2,1,0:T(8,128)(2,1)S(1)}, bf16[8,64,128]{2,1,0:T(8,128)(2,1)S(1)}, u32[]{:S(2)}, u32[]{:S(2)}) collective-permute-start(bf16[8,64,128]{2,1,0:T(8,128)(2,1)S(1)} %bitcast.203), channel_id=1, source_target_pairs={{0,16},{8,24},{16,0},{24,8},{1,17},{9,25},{17,1},{25,9},{2,18},{10... | collective-permute-start | bytes 393224 | tf_op jit(solution)/shard_map/ppermute | solution.py:20
  12.8 9.9 %collective-permute-start = (bf16[8,64,128]{2,1,0:T(8,128)(2,1)S(1)}, bf16[8,64,128]{2,1,0:T(8,128)(2,1)S(1)}, u32[]{:S(2)}, u32[]{:S(2)}) collective-permute-start(bf16[8,64,128]{2,1,0:T(8,128)(2,1)S(1)} %bitcast.204), channel_id=1, source_target_pairs={{0,8},{8,16},{16,24},{24,0},{1,9},{9,17},{17,25},{25,1},{2,10},{10... | collective-permute-start | bytes 393224 | tf_op jit(solution)/shard_map/ppermute | solution.py:20
  14.0 2.8 %collective-permute-start.15 = (f32[128,16]{0,1:T(8,128)S(1)}, f32[128,16]{0,1:T(8,128)S(1)}, u32[]{:S(2)}, u32[]{:S(2)}) collective-permute-start(f32[128,16]{0,1:T(8,128)S(1)} %pad_maximum_fusion), channel_id=1, source_target_pairs={{0,1},{1,0},{2,3},{3,2},{4,5},{5,4},{6,7},{7,6},{8,9},{9,8},{10,11... | collective-permute-start | bytes 24584 | tf_op jit(solution)/shard_map/ppermute | solution.py:24
  14.0 1.0 copy-start
  15.0 0.7 copy-start.2
  22.7 1.2 copy-start.3
  25.3 7.3 %collective-permute-start.3 = (f32[2,8,64]{2,1,0:T(8,128)S(1)}, f32[2,8,64]{2,1,0:T(8,128)S(1)}, u32[]{:S(2)}, u32[]{:S(2)}) collective-permute-start(f32[2,8,64]{2,1,0:T(8,128)S(1)} %get-tuple-element.65), channel_id=1, source_target_pairs={{0,24},{8,0},{16,8},{24,16},{1,25},{9,1},{17,9},{25,17},{2,26},{10... | collective-permute-start | bytes 12296 | tf_op jit(solution)/shard_map/ppermute | solution.py:20
  26.5 6.1 %collective-permute-start.5 = (f32[2,8,64]{2,1,0:T(8,128)S(1)}, f32[2,8,64]{2,1,0:T(8,128)S(1)}, u32[]{:S(2)}, u32[]{:S(2)}) collective-permute-start(f32[2,8,64]{2,1,0:T(8,128)S(1)} %get-tuple-element.66), channel_id=1, source_target_pairs={{0,8},{8,16},{16,24},{24,0},{1,9},{9,17},{17,25},{25,1},{2,10},{10... | collective-permute-start | bytes 12296 | tf_op jit(solution)/shard_map/ppermute | solution.py:20
  27.3 5.3 %collective-permute-start.4 = (f32[2,8,64]{2,1,0:T(8,128)S(1)}, f32[2,8,64]{2,1,0:T(8,128)S(1)}, u32[]{:S(2)}, u32[]{:S(2)}) collective-permute-start(f32[2,8,64]{2,1,0:T(8,128)S(1)} %get-tuple-element.67), channel_id=1, source_target_pairs={{0,16},{8,24},{16,0},{24,8},{1,17},{9,25},{17,1},{25,9},{2,18},{10... | collective-permute-start | bytes 12296 | tf_op jit(solution)/shard_map/ppermute | solution.py:20
  29.8 6.1 %collective-permute-start.6 = (bf16[8,64,128]{2,1,0:T(8,128)(2,1)S(1)}, bf16[8,64,128]{2,1,0:T(8,128)(2,1)S(1)}, u32[]{:S(2)}, u32[]{:S(2)}) collective-permute-start(bf16[8,64,128]{2,1,0:T(8,128)(2,1)S(1)} %get-tuple-element.27), channel_id=1, source_target_pairs={{0,24},{8,0},{16,8},{24,16},{1,25},{9,1},{17,9},{25,17},{2,26},{10... | collective-permute-start | bytes 393224 | tf_op jit(solution)/shard_map/ppermute | solution.py:20
  30.7 11.7 %collective-permute-start.7 = (bf16[8,64,128]{2,1,0:T(8,128)(2,1)S(1)}, bf16[8,64,128]{2,1,0:T(8,128)(2,1)S(1)}, u32[]{:S(2)}, u32[]{:S(2)}) collective-permute-start(bf16[8,64,128]{2,1,0:T(8,128)(2,1)S(1)} %get-tuple-element.28), channel_id=1, source_target_pairs={{0,16},{8,24},{16,0},{24,8},{1,17},{9,25},{17,1},{25,9},{2,18},{10... | collective-permute-start | bytes 393224 | tf_op jit(solution)/shard_map/ppermute | solution.py:20
  32.6 9.9 %collective-permute-start.8 = (bf16[8,64,128]{2,1,0:T(8,128)(2,1)S(1)}, bf16[8,64,128]{2,1,0:T(8,128)(2,1)S(1)}, u32[]{:S(2)}, u32[]{:S(2)}) collective-permute-start(bf16[8,64,128]{2,1,0:T(8,128)(2,1)S(1)} %get-tuple-element.29), channel_id=1, source_target_pairs={{0,8},{8,16},{16,24},{24,0},{1,9},{9,17},{17,25},{25,1},{2,10},{10... | collective-permute-start | bytes 393224 | tf_op jit(solution)/shard_map/ppermute | solution.py:20
  43.0 5.6 %collective-permute-start.11 = (bf16[8,8192]{1,0:T(8,128)(2,1)S(1)}, bf16[8,8192]{1,0:T(8,128)(2,1)S(1)}, u32[]{:S(2)}, u32[]{:S(2)}) collective-permute-start(bf16[8,8192]{1,0:T(8,128)(2,1)S(1)} %bitcast.197), channel_id=1, source_target_pairs={{0,24},{8,0},{16,8},{24,16},{1,25},{9,1},{17,9},{25,17},{2,26},{10... | collective-permute-start | bytes 393224 | tf_op jit(solution)/shard_map/ppermute | solution.py:20
  43.1 13.4 %collective-permute-start.10 = (bf16[8,8192]{1,0:T(8,128)(2,1)S(1)}, bf16[8,8192]{1,0:T(8,128)(2,1)S(1)}, u32[]{:S(2)}, u32[]{:S(2)}) collective-permute-start(bf16[8,8192]{1,0:T(8,128)(2,1)S(1)} %bitcast.198), channel_id=1, source_target_pairs={{0,16},{8,24},{16,0},{24,8},{1,17},{9,25},{17,1},{25,9},{2,18},{10... | collective-permute-start | bytes 393224 | tf_op jit(solution)/shard_map/ppermute | solution.py:20
  44.8 11.7 %collective-permute-start.9 = (bf16[8,8192]{1,0:T(8,128)(2,1)S(1)}, bf16[8,8192]{1,0:T(8,128)(2,1)S(1)}, u32[]{:S(2)}, u32[]{:S(2)}) collective-permute-start(bf16[8,8192]{1,0:T(8,128)(2,1)S(1)} %bitcast.199), channel_id=1, source_target_pairs={{0,8},{8,16},{16,24},{24,0},{1,9},{9,17},{17,25},{25,1},{2,10},{10... | collective-permute-start | bytes 393224 | tf_op jit(solution)/shard_map/ppermute | solution.py:20
  56.5 0.7 copy-start.1
  63.7 7.4 %collective-permute-start.18 = (bf16[32,1152]{1,0:T(8,128)(2,1)S(1)}, bf16[32,1152]{1,0:T(8,128)(2,1)S(1)}, u32[]{:S(2)}, u32[]{:S(2)}) collective-permute-start(bf16[32,1152]{1,0:T(8,128)(2,1)S(1)} %get-tuple-element.31), channel_id=1, source_target_pairs={{0,6},{1,7},{2,4},{3,5},{4,2},{5,3},{6,0},{7,1},{8,14},{9,15},{10,... | collective-permute-start | bytes 221192 | tf_op jit(solution)/shard_map/ppermute | solution.py:24
  66.2 4.9 %collective-permute-start.17 = (bf16[32,1152]{1,0:T(8,128)(2,1)S(1)}, bf16[32,1152]{1,0:T(8,128)(2,1)S(1)}, u32[]{:S(2)}, u32[]{:S(2)}) collective-permute-start(bf16[32,1152]{1,0:T(8,128)(2,1)S(1)} %get-tuple-element.31), channel_id=1, source_target_pairs={{0,4},{1,5},{2,6},{3,7},{4,0},{5,1},{6,2},{7,3},{8,12},{9,13},{10,... | collective-permute-start | bytes 221192 | tf_op jit(solution)/shard_map/ppermute | solution.py:24
  66.7 4.4 %collective-permute-start.16 = (bf16[32,1152]{1,0:T(8,128)(2,1)S(1)}, bf16[32,1152]{1,0:T(8,128)(2,1)S(1)}, u32[]{:S(2)}, u32[]{:S(2)}) collective-permute-start(bf16[32,1152]{1,0:T(8,128)(2,1)S(1)} %get-tuple-element.31), channel_id=1, source_target_pairs={{0,2},{1,3},{2,0},{3,1},{4,6},{5,7},{6,4},{7,5},{8,10},{9,11},{10,... | collective-permute-start | bytes 221192 | tf_op jit(solution)/shard_map/ppermute | solution.py:24
  71.1 1.6 %collective-permute-start.19 = (bf16[128,1152]{1,0:T(8,128)(2,1)S(1)}, bf16[128,1152]{1,0:T(8,128)(2,1)S(1)}, u32[]{:S(2)}, u32[]{:S(2)}) collective-permute-start(bf16[128,1152]{1,0:T(8,128)(2,1)S(1)} %constant_dynamic-update-slice_fusion.2.near_ref), channel_id=1, source_target_pairs={{0,1},{1,0},{2,3},{3,2},{4,5},{5,4},{6,7},{7,6},{8,9},{9,8},{10,11... | collective-permute-start | bytes 884744 | tf_op jit(solution)/shard_map/ppermute | solution.py:24
  72.9 17.4 %collective-permute-start.25 = (f32[256]{0:T(256)S(1)}, f32[256]{0:T(256)S(1)}, u32[]{:S(2)}, u32[]{:S(2)}) collective-permute-start(f32[256]{0:T(256)S(1)} %convert_reduce_fusion), channel_id=1, source_target_pairs={{0,24},{8,0},{16,8},{24,16},{1,25},{9,1},{17,9},{25,17},{2,26},{10... | collective-permute-start | bytes 3080 | tf_op jit(solution)/shard_map/ppermute | solution.py:20
  73.0 19.9 %collective-permute-start.24 = (f32[256]{0:T(256)S(1)}, f32[256]{0:T(256)S(1)}, u32[]{:S(2)}, u32[]{:S(2)}) collective-permute-start(f32[256]{0:T(256)S(1)} %convert_reduce_fusion), channel_id=1, source_target_pairs={{0,16},{8,24},{16,0},{24,8},{1,17},{9,25},{17,1},{25,9},{2,18},{10... | collective-permute-start | bytes 3080 | tf_op jit(solution)/shard_map/ppermute | solution.py:20
  74.0 18.9 %collective-permute-start.23 = (f32[256]{0:T(256)S(1)}, f32[256]{0:T(256)S(1)}, u32[]{:S(2)}, u32[]{:S(2)}) collective-permute-start(f32[256]{0:T(256)S(1)} %convert_reduce_fusion), channel_id=1, source_target_pairs={{0,8},{8,16},{16,24},{24,0},{1,9},{9,17},{17,25},{25,1},{2,10},{10... | collective-permute-start | bytes 3080 | tf_op jit(solution)/shard_map/ppermute | solution.py:20
  79.6 14.6 %collective-permute-start.35 = (bf16[104,768]{1,0:T(8,128)(2,1)S(1)}, bf16[104,768]{1,0:T(8,128)(2,1)S(1)}, u32[]{:S(2)}, u32[]{:S(2)}) collective-permute-start(bf16[104,768]{1,0:T(8,128)(2,1)S(1)} %get-tuple-element.41), channel_id=1, source_target_pairs={{0,8},{8,16},{16,24},{24,0},{1,9},{9,17},{17,25},{25,1},{2,10},{10... | collective-permute-start | bytes 479240 | tf_op jit(solution)/shard_map/ppermute | solution.py:20
  80.4 16.6 %collective-permute-start.36 = (bf16[104,768]{1,0:T(8,128)(2,1)S(1)}, bf16[104,768]{1,0:T(8,128)(2,1)S(1)}, u32[]{:S(2)}, u32[]{:S(2)}) collective-permute-start(bf16[104,768]{1,0:T(8,128)(2,1)S(1)} %get-tuple-element.42), channel_id=1, source_target_pairs={{0,16},{8,24},{16,0},{24,8},{1,17},{9,25},{17,1},{25,9},{2,18},{10... | collective-permute-start | bytes 479240 | tf_op jit(solution)/shard_map/ppermute | solution.py:20
  82.2 57.5 %slice-start = ((s8[9437184]{0:T(1024)(128)(4,1)}), s8[4194304]{0:T(1024)(128)(4,1)S(1)}, s32[]{:S(2)}) async-start(s8[9437184]{0:T(1024)(128)(4,1)} %bitcast.195), calls=%async_computation | async-start | bytes 8388608
  82.2 57.5 %slice-start.1 = ((s8[9437184]{0:T(1024)(128)(4,1)}), s8[4194304]{0:T(1024)(128)(4,1)S(1)}, s32[]{:S(2)}) async-start(s8[9437184]{0:T(1024)(128)(4,1)} %bitcast.195), calls=%async_computation.1 | async-start | bytes 8388608
  86.1 53.7 %slice-start.2 = ((s8[9437184]{0:T(1024)(128)(4,1)}), s8[1048576]{0:T(1024)(128)(4,1)S(1)}, s32[]{:S(2)}) async-start(s8[9437184]{0:T(1024)(128)(4,1)} %bitcast.195), calls=%async_computation.2 | async-start | bytes 2097152
  90.4 11.3 %collective-permute-start.37 = (bf16[104,768]{1,0:T(8,128)(2,1)S(1)}, bf16[104,768]{1,0:T(8,128)(2,1)S(1)}, u32[]{:S(2)}, u32[]{:S(2)}) collective-permute-start(bf16[104,768]{1,0:T(8,128)(2,1)S(1)} %get-tuple-element.43), channel_id=1, source_target_pairs={{0,24},{8,0},{16,8},{24,16},{1,25},{9,1},{17,9},{25,17},{2,26},{10... | collective-permute-start | bytes 479240 | tf_op jit(solution)/shard_map/ppermute | solution.py:20
  92.9 13.2 %collective-permute-start.29 = (bf16[104,768]{1,0:T(8,128)(2,1)S(1)}, bf16[104,768]{1,0:T(8,128)(2,1)S(1)}, u32[]{:S(2)}, u32[]{:S(2)}) collective-permute-start(bf16[104,768]{1,0:T(8,128)(2,1)S(1)} %get-tuple-element.37), channel_id=1, source_target_pairs={{0,8},{8,16},{16,24},{24,0},{1,9},{9,17},{17,25},{25,1},{2,10},{10... | collective-permute-start | bytes 479240 | tf_op jit(solution)/shard_map/ppermute | solution.py:20
  92.9 23.1 %collective-permute-start.30 = (bf16[104,768]{1,0:T(8,128)(2,1)S(1)}, bf16[104,768]{1,0:T(8,128)(2,1)S(1)}, u32[]{:S(2)}, u32[]{:S(2)}) collective-permute-start(bf16[104,768]{1,0:T(8,128)(2,1)S(1)} %get-tuple-element.38), channel_id=1, source_target_pairs={{0,16},{8,24},{16,0},{24,8},{1,17},{9,25},{17,1},{25,9},{2,18},{10... | collective-permute-start | bytes 479240 | tf_op jit(solution)/shard_map/ppermute | solution.py:20
  94.2 28.2 %collective-permute-start.31 = (bf16[104,768]{1,0:T(8,128)(2,1)S(1)}, bf16[104,768]{1,0:T(8,128)(2,1)S(1)}, u32[]{:S(2)}, u32[]{:S(2)}) collective-permute-start(bf16[104,768]{1,0:T(8,128)(2,1)S(1)} %get-tuple-element.39), channel_id=1, source_target_pairs={{0,24},{8,0},{16,8},{24,16},{1,25},{9,1},{17,9},{25,17},{2,26},{10... | collective-permute-start | bytes 479240 | tf_op jit(solution)/shard_map/ppermute | solution.py:20
  97.1 25.5 %collective-permute-start.20 = (bf16[104,768]{1,0:T(8,128)(2,1)S(1)}, bf16[104,768]{1,0:T(8,128)(2,1)S(1)}, u32[]{:S(2)}, u32[]{:S(2)}) collective-permute-start(bf16[104,768]{1,0:T(8,128)(2,1)S(1)} %get-tuple-element.33), channel_id=1, source_target_pairs={{0,8},{8,16},{16,24},{24,0},{1,9},{9,17},{17,25},{25,1},{2,10},{10... | collective-permute-start | bytes 479240 | tf_op jit(solution)/shard_map/ppermute | solution.py:20
  101.6 22.0 %collective-permute-start.21 = (bf16[104,768]{1,0:T(8,128)(2,1)S(1)}, bf16[104,768]{1,0:T(8,128)(2,1)S(1)}, u32[]{:S(2)}, u32[]{:S(2)}) collective-permute-start(bf16[104,768]{1,0:T(8,128)(2,1)S(1)} %get-tuple-element.34), channel_id=1, source_target_pairs={{0,16},{8,24},{16,0},{24,8},{1,17},{9,25},{17,1},{25,9},{2,18},{10... | collective-permute-start | bytes 479240 | tf_op jit(solution)/shard_map/ppermute | solution.py:20
  106.1 19.6 %collective-permute-start.22 = (bf16[104,768]{1,0:T(8,128)(2,1)S(1)}, bf16[104,768]{1,0:T(8,128)(2,1)S(1)}, u32[]{:S(2)}, u32[]{:S(2)}) collective-permute-start(bf16[104,768]{1,0:T(8,128)(2,1)S(1)} %get-tuple-element.35), channel_id=1, source_target_pairs={{0,24},{8,0},{16,8},{24,16},{1,25},{9,1},{17,9},{25,17},{2,26},{10... | collective-permute-start | bytes 479240 | tf_op jit(solution)/shard_map/ppermute | solution.py:20
  116.0 24.8 %collective-permute-start.40 = (bf16[104,384]{1,0:T(8,128)(2,1)S(1)}, bf16[104,384]{1,0:T(8,128)(2,1)S(1)}, u32[]{:S(2)}, u32[]{:S(2)}) collective-permute-start(bf16[104,384]{1,0:T(8,128)(2,1)S(1)} %fusion.5.refs_0_), channel_id=1, source_target_pairs={{0,24},{8,0},{16,8},{24,16},{1,25},{9,1},{17,9},{25,17},{2,26},{10... | collective-permute-start | bytes 239624 | tf_op jit(solution)/shard_map/ppermute | solution.py:20
  122.3 19.1 %collective-permute-start.39 = (bf16[104,384]{1,0:T(8,128)(2,1)S(1)}, bf16[104,384]{1,0:T(8,128)(2,1)S(1)}, u32[]{:S(2)}, u32[]{:S(2)}) collective-permute-start(bf16[104,384]{1,0:T(8,128)(2,1)S(1)} %fusion.5.refs_0_), channel_id=1, source_target_pairs={{0,16},{8,24},{16,0},{24,8},{1,17},{9,25},{17,1},{25,9},{2,18},{10... | collective-permute-start | bytes 239624 | tf_op jit(solution)/shard_map/ppermute | solution.py:20
  122.5 12.5 %collective-permute-start.34 = (bf16[104,384]{1,0:T(8,128)(2,1)S(1)}, bf16[104,384]{1,0:T(8,128)(2,1)S(1)}, u32[]{:S(2)}, u32[]{:S(2)}) collective-permute-start(bf16[104,384]{1,0:T(8,128)(2,1)S(1)} %fusion.7.refs_0_), channel_id=1, source_target_pairs={{0,24},{8,0},{16,8},{24,16},{1,25},{9,1},{17,9},{25,17},{2,26},{10... | collective-permute-start | bytes 239624 | tf_op jit(solution)/shard_map/ppermute | solution.py:20
  123.7 11.5 %collective-permute-start.33 = (bf16[104,384]{1,0:T(8,128)(2,1)S(1)}, bf16[104,384]{1,0:T(8,128)(2,1)S(1)}, u32[]{:S(2)}, u32[]{:S(2)}) collective-permute-start(bf16[104,384]{1,0:T(8,128)(2,1)S(1)} %fusion.7.refs_0_), channel_id=1, source_target_pairs={{0,16},{8,24},{16,0},{24,8},{1,17},{9,25},{17,1},{25,9},{2,18},{10... | collective-permute-start | bytes 239624 | tf_op jit(solution)/shard_map/ppermute | solution.py:20
  125.7 14.0 %collective-permute-start.32 = (bf16[104,384]{1,0:T(8,128)(2,1)S(1)}, bf16[104,384]{1,0:T(8,128)(2,1)S(1)}, u32[]{:S(2)}, u32[]{:S(2)}) collective-permute-start(bf16[104,384]{1,0:T(8,128)(2,1)S(1)} %fusion.7.refs_0_), channel_id=1, source_target_pairs={{0,8},{8,16},{16,24},{24,0},{1,9},{9,17},{17,25},{25,1},{2,10},{10... | collective-permute-start | bytes 239624 | tf_op jit(solution)/shard_map/ppermute | solution.py:20
  135.1 6.4 %collective-permute-start.38 = (bf16[104,384]{1,0:T(8,128)(2,1)S(1)}, bf16[104,384]{1,0:T(8,128)(2,1)S(1)}, u32[]{:S(2)}, u32[]{:S(2)}) collective-permute-start(bf16[104,384]{1,0:T(8,128)(2,1)S(1)} %fusion.5.refs_0_), channel_id=1, source_target_pairs={{0,8},{8,16},{16,24},{24,0},{1,9},{9,17},{17,25},{25,1},{2,10},{10... | collective-permute-start | bytes 239624 | tf_op jit(solution)/shard_map/ppermute | solution.py:20
  135.1 7.3 %collective-permute-start.28 = (bf16[104,384]{1,0:T(8,128)(2,1)S(1)}, bf16[104,384]{1,0:T(8,128)(2,1)S(1)}, u32[]{:S(2)}, u32[]{:S(2)}) collective-permute-start(bf16[104,384]{1,0:T(8,128)(2,1)S(1)} %fusion.9.refs_0_), channel_id=1, source_target_pairs={{0,24},{8,0},{16,8},{24,16},{1,25},{9,1},{17,9},{25,17},{2,26},{10... | collective-permute-start | bytes 239624 | tf_op jit(solution)/shard_map/ppermute | solution.py:20
  139.7 5.7 %collective-permute-start.27 = (bf16[104,384]{1,0:T(8,128)(2,1)S(1)}, bf16[104,384]{1,0:T(8,128)(2,1)S(1)}, u32[]{:S(2)}, u32[]{:S(2)}) collective-permute-start(bf16[104,384]{1,0:T(8,128)(2,1)S(1)} %fusion.9.refs_0_), channel_id=1, source_target_pairs={{0,16},{8,24},{16,0},{24,8},{1,17},{9,25},{17,1},{25,9},{2,18},{10... | collective-permute-start | bytes 239624 | tf_op jit(solution)/shard_map/ppermute | solution.py:20
  140.8 6.3 %collective-permute-start.26 = (bf16[104,384]{1,0:T(8,128)(2,1)S(1)}, bf16[104,384]{1,0:T(8,128)(2,1)S(1)}, u32[]{:S(2)}, u32[]{:S(2)}) collective-permute-start(bf16[104,384]{1,0:T(8,128)(2,1)S(1)} %fusion.9.refs_0_), channel_id=1, source_target_pairs={{0,8},{8,16},{16,24},{24,0},{1,9},{9,17},{17,25},{25,1},{2,10},{10... | collective-permute-start | bytes 239624 | tf_op jit(solution)/shard_map/ppermute | solution.py:20
  148.2 1.6 %collective-permute-start.41 = (bf16[4,32,1024]{2,1,0:T(8,128)(2,1)S(1)}, bf16[4,32,1024]{2,1,0:T(8,128)(2,1)S(1)}, u32[]{:S(2)}, u32[]{:S(2)}) collective-permute-start(bf16[4,32,1024]{2,1,0:T(8,128)(2,1)S(1)} %bitcast.212), channel_id=1, source_target_pairs={{0,1},{1,0},{2,3},{3,2},{4,5},{5,4},{6,7},{7,6},{8,9},{9,8},{10,11... | collective-permute-start | bytes 786440 | tf_op jit(solution)/shard_map/ppermute | solution.py:24
  149.9 5.4 %collective-permute-start.42 = (bf16[32,1024]{1,0:T(8,128)(2,1)S(1)}, bf16[32,1024]{1,0:T(8,128)(2,1)S(1)}, u32[]{:S(2)}, u32[]{:S(2)}) collective-permute-start(bf16[32,1024]{1,0:T(8,128)(2,1)S(1)} %get-tuple-element.57), channel_id=1, source_target_pairs={{0,2},{1,3},{2,0},{3,1},{4,6},{5,7},{6,4},{7,5},{8,10},{9,11},{10,... | collective-permute-start | bytes 196616 | tf_op jit(solution)/shard_map/ppermute | solution.py:24
  152.3 5.2 %collective-permute-start.44 = (bf16[32,1024]{1,0:T(8,128)(2,1)S(1)}, bf16[32,1024]{1,0:T(8,128)(2,1)S(1)}, u32[]{:S(2)}, u32[]{:S(2)}) collective-permute-start(bf16[32,1024]{1,0:T(8,128)(2,1)S(1)} %get-tuple-element.58), channel_id=1, source_target_pairs={{0,6},{1,7},{2,4},{3,5},{4,2},{5,3},{6,0},{7,1},{8,14},{9,15},{10,... | collective-permute-start | bytes 196616 | tf_op jit(solution)/shard_map/ppermute | solution.py:24
  152.9 5.0 %collective-permute-start.43 = (bf16[32,1024]{1,0:T(8,128)(2,1)S(1)}, bf16[32,1024]{1,0:T(8,128)(2,1)S(1)}, u32[]{:S(2)}, u32[]{:S(2)}) collective-permute-start(bf16[32,1024]{1,0:T(8,128)(2,1)S(1)} %get-tuple-element.59), channel_id=1, source_target_pairs={{0,4},{1,5},{2,6},{3,7},{4,0},{5,1},{6,2},{7,3},{8,12},{9,13},{10,... | collective-permute-start | bytes 196616 | tf_op jit(solution)/shard_map/ppermute | solution.py:24

commit v3 on v2

--- a/solution.py
+++ b/solution.py
@@ -12,6 +12,7 @@
 TOPK = 8
 NEGATIVE = -1e30
 EPSILON = 1e-06
+DIRECT = ()
 MIB = 1 << 20
 SCOPED = 10 * MIB
 
@@ -56,10 +57,10 @@
 
 
 def prompt_kernel(samples, *refs):
-    query_refs, cache_ref = refs[:samples], refs[samples]
-    out_refs, stat_ref = refs[samples + 1 : 2 * samples + 1], refs[2 * samples + 1]
+    query_refs, cache_ref, out_refs = refs[:samples], refs[samples], refs[samples + 1 :]
     prompts, tokens, _ = cache_ref.shape
     heads = query_refs[0].shape[1]
+    marks = [[] for _ in range(samples // 2)]
     for p in range(prompts):
         rows = cache_ref[p]
         keys, values = stacked_heads(rows, 0), stacked_heads(rows, KVHEADS)
@@ -69,8 +70,25 @@
             highest, total, numerator = softmax_part(scores, values)
             out_refs[2 * pair][p] = numerator[:heads].astype(jnp.bfloat16)
             out_refs[2 * pair + 1][p] = numerator[heads:].astype(jnp.bfloat16)
-            stat_ref[pair, 0, p : p + 1, :] = highest
-            stat_ref[pair, 1, p : p + 1, :] = total
+            marks[pair].append((highest, total))
+    for pair, found in enumerate(marks):
+        highest = jnp.concatenate([m[0] for m in found], axis=0)
+        total = jnp.concatenate([m[1] for m in found], axis=0)
+        rows = in_parts(highest, 3) + in_parts(total, 2)
+        spare = out_refs[0].shape[0] * heads - prompts * (heads + len(rows))
+        rows = rows + [jnp.zeros((spare, rows[0].shape[1]), jnp.float32)]
+        slab = jnp.concatenate(rows, axis=0).astype(jnp.bfloat16)
+        for i in range(slab.shape[0] // heads):
+            for k in (2 * pair, 2 * pair + 1):
+                out_refs[k][prompts + i] = slab[i * heads : (i + 1) * heads]
+
+
+def in_parts(values, count):
+    parts = []
+    for _ in range(count):
+        parts.append(values.astype(jnp.bfloat16).astype(jnp.float32))
+        values = values - parts[-1]
+    return parts
 
 
 def gen_kernel(length_ref, query_ref, cache_ref, out_ref, stat_ref):
@@ -97,23 +115,26 @@
 
 def prompt_part(queries, cache):
     samples = len(queries)
-    shape = queries[0].shape
-    results = pl.pallas_call(
+    prompts, heads, _ = queries[0].shape
+    slabs = -(-5 * prompts // heads)
+    return pl.pallas_call(
         functools.partial(prompt_kernel, samples),
-        out_shape=[jax.ShapeDtypeStruct(shape, jnp.bfloat16)] * samples
-        + [jax.ShapeDtypeStruct((samples // 2, 2, shape[0], 2 * shape[1]), jnp.float32)],
+        out_shape=[jax.ShapeDtypeStruct((prompts + slabs, heads, HDIM), jnp.bfloat16)] * samples,
         in_specs=[VMEM_SPEC] * (samples + 1),
-        out_specs=[VMEM_SPEC] * (samples + 1),
+        out_specs=[VMEM_SPEC] * samples,
         compiler_params=pltpu.CompilerParams(vmem_limit_bytes=SCOPED),
         cost_estimate=pl.CostEstimate(
             flops=1000 * 1000 * 1000, bytes_accessed=4 * MIB, transcendentals=500 * 1000
         ),
     )(*queries, cache)
-    stats = results[samples]
-    heads = shape[1]
-    return results[:samples], [
-        stats[k // 2, :, :, (k % 2) * heads : (k % 2 + 1) * heads] for k in range(samples)
-    ]
+
+
+def part_marks(part, prompts, k):
+    heads = part.shape[1]
+    slab = part[prompts:].reshape(-1, HDIM)[:, k % 2 * heads : (k % 2 + 1) * heads]
+    slab = slab.astype(jnp.float32)
+    rows = [slab[i * prompts : (i + 1) * prompts] for i in range(5)]
+    return rows[0] + rows[1] + rows[2], rows[3] + rows[4]
 
 
 def gen_part(query, cache, lengths):
@@ -197,31 +218,32 @@
 
 
 def gate_kernel(features, expert, place_ref, pick_ref, near_ref, far_ref, weight_ref, *refs):
-    out_refs, held_ref, sems = refs[:-2], refs[-2], refs[-1]
+    keep_refs, give_ref, held_ref, sems = refs[:-3], refs[-3], refs[-2], refs[-1]
     half = near_ref.shape[0]
-    samples = len(out_refs)
+    samples = 2 * len(keep_refs)
     hidden = weight_ref.shape[2] // 2
     part = hidden // samples
-    order = list(range(1, samples)) + [0]
+    order = list(range(1, samples, 2)) + list(range(samples - 2, -1, -2))
     copies = {}
-    for k in order:
-        column = lax.rem(place_ref[0] + k, samples) * part
+    for m in order:
+        column = lax.bitwise_xor(place_ref[0], m) * part
         for side in range(2):
             columns = pl.ds(pl.multiple_of(side * hidden + column, HDIM), part)
-            copies[k, side] = pltpu.make_async_copy(
-                weight_ref.at[expert, :, columns], held_ref.at[k, side], sems.at[k, side]
+            copies[m, side] = pltpu.make_async_copy(
+                weight_ref.at[expert, :, columns], held_ref.at[m, side], sems.at[m, side]
             )
-            copies[k, side].start()
+            copies[m, side].start()
     pick = pick_ref[...]
     chosen = jnp.dot(
         pick[:, :half], near_ref[:, :features], preferred_element_type=jnp.float32
     ) + jnp.dot(pick[:, half:], far_ref[:, :features], preferred_element_type=jnp.float32)
     chosen = chosen.astype(jnp.bfloat16)
-    for k in order:
+    for m in order:
+        out_ref = give_ref.at[m // 2] if m % 2 else keep_refs[m // 2]
         for side in range(2):
-            copies[k, side].wait()
-            out_refs[k][:, side * part : (side + 1) * part] = jnp.dot(
-                chosen, held_ref[k, side], preferred_element_type=jnp.float32
+            copies[m, side].wait()
+            out_ref[:, side * part : (side + 1) * part] = jnp.dot(
+                chosen, held_ref[m, side], preferred_element_type=jnp.float32
             ).astype(jnp.bfloat16)
 
 
@@ -238,13 +260,19 @@
         ).astype(jnp.bfloat16)
         shares = jnp.dot(chosen, weights[expert], preferred_element_type=jnp.float32)
         shares = shares.astype(jnp.bfloat16).reshape(slots, 2, samples, part)
-        shares = jnp.roll(shares, -place[0], axis=2)
-        return [shares[:, :, k].reshape(slots, 2 * part) for k in range(samples)]
-    return pl.pallas_call(
+        wanted = (jnp.bitwise_xor(place[0], jnp.arange(samples))[:, None] == jnp.arange(samples)).astype(
+            jnp.bfloat16
+        )
+        shares = jnp.einsum("mn,sgnp->msgp", wanted, shares, preferred_element_type=jnp.float32)
+        shares = shares.astype(jnp.bfloat16).reshape(samples, slots, 2 * part)
+        return [shares[m] for m in range(0, samples, 2)], shares[1::2]
+    one = jax.ShapeDtypeStruct((slots, 2 * part), jnp.bfloat16)
+    results = pl.pallas_call(
         functools.partial(gate_kernel, features, expert),
-        out_shape=[jax.ShapeDtypeStruct((slots, 2 * part), jnp.bfloat16)] * samples,
+        out_shape=[one] * (samples // 2)
+        + [jax.ShapeDtypeStruct((samples // 2, slots, 2 * part), jnp.bfloat16)],
         in_specs=[SMEM_SPEC] + [VMEM_SPEC] * 3 + [ANY_SPEC],
-        out_specs=[VMEM_SPEC] * samples,
+        out_specs=[VMEM_SPEC] * (samples // 2 + 1),
         scratch_shapes=[
             pltpu.VMEM((samples, 2, features, part), jnp.bfloat16),
             pltpu.SemaphoreType.DMA((samples, 2)),
@@ -254,44 +282,95 @@
             flops=2 * slots * features * wide, bytes_accessed=2 * features * wide, transcendentals=0
         ),
     )(place, pick, near, far, in_hbm(weights))
-
-
-def down_kernel(expert, place_ref, *refs):
-    samples = len(refs) - 2
-    act_refs, (weight_ref, out_ref) = refs[:samples], refs[samples:]
-    part = act_refs[0].shape[1]
+    return results[:-1], results[-1]
+
+
+def first_swap(keep, give, samples, direct):
+    if not direct:
+        return swap(give, "sample", samples, 1)
+    shares = [give[m // 2] if m % 2 else keep[m // 2] for m in range(samples)]
+    return [swap(shares[m], "sample", samples, m) for m in range(1, samples)]
+
+
+def reduce_parts(keep, give, arrived, samples, direct):
+    if direct:
+        return sum((a.astype(jnp.float32) for a in arrived), keep[0].astype(jnp.float32))
+    bits = 1
+    while True:
+        keep = [a.astype(jnp.float32) + arrived[i].astype(jnp.float32) for i, a in enumerate(keep)]
+        bits *= 2
+        if bits == samples:
+            return keep[0]
+        arrived = swap(
+            jnp.stack([a.astype(jnp.bfloat16) for a in keep[1::2]]), "sample", samples, bits
+        )
+        keep = keep[0::2]
+
+
+def gather_parts(act, samples, direct):
+    if direct:
+        acts = [act] + [swap(act, "sample", samples, m) for m in range(1, samples)]
+        return jnp.stack(acts[0::2]), jnp.stack(acts[1::2]), list(range(0, samples, 2))
+    held, order, bits = [act], [0], samples // 2
+    while bits > 1:
+        arrived = swap(jnp.stack(held), "sample", samples, bits)
+        held = held + [arrived[i] for i in range(len(held))]
+        order = order + [m + bits for m in order]
+        bits //= 2
+    near = jnp.stack(held)
+    return near, swap(near, "sample", samples, 1), order
+
+
+def down_kernel(expert, order, place_ref, near_ref, far_ref, weight_ref, out_ref, held_ref, sems):
+    part = near_ref.shape[2]
+    known = [(m + odd, i, act_ref) for i, m in enumerate(order) for odd, act_ref in enumerate((near_ref, far_ref))]
+    copies = []
+    for n, (m, _, _) in enumerate(known):
+        row = pl.multiple_of(lax.bitwise_xor(place_ref[0], m) * part, HDIM)
+        copies.append(
+            pltpu.make_async_copy(
+                weight_ref.at[expert, pl.ds(row, part)], held_ref.at[n], sems.at[n]
+            )
+        )
+        copies[n].start()
     total = None
-    for k, act_ref in enumerate(act_refs):
-        row = lax.rem(place_ref[0] - k + samples, samples) * part
-        share = jnp.dot(
-            act_ref[...],
-            weight_ref[expert, pl.ds(pl.multiple_of(row, HDIM), part), :],
-            preferred_element_type=jnp.float32,
-        )
+    for n, (_, i, act_ref) in enumerate(known):
+        copies[n].wait()
+        share = jnp.dot(act_ref[i], held_ref[n], preferred_element_type=jnp.float32)
         total = share if total is None else total + share
     out_ref[...] = total.astype(jnp.bfloat16)
 
 
-def down_rows(acts, weights, expert, place):
-    samples = len(acts)
-    slots, part = acts[0].shape
+def down_rows(near, far, order, weights, expert, place):
+    pairs, slots, part = near.shape
     _, hidden, width = weights.shape
     if part % HDIM:
-        joined = jnp.stack(acts, axis=1)[:, ::-1]
-        joined = jnp.roll(joined, place[0] + 1, axis=1).reshape(slots, hidden)
+        known = jnp.array(order + [m + 1 for m in order], jnp.int32)
+        held = jnp.bitwise_xor(place[0], known)[None, :] == jnp.arange(2 * pairs)[:, None]
+        joined = jnp.einsum(
+            "ni,isp->snp",
+            held.astype(jnp.bfloat16),
+            jnp.concatenate([near, far], axis=0),
+            preferred_element_type=jnp.float32,
+        )
+        joined = joined.astype(jnp.bfloat16).reshape(slots, hidden)
         return jnp.dot(joined, weights[expert], preferred_element_type=jnp.float32).astype(
             jnp.bfloat16
         )
     return pl.pallas_call(
-        functools.partial(down_kernel, expert),
+        functools.partial(down_kernel, expert, order),
         out_shape=jax.ShapeDtypeStruct((slots, width), jnp.bfloat16),
-        in_specs=[SMEM_SPEC] + [VMEM_SPEC] * (samples + 1),
+        in_specs=[SMEM_SPEC] + [VMEM_SPEC] * 2 + [ANY_SPEC],
         out_specs=VMEM_SPEC,
-        compiler_params=pltpu.CompilerParams(vmem_limit_bytes=SCOPED),
+        scratch_shapes=[
+            pltpu.VMEM((2 * pairs, part, width), jnp.bfloat16),
+            pltpu.SemaphoreType.DMA((2 * pairs,)),
+        ],
+        compiler_params=pltpu.CompilerParams(vmem_limit_bytes=SCOPED + 2 * hidden * width),
         cost_estimate=pl.CostEstimate(
             flops=2 * slots * hidden * width, bytes_accessed=2 * hidden * width, transcendentals=0
         ),
-    )(place, *acts, weights)
+    )(place, near, far, in_hbm(weights))
 
 
 def gather_experts(array, owners):
@@ -327,6 +406,31 @@
     query = queries.reshape(prompts, heads, HDIM)
     all_queries = [query] + [send(query, "sample", samples, k) for k in range(1, samples)]
 
+    gen_out, gen_stat = gen_part(query, gen_kv[:, 0], gen_lengths[:, 0])
+    parts = list(prompt_part(all_queries, prompt_kv))
+    parts = [parts[0]] + [send(parts[k], "sample", samples, -k) for k in range(1, samples)]
+    outs = [gen_out] + [part[:prompts] for part in parts]
+    marks = [(gen_stat[0], gen_stat[1])] + [
+        part_marks(part, prompts, k) for k, part in enumerate(parts)
+    ]
+    highest = functools.reduce(jnp.maximum, [m[0] for m in marks])
+    scales = [jnp.exp(m[0] - highest) for m in marks]
+    total = sum(c * m[1] for c, m in zip(scales, marks))
+    attended = sum(
+        o.astype(jnp.float32) * (c / total)[:, :, None] for o, c in zip(outs, scales)
+    )
+    attended = attended.astype(jnp.bfloat16).reshape(prompts, heads * HDIM)
+    attended = [attended] + [send(attended, "sample", samples, k) for k in range(1, samples)]
+    routes, route_probs, attended[1] = lax.optimization_barrier((routes, route_probs, attended[1]))
+    mixed, row_block = project(
+        attended,
+        out_proj,
+        jnp.swapaxes(residual, 0, 1).reshape(rows, width),
+        norm_gain.reshape(1, width),
+        place,
+    )
+    mixed = jnp.swapaxes(mixed.reshape(samples, prompts, width), 0, 1)
+
     by_sample = lambda a: jnp.swapaxes(a, 0, 1).reshape(rows, TOPK)
     table = jnp.concatenate(
         [by_sample(routes).astype(jnp.float32), by_sample(route_probs)], axis=1
@@ -353,47 +457,28 @@
     pick = chosen.astype(jnp.bfloat16)
     slot_weight = jnp.sum(jnp.where(chosen, weight[:, None, :], 0.0), axis=2)
 
-    gen_out, gen_stat = gen_part(query, gen_kv[:, 0], gen_lengths[:, 0])
-    parts, stats = prompt_part(all_queries, prompt_kv)
-    outs, marks = [gen_out, parts[0]], [gen_stat, stats[0]]
-    for k in range(1, samples):
-        outs.append(send(parts[k], "sample", samples, -k))
-        marks.append(send(stats[k], "sample", samples, -k))
-    highest = functools.reduce(jnp.maximum, [m[0] for m in marks])
-    scales = [jnp.exp(m[0] - highest) for m in marks]
-    total = sum(c * m[1] for c, m in zip(scales, marks))
-    attended = sum(
-        o.astype(jnp.float32) * (c / total)[:, :, None] for o, c in zip(outs, scales)
-    )
-    attended = attended.astype(jnp.bfloat16).reshape(prompts, heads * HDIM)
-    attended = [attended] + [send(attended, "sample", samples, k) for k in range(1, samples)]
-    mixed, row_block = project(
-        attended,
-        out_proj,
-        jnp.swapaxes(residual, 0, 1).reshape(rows, width),
-        norm_gain.reshape(1, width),
-        place,
-    )
-    mixed = jnp.swapaxes(mixed.reshape(samples, prompts, width), 0, 1)
-
     near, far = gather_experts(row_block, owners)
+    finished = []
+    shares, first_hop = [], []
+    for j in range(per_owner):
+        keep, give = gate_up_parts(pick[j], near, far, w_gate_up, j, place, samples)
+        arrived = first_swap(keep, give, samples, j in DIRECT)
+        if 0 < j < per_owner - 1:
+            near, far, shares[j - 1] = lax.optimization_barrier((near, far, shares[j - 1]))
+        shares.append((keep, give, arrived))
+    near, far, shares[-1] = lax.optimization_barrier((near, far, shares[-1]))
     square = jnp.concatenate([near[:, width : width + 2], far[:, width : width + 2]], axis=0)
     square = jnp.sum(square.astype(jnp.float32), axis=1)
     square = square + sum(send(square, "sample", samples, k) for k in range(1, samples))
     factor = lax.rsqrt(square / (width * samples) + EPSILON)
     slot_factor = jnp.sum(jnp.where(chosen, factor[None, None, :], 0.0), axis=2)
 
-    finished = []
     for j in range(per_owner):
-        shares = gate_up_parts(pick[j], near, far, w_gate_up, j, place, samples)
-        gate_up = shares[0].astype(jnp.float32)
-        for k in range(1, samples):
-            gate_up = gate_up + send(shares[k], "sample", samples, k).astype(jnp.float32)
+        gate_up = reduce_parts(*shares[j], samples, j in DIRECT)
         gate_up = gate_up * slot_factor[j][:, None]
         act = jax.nn.silu(gate_up[:, :part]) * gate_up[:, part:] * slot_weight[j][:, None]
         act = act.astype(jnp.bfloat16)
-        acts = [act] + [send(act, "sample", samples, k) for k in range(1, samples)]
-        finished.append(down_rows(acts, w_down, j, place))
+        finished.append(down_rows(*gather_parts(act, samples, j in DIRECT), w_down, j, place))
     returned = sum(
         lax.dot_general(
             pick[j], finished[j], (((0,), (0,)), ((), ())), preferred_element_type=jnp.float32

time: 159 us -> 144 us (0.906)
  starting transfers between devices: 72.9 us -> 50.6 us
  waiting for transfers between devices: 50 us -> 53.8 us
  Pallas kernels: 22.6 us -> 26.2 us
    ppermute x33 -> x12, starting transfers between devices: 60.6 us -> 22.8 us  [send(): lax.ppermute(array, axis, [(i, (i + shift) % size) for i in range(size)])]
    ppermute x12 -> x24, waiting for transfers between devices: 9.99 us -> 37.2 us  [swap(): return lax.ppermute(array, axis, [(i, i ^ bits) for i in range(size)])]
    ppermute x33 -> x12, waiting for transfers between devices: 40 us -> 16.6 us  [send(): lax.ppermute(array, axis, [(i, (i + shift) % size) for i in range(size)])]
    ppermute x12 -> x24, starting transfers between devices: 12.3 us -> 27.8 us  [swap(): return lax.ppermute(array, axis, [(i, i ^ bits) for i in range(size)])]
    pallas_call x3, Pallas kernels: 2.03 us -> 6.66 us  [down_rows(): pl.pallas_call(functools.partial(down_kernel, expert, order), out_shape=j...]
    unnamed x21 -> x15, local copies, waits for them, and re-layouts: 5.36 us -> 5.34 us
  transfers between devices with their start and end apart: 45 -> 36, of which waited for: 16 -> 18; matrix products, arithmetic and copies ran while one was open for 3% -> 4% of each run, Pallas kernels for 9% -> 13%
where the time goes in v3:
time: 144 us
  waiting for transfers between devices  53.8 us (37%)
  starting transfers between devices  50.6 us (35%)
  Pallas kernels  26.2 us (18%)
  local copies, waits for them, and re-layouts  8.54 us (6%)
  other arithmetic  2.75 us (2%)
    ppermute x24, waiting for transfers between devices, swap(): return lax.ppermute(array, axis, [(i, i ^ bits) for i in range(size)])  37.2 us
    ppermute x24, starting transfers between devices, swap(): return lax.ppermute(array, axis, [(i, i ^ bits) for i in range(size)])  27.8 us
    ppermute x12, starting transfers between devices, send(): lax.ppermute(array, axis, [(i, (i + shift) % size) for i in range(size)])  22.8 us
    ppermute x12, waiting for transfers between devices, send(): lax.ppermute(array, axis, [(i, (i + shift) % size) for i in range(size)])  16.6 us
    pallas_call x3, Pallas kernels, gate_up_parts(): pl.pallas_call(functools.partial(gate_kernel, features, expert), out_shap...  10.7 us
    pallas_call x3, Pallas kernels, down_rows(): pl.pallas_call(functools.partial(down_kernel, expert, order), out_shape=j...  6.66 us
    pallas_call x1, Pallas kernels, project(): pl.pallas_call(functools.partial(project_kernel, samples, width), out_sha...  6.5 us
    unnamed x15, local copies, waits for them, and re-layouts  5.34 us
  transfers between devices with their start and end apart: 36, of which 18 were waited for; matrix products, arithmetic and copies ran while one was open for 4% of the time, Pallas kernels for 13%

profile of v3, /device:TPU:0, one launch (start us, length us, event | category | flops | bytes accessed | tf_op | source)
XLA Modules:
  0.0 144.0 jit_solution(15579103486513429176)
XLA Ops:
  0.6 0.9 copy.45
  1.6 3.1 %collective-permute-start = (bf16[8,64,128]{2,1,0:T(8,128)(2,1)S(1)}, bf16[8,64,128]{2,1,0:T(8,128)(2,1)S(1)}, u32[]{:S(2)}, u32[]{:S(2)}) collective-permute-start(bf16[8,64,128]{2,1,0:T(8,128)(2,1)S(1)} %bitcast.166), channel_id=1, source_target_pairs={{0,8},{8,16},{16,24},{24,0},{1,9},{9,17},{17,25},{25,1},{2,10},{10... | collective-permute-start | bytes 393224 | tf_op jit(solution)/shard_map/ppermute | solution.py:21
  4.6 2.6 %collective-permute-start.1 = (bf16[8,64,128]{2,1,0:T(8,128)(2,1)S(1)}, bf16[8,64,128]{2,1,0:T(8,128)(2,1)S(1)}, u32[]{:S(2)}, u32[]{:S(2)}) collective-permute-start(bf16[8,64,128]{2,1,0:T(8,128)(2,1)S(1)} %bitcast.167), channel_id=1, source_target_pairs={{0,16},{8,24},{16,0},{24,8},{1,17},{9,25},{17,1},{25,9},{2,18},{10... | collective-permute-start | bytes 393224 | tf_op jit(solution)/shard_map/ppermute | solution.py:21
  7.2 1.3 collective-permute-start.2
  8.6 1.0 copy-done
  9.6 0.7 copy-done.2
  10.3 1.1 shard_map.122
  11.3 4.5 %collective-permute-done.1.refs_2_ = bf16[8,64,128]{2,1,0:T(8,128)(2,1)S(1)} collective-permute-done((bf16[8,64,128]{2,1,0:T(8,128)(2,1)S(1)}, bf16[8,64,128]{2,1,0:T(8,128)(2,1)S(1)}, u32[]{:S(2)}, u32[]{:S(2)}) %collective-permute-start.1) | collective-permute-done | bytes 131104 | tf_op jit(solution)/shard_map/ppermute | solution.py:21
  15.9 1.2 copy-done.3
  17.1 1.3 shard_map.123
  18.4 3.3 %collective-permute-start.5 = (bf16[9,64,128]{2,1,0:T(8,128)(2,1)S(1)}, bf16[9,64,128]{2,1,0:T(8,128)(2,1)S(1)}, u32[]{:S(2)}, u32[]{:S(2)}) collective-permute-start(bf16[9,64,128]{2,1,0:T(8,128)(2,1)S(1)} %get-tuple-element.37), channel_id=1, source_target_pairs={{0,8},{8,16},{16,24},{24,0},{1,9},{9,17},{17,25},{25,1},{2,10},{10... | collective-permute-start | bytes 442376 | tf_op jit(solution)/shard_map/ppermute | solution.py:21
  21.7 1.6 %collective-permute-start.4 = (bf16[9,64,128]{2,1,0:T(8,128)(2,1)S(1)}, bf16[9,64,128]{2,1,0:T(8,128)(2,1)S(1)}, u32[]{:S(2)}, u32[]{:S(2)}) collective-permute-start(bf16[9,64,128]{2,1,0:T(8,128)(2,1)S(1)} %get-tuple-element.36), channel_id=1, source_target_pairs={{0,16},{8,24},{16,0},{24,8},{1,17},{9,25},{17,1},{25,9},{2,18},{10... | collective-permute-start | bytes 442376 | tf_op jit(solution)/shard_map/ppermute | solution.py:21
  23.3 0.8 collective-permute-start.3
  24.2 3.1 %collective-permute-done.5 = bf16[9,64,128]{2,1,0:T(8,128)(2,1)S(1)} collective-permute-done((bf16[9,64,128]{2,1,0:T(8,128)(2,1)S(1)}, bf16[9,64,128]{2,1,0:T(8,128)(2,1)S(1)}, u32[]{:S(2)}, u32[]{:S(2)}) %collective-permute-start.5) | collective-permute-done | bytes 147488 | tf_op jit(solution)/shard_map/ppermute | solution.py:21
  27.3 5.0 %collective-permute-done.4 = bf16[9,64,128]{2,1,0:T(8,128)(2,1)S(1)} collective-permute-done((bf16[9,64,128]{2,1,0:T(8,128)(2,1)S(1)}, bf16[9,64,128]{2,1,0:T(8,128)(2,1)S(1)}, u32[]{:S(2)}, u32[]{:S(2)}) %collective-permute-start.4) | collective-permute-done | bytes 147488 | tf_op jit(solution)/shard_map/ppermute | solution.py:21
  33.0 3.7 %collective-permute-start.6 = (bf16[8,8192]{1,0:T(8,128)(2,1)S(1)}, bf16[8,8192]{1,0:T(8,128)(2,1)S(1)}, u32[]{:S(2)}, u32[]{:S(2)}) collective-permute-start(bf16[8,8192]{1,0:T(8,128)(2,1)S(1)} %bitcast.161), channel_id=1, source_target_pairs={{0,8},{8,16},{16,24},{24,0},{1,9},{9,17},{17,25},{25,1},{2,10},{10... | collective-permute-start | bytes 393224 | tf_op jit(solution)/shard_map/ppermute | solution.py:21
  36.7 0.9 copy.47
  37.5 2.3 %collective-permute-start.7 = (bf16[8,8192]{1,0:T(8,128)(2,1)S(1)}, bf16[8,8192]{1,0:T(8,128)(2,1)S(1)}, u32[]{:S(2)}, u32[]{:S(2)}) collective-permute-start(bf16[8,8192]{1,0:T(8,128)(2,1)S(1)} %bitcast.162), channel_id=1, source_target_pairs={{0,16},{8,24},{16,0},{24,8},{1,17},{9,25},{17,1},{25,9},{2,18},{10... | collective-permute-start | bytes 393224 | tf_op jit(solution)/shard_map/ppermute | solution.py:21
  40.0 2.5 %collective-permute-done.6.refs_1_ = bf16[8,8192]{1,0:T(8,128)(2,1)S(1)} collective-permute-done((bf16[8,8192]{1,0:T(8,128)(2,1)S(1)}, bf16[8,8192]{1,0:T(8,128)(2,1)S(1)}, u32[]{:S(2)}, u32[]{:S(2)}) %collective-permute-start.6) | collective-permute-done | bytes 131104 | tf_op jit(solution)/shard_map/ppermute | solution.py:21
  42.4 0.7 convert_bitcast_fusion
  43.3 0.8 copy.34
  44.2 1.5 %collective-permute-start.10 = (f32[32,16]{0,1:T(8,128)S(1)}, f32[32,16]{0,1:T(8,128)S(1)}, u32[]{:S(2)}, u32[]{:S(2)}) collective-permute-start(f32[32,16]{0,1:T(8,128)S(1)} %constant_dynamic-update-slice_fusion), channel_id=1, source_target_pairs={{0,4},{1,5},{2,6},{3,7},{4,0},{5,1},{6,2},{7,3},{8,12},{9,13},{10,... | collective-permute-start | bytes 6152 | tf_op jit(solution)/shard_map/ppermute | solution.py:25
  45.8 1.4 collective-permute-start.11
  47.2 0.5 collective-permute-start.9
  47.7 0.7 copy-done.1
  48.4 6.5 %shard_map.124 = (bf16[32,1024]{1,0:T(8,128)(2,1)S(1)}, bf16[32,1152]{1,0:T(8,128)(2,1)S(1)}) custom-call(s32[1]{0:T(128)} %bitcast.place_ref, bf16[8,8192]{1,0:T(8,128)(2,1)S(1)} %bitcast.164, bf16[8,8192]{1,0:T(8,128)(2,1)S(1)} %collective-permute-done.6.refs_1_, bf16[8,8192]{1,0:T(8,128)(2,1)S(1)} %collective-permute-done.7.refs_2_, ...), custom_call_target="tpu_custom_call" | custom-call | flops 536870912 | bytes 16777216 | tf_op jit(solution)/shard_map/pallas_call | solution.py:200
  55.1 1.6 %collective-permute-start.13 = (bf16[32,1152]{1,0:T(8,128)(2,1)S(1)}, bf16[32,1152]{1,0:T(8,128)(2,1)S(1)}, u32[]{:S(2)}, u32[]{:S(2)}) collective-permute-start(bf16[32,1152]{1,0:T(8,128)(2,1)S(1)} %get-tuple-element.42), channel_id=1, source_target_pairs={{0,2},{1,3},{2,0},{3,1},{4,6},{5,7},{6,4},{7,5},{8,10},{9,11},{10,... | collective-permute-start | bytes 221192 | tf_op jit(solution)/shard_map/ppermute | solution.py:25
  56.6 1.5 %collective-permute-start.14 = (bf16[32,1152]{1,0:T(8,128)(2,1)S(1)}, bf16[32,1152]{1,0:T(8,128)(2,1)S(1)}, u32[]{:S(2)}, u32[]{:S(2)}) collective-permute-start(bf16[32,1152]{1,0:T(8,128)(2,1)S(1)} %get-tuple-element.42), channel_id=1, source_target_pairs={{0,4},{1,5},{2,6},{3,7},{4,0},{5,1},{6,2},{7,3},{8,12},{9,13},{10,... | collective-permute-start | bytes 221192 | tf_op jit(solution)/shard_map/ppermute | solution.py:25
  59.1 0.6 collective-permute-done.13
  59.8 1.2 collective-permute-done.14
  61.0 2.4 %collective-permute-done.15 = bf16[32,1152]{1,0:T(8,128)(2,1)S(1)} collective-permute-done((bf16[32,1152]{1,0:T(8,128)(2,1)S(1)}, bf16[32,1152]{1,0:T(8,128)(2,1)S(1)}, u32[]{:S(2)}, u32[]{:S(2)}) %collective-permute-start.15) | collective-permute-done | bytes 73760 | tf_op jit(solution)/shard_map/ppermute | solution.py:25
  63.6 1.5 %collective-permute-done.16.far_ref = bf16[128,1152]{1,0:T(8,128)(2,1)S(1)} collective-permute-done((bf16[128,1152]{1,0:T(8,128)(2,1)S(1)}, bf16[128,1152]{1,0:T(8,128)(2,1)S(1)}, u32[]{:S(2)}, u32[]{:S(2)}) %collective-permute-start.16) | collective-permute-done | bytes 294944 | tf_op jit(solution)/shard_map/ppermute | solution.py:25
  65.1 3.6 %shard_map.125 = (bf16[104,768]{1,0:T(8,128)(2,1)S(1)}, bf16[104,768]{1,0:T(8,128)(2,1)S(1)}, bf16[2,104,768]{2,1,0:T(8,128)(2,1)S(1)}) custom-call(s32[1]{0:T(128)} %bitcast.place_ref, bf16[104,256]{1,0:T(8,128)(2,1)S(1)} %get-tuple-element.84.pick_ref, bf16[128,1152]{1,0:T(8,128)(2,1)S(1)} %constant_dynamic-update-slice_fusion.2.near_ref, ...), custom_call_target="tpu_custom_call" | custom-call | flops 654311424 | bytes 6291456 | tf_op jit(solution)/shard_map/pallas_call | solution.py:270
  68.7 2.8 %collective-permute-start.17 = (bf16[2,104,768]{2,1,0:T(8,128)(2,1)S(1)}, bf16[2,104,768]{2,1,0:T(8,128)(2,1)S(1)}, u32[]{:S(2)}, u32[]{:S(2)}) collective-permute-start(bf16[2,104,768]{2,1,0:T(8,128)(2,1)S(1)} %get-tuple-element.45), channel_id=1, source_target_pairs={{0,8},{8,0},{16,24},{24,16},{1,9},{9,1},{17,25},{25,17},{2,10},{10... | collective-permute-start | bytes 958472 | tf_op jit(solution)/shard_map/ppermute | solution.py:25
  71.5 3.6 %shard_map.128 = (bf16[104,768]{1,0:T(8,128)(2,1)S(1)}, bf16[104,768]{1,0:T(8,128)(2,1)S(1)}, bf16[2,104,768]{2,1,0:T(8,128)(2,1)S(1)}) custom-call(s32[1]{0:T(128)} %bitcast.place_ref, bf16[104,256]{1,0:T(8,128)(2,1)S(1)} %get-tuple-element.82.pick_ref, bf16[128,1152]{1,0:T(8,128)(2,1)S(1)} %constant_dynamic-update-slice_fusion.2.near_ref, ...), custom_call_target="tpu_custom_call" | custom-call | flops 654311424 | bytes 6291456 | tf_op jit(solution)/shard_map/pallas_call | solution.py:270
  75.2 4.6 %collective-permute-done.17 = bf16[2,104,768]{2,1,0:T(8,128)(2,1)S(1)} collective-permute-done((bf16[2,104,768]{2,1,0:T(8,128)(2,1)S(1)}, bf16[2,104,768]{2,1,0:T(8,128)(2,1)S(1)}, u32[]{:S(2)}, u32[]{:S(2)}) %collective-permute-start.17) | collective-permute-done | bytes 319520 | tf_op jit(solution)/shard_map/ppermute | solution.py:25
  79.8 3.6 %shard_map.126 = (bf16[104,768]{1,0:T(8,128)(2,1)S(1)}, bf16[104,768]{1,0:T(8,128)(2,1)S(1)}, bf16[2,104,768]{2,1,0:T(8,128)(2,1)S(1)}) custom-call(s32[1]{0:T(128)} %bitcast.place_ref, bf16[104,256]{1,0:T(8,128)(2,1)S(1)} %get-tuple-element.83.pick_ref, bf16[128,1152]{1,0:T(8,128)(2,1)S(1)} %constant_dynamic-update-slice_fusion.2.near_ref, ...), custom_call_target="tpu_custom_call" | custom-call | flops 654311424 | bytes 6291456 | tf_op jit(solution)/shard_map/pallas_call | solution.py:270
  83.4 2.1 %collective-permute-start.19 = (bf16[2,104,768]{2,1,0:T(8,128)(2,1)S(1)}, bf16[2,104,768]{2,1,0:T(8,128)(2,1)S(1)}, u32[]{:S(2)}, u32[]{:S(2)}) collective-permute-start(bf16[2,104,768]{2,1,0:T(8,128)(2,1)S(1)} %get-tuple-element.53), channel_id=1, source_target_pairs={{0,8},{8,0},{16,24},{24,16},{1,9},{9,1},{17,25},{25,17},{2,10},{10... | collective-permute-start | bytes 958472 | tf_op jit(solution)/shard_map/ppermute | solution.py:25
  85.5 1.3 collective-permute-start.18
  86.9 2.2 %collective-permute-start.26 = (bf16[1,104,768]{2,1,0:T(8,128)(2,1)S(1)}, bf16[1,104,768]{2,1,0:T(8,128)(2,1)S(1)}, u32[]{:S(2)}, u32[]{:S(2)}) collective-permute-start(bf16[1,104,768]{2,1,0:T(8,128)(2,1)S(1)} %fusion.11), channel_id=1, source_target_pairs={{0,16},{8,24},{16,0},{24,8},{1,17},{9,25},{17,1},{25,9},{2,18},{10... | collective-permute-start | bytes 479240 | tf_op jit(solution)/shard_map/ppermute | solution.py:25
  89.1 10.0 %collective-permute-done.19 = bf16[2,104,768]{2,1,0:T(8,128)(2,1)S(1)} collective-permute-done((bf16[2,104,768]{2,1,0:T(8,128)(2,1)S(1)}, bf16[2,104,768]{2,1,0:T(8,128)(2,1)S(1)}, u32[]{:S(2)}, u32[]{:S(2)}) %collective-permute-start.19) | collective-permute-done | bytes 319520 | tf_op jit(solution)/shard_map/ppermute | solution.py:25
  99.3 2.1 %collective-permute-start.21 = (f32[256]{0:T(256)S(1)}, f32[256]{0:T(256)S(1)}, u32[]{:S(2)}, u32[]{:S(2)}) collective-permute-start(f32[256]{0:T(256)S(1)} %convert_reduce_fusion), channel_id=1, source_target_pairs={{0,16},{8,24},{16,0},{24,8},{1,17},{9,25},{17,1},{25,9},{2,18},{10... | collective-permute-start | bytes 3080 | tf_op jit(solution)/shard_map/ppermute | solution.py:21
  101.4 1.7 %collective-permute-start.22 = (f32[256]{0:T(256)S(1)}, f32[256]{0:T(256)S(1)}, u32[]{:S(2)}, u32[]{:S(2)}) collective-permute-start(f32[256]{0:T(256)S(1)} %convert_reduce_fusion), channel_id=1, source_target_pairs={{0,24},{8,0},{16,8},{24,16},{1,25},{9,1},{17,9},{25,17},{2,26},{10... | collective-permute-start | bytes 3080 | tf_op jit(solution)/shard_map/ppermute | solution.py:21
  103.2 1.5 %collective-permute-done.20 = f32[256]{0:T(256)S(1)} collective-permute-done((f32[256]{0:T(256)S(1)}, f32[256]{0:T(256)S(1)}, u32[]{:S(2)}, u32[]{:S(2)}) %collective-permute-start.20) | collective-permute-done | bytes 1056 | tf_op jit(solution)/shard_map/ppermute | solution.py:21
  104.7 0.6 collective-permute-start.29
  105.7 2.4 %collective-permute-start.23 = (bf16[1,104,384]{2,1,0:T(8,128)(2,1)S(1)}, bf16[1,104,384]{2,1,0:T(8,128)(2,1)S(1)}, u32[]{:S(2)}, u32[]{:S(2)}) collective-permute-start(bf16[1,104,384]{2,1,0:T(8,128)(2,1)S(1)} %fusion.26), channel_id=1, source_target_pairs={{0,16},{8,24},{16,0},{24,8},{1,17},{9,25},{17,1},{25,9},{2,18},{10... | collective-permute-start | bytes 239624 | tf_op jit(solution)/shard_map/ppermute | solution.py:25
  108.3 0.7 collective-permute-start.27
  109.0 9.2 %collective-permute-done.23 = bf16[1,104,384]{2,1,0:T(8,128)(2,1)S(1)} collective-permute-done((bf16[1,104,384]{2,1,0:T(8,128)(2,1)S(1)}, bf16[1,104,384]{2,1,0:T(8,128)(2,1)S(1)}, u32[]{:S(2)}, u32[]{:S(2)}) %collective-permute-start.23) | collective-permute-done | bytes 79904 | tf_op jit(solution)/shard_map/ppermute | solution.py:25
  118.5 1.7 %collective-permute-start.30 = (bf16[1,104,384]{2,1,0:T(8,128)(2,1)S(1)}, bf16[1,104,384]{2,1,0:T(8,128)(2,1)S(1)}, u32[]{:S(2)}, u32[]{:S(2)}) collective-permute-start(bf16[1,104,384]{2,1,0:T(8,128)(2,1)S(1)} %fusion.28), channel_id=1, source_target_pairs={{0,16},{8,24},{16,0},{24,8},{1,17},{9,25},{17,1},{25,9},{2,18},{10... | collective-permute-start | bytes 239624 | tf_op jit(solution)/shard_map/ppermute | solution.py:25
  120.2 0.5 collective-permute-start.28
  120.7 3.5 %collective-permute-done.30 = bf16[1,104,384]{2,1,0:T(8,128)(2,1)S(1)} collective-permute-done((bf16[1,104,384]{2,1,0:T(8,128)(2,1)S(1)}, bf16[1,104,384]{2,1,0:T(8,128)(2,1)S(1)}, u32[]{:S(2)}, u32[]{:S(2)}) %collective-permute-start.30) | collective-permute-done | bytes 79904 | tf_op jit(solution)/shard_map/ppermute | solution.py:25
  124.2 2.7 %collective-permute-start.31 = (bf16[2,104,384]{2,1,0:T(8,128)(2,1)S(1)}, bf16[2,104,384]{2,1,0:T(8,128)(2,1)S(1)}, u32[]{:S(2)}, u32[]{:S(2)}) collective-permute-start(bf16[2,104,384]{2,1,0:T(8,128)(2,1)S(1)} %pad_maximum_fusion.2.near_ref), channel_id=1, source_target_pairs={{0,8},{8,0},{16,24},{24,16},{1,9},{9,1},{17,25},{25,17},{2,10},{10... | collective-permute-start | bytes 479240 | tf_op jit(solution)/shard_map/ppermute | solution.py:25
  126.9 2.2 %shard_map.127 = bf16[104,1024]{1,0:T(8,128)(2,1)S(1)} custom-call(s32[1]{0:T(128)} %bitcast.place_ref, bf16[2,104,384]{2,1,0:T(8,128)(2,1)S(1)} %pad_maximum_fusion.near_ref, bf16[2,104,384]{2,1,0:T(8,128)(2,1)S(1)} %collective-permute-done.24.far_ref, bf16[3,1536,1024]{2,1,0:T(8,128)(2,1)} %weight_ref.11), custom_call_target="tpu_custom_call" | custom-call | flops 327155712 | bytes 3145728 | tf_op jit(solution)/shard_map/pallas_call | solution.py:360
  129.1 0.5 collective-permute-done.28.far_ref
  129.6 2.2 %shard_map.129 = bf16[104,1024]{1,0:T(8,128)(2,1)S(1)} custom-call(s32[1]{0:T(128)} %bitcast.place_ref, bf16[2,104,384]{2,1,0:T(8,128)(2,1)S(1)} %pad_maximum_fusion.1.near_ref, bf16[2,104,384]{2,1,0:T(8,128)(2,1)S(1)} %collective-permute-done.28.far_ref, bf16[3,1536,1024]{2,1,0:T(8,128)(2,1)} %weight_ref.11), custom_call_target="tpu_custom_call" | custom-call | flops 327155712 | bytes 3145728 | tf_op jit(solution)/shard_map/pallas_call | solution.py:360
  132.2 2.2 %shard_map.130 = bf16[104,1024]{1,0:T(8,128)(2,1)S(1)} custom-call(s32[1]{0:T(128)} %bitcast.place_ref, bf16[2,104,384]{2,1,0:T(8,128)(2,1)S(1)} %pad_maximum_fusion.2.near_ref, bf16[2,104,384]{2,1,0:T(8,128)(2,1)S(1)} %collective-permute-done.31.far_ref, bf16[3,1536,1024]{2,1,0:T(8,128)(2,1)} %weight_ref.11), custom_call_target="tpu_custom_call" | custom-call | flops 327155712 | bytes 3145728 | tf_op jit(solution)/shard_map/pallas_call | solution.py:360
  135.3 1.5 %collective-permute-done.32 = bf16[4,32,1024]{2,1,0:T(8,128)(2,1)S(1)} collective-permute-done((bf16[4,32,1024]{2,1,0:T(8,128)(2,1)S(1)}, bf16[4,32,1024]{2,1,0:T(8,128)(2,1)S(1)}, u32[]{:S(2)}, u32[]{:S(2)}) %collective-permute-start.32) | collective-permute-done | bytes 262176 | tf_op jit(solution)/shard_map/ppermute | solution.py:25
  136.8 0.6 collective-permute-start.33
  137.4 0.7 collective-permute-start.34
  138.2 2.2 %collective-permute-start.35 = (bf16[32,1024]{1,0:T(8,128)(2,1)S(1)}, bf16[32,1024]{1,0:T(8,128)(2,1)S(1)}, u32[]{:S(2)}, u32[]{:S(2)}) collective-permute-start(bf16[32,1024]{1,0:T(8,128)(2,1)S(1)} %get-tuple-element.80), channel_id=1, source_target_pairs={{0,6},{1,7},{2,4},{3,5},{4,2},{5,3},{6,0},{7,1},{8,14},{9,15},{10,... | collective-permute-start | bytes 196616 | tf_op jit(solution)/shard_map/ppermute | solution.py:25
  140.4 0.7 copy.46
  141.3 1.1 collective-permute-done.34
  142.4 0.9 collective-permute-done.35
  143.4 0.7 copy.37
  (92 shorter events, 5.4 us)
Async XLA Ops:
  1.6 9.8 %collective-permute-start = (bf16[8,64,128]{2,1,0:T(8,128)(2,1)S(1)}, bf16[8,64,128]{2,1,0:T(8,128)(2,1)S(1)}, u32[]{:S(2)}, u32[]{:S(2)}) collective-permute-start(bf16[8,64,128]{2,1,0:T(8,128)(2,1)S(1)} %bitcast.166), channel_id=1, source_target_pairs={{0,8},{8,16},{16,24},{24,0},{1,9},{9,17},{17,25},{25,1},{2,10},{10... | collective-permute-start | bytes 393224 | tf_op jit(solution)/shard_map/ppermute | solution.py:21
  4.6 11.2 %collective-permute-start.1 = (bf16[8,64,128]{2,1,0:T(8,128)(2,1)S(1)}, bf16[8,64,128]{2,1,0:T(8,128)(2,1)S(1)}, u32[]{:S(2)}, u32[]{:S(2)}) collective-permute-start(bf16[8,64,128]{2,1,0:T(8,128)(2,1)S(1)} %bitcast.167), channel_id=1, source_target_pairs={{0,16},{8,24},{16,0},{24,8},{1,17},{9,25},{17,1},{25,9},{2,18},{10... | collective-permute-start | bytes 393224 | tf_op jit(solution)/shard_map/ppermute | solution.py:21
  7.2 8.6 %collective-permute-start.2 = (bf16[8,64,128]{2,1,0:T(8,128)(2,1)S(1)}, bf16[8,64,128]{2,1,0:T(8,128)(2,1)S(1)}, u32[]{:S(2)}, u32[]{:S(2)}) collective-permute-start(bf16[8,64,128]{2,1,0:T(8,128)(2,1)S(1)} %bitcast.168), channel_id=1, source_target_pairs={{0,24},{8,0},{16,8},{24,16},{1,25},{9,1},{17,9},{25,17},{2,26},{10... | collective-permute-start | bytes 393224 | tf_op jit(solution)/shard_map/ppermute | solution.py:21
  8.6 1.0 copy-start
  9.6 0.7 copy-start.2
  15.9 1.2 copy-start.3
  18.4 8.9 %collective-permute-start.5 = (bf16[9,64,128]{2,1,0:T(8,128)(2,1)S(1)}, bf16[9,64,128]{2,1,0:T(8,128)(2,1)S(1)}, u32[]{:S(2)}, u32[]{:S(2)}) collective-permute-start(bf16[9,64,128]{2,1,0:T(8,128)(2,1)S(1)} %get-tuple-element.37), channel_id=1, source_target_pairs={{0,8},{8,16},{16,24},{24,0},{1,9},{9,17},{17,25},{25,1},{2,10},{10... | collective-permute-start | bytes 442376 | tf_op jit(solution)/shard_map/ppermute | solution.py:21
  21.7 10.6 %collective-permute-start.4 = (bf16[9,64,128]{2,1,0:T(8,128)(2,1)S(1)}, bf16[9,64,128]{2,1,0:T(8,128)(2,1)S(1)}, u32[]{:S(2)}, u32[]{:S(2)}) collective-permute-start(bf16[9,64,128]{2,1,0:T(8,128)(2,1)S(1)} %get-tuple-element.36), channel_id=1, source_target_pairs={{0,16},{8,24},{16,0},{24,8},{1,17},{9,25},{17,1},{25,9},{2,18},{10... | collective-permute-start | bytes 442376 | tf_op jit(solution)/shard_map/ppermute | solution.py:21
  23.3 9.0 %collective-permute-start.3 = (bf16[9,64,128]{2,1,0:T(8,128)(2,1)S(1)}, bf16[9,64,128]{2,1,0:T(8,128)(2,1)S(1)}, u32[]{:S(2)}, u32[]{:S(2)}) collective-permute-start(bf16[9,64,128]{2,1,0:T(8,128)(2,1)S(1)} %get-tuple-element.35), channel_id=1, source_target_pairs={{0,24},{8,0},{16,8},{24,16},{1,25},{9,1},{17,9},{25,17},{2,26},{10... | collective-permute-start | bytes 442376 | tf_op jit(solution)/shard_map/ppermute | solution.py:21
  33.0 9.5 %collective-permute-start.6 = (bf16[8,8192]{1,0:T(8,128)(2,1)S(1)}, bf16[8,8192]{1,0:T(8,128)(2,1)S(1)}, u32[]{:S(2)}, u32[]{:S(2)}) collective-permute-start(bf16[8,8192]{1,0:T(8,128)(2,1)S(1)} %bitcast.161), channel_id=1, source_target_pairs={{0,8},{8,16},{16,24},{24,0},{1,9},{9,17},{17,25},{25,1},{2,10},{10... | collective-permute-start | bytes 393224 | tf_op jit(solution)/shard_map/ppermute | solution.py:21
  37.5 10.2 %collective-permute-start.7 = (bf16[8,8192]{1,0:T(8,128)(2,1)S(1)}, bf16[8,8192]{1,0:T(8,128)(2,1)S(1)}, u32[]{:S(2)}, u32[]{:S(2)}) collective-permute-start(bf16[8,8192]{1,0:T(8,128)(2,1)S(1)} %bitcast.162), channel_id=1, source_target_pairs={{0,16},{8,24},{16,0},{24,8},{1,17},{9,25},{17,1},{25,9},{2,18},{10... | collective-permute-start | bytes 393224 | tf_op jit(solution)/shard_map/ppermute | solution.py:21
  39.8 7.9 %collective-permute-start.8 = (bf16[8,8192]{1,0:T(8,128)(2,1)S(1)}, bf16[8,8192]{1,0:T(8,128)(2,1)S(1)}, u32[]{:S(2)}, u32[]{:S(2)}) collective-permute-start(bf16[8,8192]{1,0:T(8,128)(2,1)S(1)} %bitcast.163), channel_id=1, source_target_pairs={{0,24},{8,0},{16,8},{24,16},{1,25},{9,1},{17,9},{25,17},{2,26},{10... | collective-permute-start | bytes 393224 | tf_op jit(solution)/shard_map/ppermute | solution.py:21
  44.2 10.7 %collective-permute-start.10 = (f32[32,16]{0,1:T(8,128)S(1)}, f32[32,16]{0,1:T(8,128)S(1)}, u32[]{:S(2)}, u32[]{:S(2)}) collective-permute-start(f32[32,16]{0,1:T(8,128)S(1)} %constant_dynamic-update-slice_fusion), channel_id=1, source_target_pairs={{0,4},{1,5},{2,6},{3,7},{4,0},{5,1},{6,2},{7,3},{8,12},{9,13},{10,... | collective-permute-start | bytes 6152 | tf_op jit(solution)/shard_map/ppermute | solution.py:25
  45.8 9.2 %collective-permute-start.11 = (f32[32,16]{0,1:T(8,128)S(1)}, f32[32,16]{0,1:T(8,128)S(1)}, u32[]{:S(2)}, u32[]{:S(2)}) collective-permute-start(f32[32,16]{0,1:T(8,128)S(1)} %constant_dynamic-update-slice_fusion), channel_id=1, source_target_pairs={{0,6},{1,7},{2,4},{3,5},{4,2},{5,3},{6,0},{7,1},{8,14},{9,15},{10,... | collective-permute-start | bytes 6152 | tf_op jit(solution)/shard_map/ppermute | solution.py:25
  47.2 7.7 %collective-permute-start.9 = (f32[32,16]{0,1:T(8,128)S(1)}, f32[32,16]{0,1:T(8,128)S(1)}, u32[]{:S(2)}, u32[]{:S(2)}) collective-permute-start(f32[32,16]{0,1:T(8,128)S(1)} %constant_dynamic-update-slice_fusion), channel_id=1, source_target_pairs={{0,2},{1,3},{2,0},{3,1},{4,6},{5,7},{6,4},{7,5},{8,10},{9,11},{10,... | collective-permute-start | bytes 6152 | tf_op jit(solution)/shard_map/ppermute | solution.py:25
  47.7 0.7 copy-start.1
  55.0 3.6 %collective-permute-start.12 = (f32[128,16]{0,1:T(8,128)S(1)}, f32[128,16]{0,1:T(8,128)S(1)}, u32[]{:S(2)}, u32[]{:S(2)}) collective-permute-start(f32[128,16]{0,1:T(8,128)S(1)} %pad_maximum_fusion.3), channel_id=1, source_target_pairs={{0,1},{1,0},{2,3},{3,2},{4,5},{5,4},{6,7},{7,6},{8,9},{9,8},{10,11... | collective-permute-start | bytes 24584 | tf_op jit(solution)/shard_map/ppermute | solution.py:25
  55.1 4.7 %collective-permute-start.13 = (bf16[32,1152]{1,0:T(8,128)(2,1)S(1)}, bf16[32,1152]{1,0:T(8,128)(2,1)S(1)}, u32[]{:S(2)}, u32[]{:S(2)}) collective-permute-start(bf16[32,1152]{1,0:T(8,128)(2,1)S(1)} %get-tuple-element.42), channel_id=1, source_target_pairs={{0,2},{1,3},{2,0},{3,1},{4,6},{5,7},{6,4},{7,5},{8,10},{9,11},{10,... | collective-permute-start | bytes 221192 | tf_op jit(solution)/shard_map/ppermute | solution.py:25
  56.6 4.4 %collective-permute-start.14 = (bf16[32,1152]{1,0:T(8,128)(2,1)S(1)}, bf16[32,1152]{1,0:T(8,128)(2,1)S(1)}, u32[]{:S(2)}, u32[]{:S(2)}) collective-permute-start(bf16[32,1152]{1,0:T(8,128)(2,1)S(1)} %get-tuple-element.42), channel_id=1, source_target_pairs={{0,4},{1,5},{2,6},{3,7},{4,0},{5,1},{6,2},{7,3},{8,12},{9,13},{10,... | collective-permute-start | bytes 221192 | tf_op jit(solution)/shard_map/ppermute | solution.py:25
  58.2 5.3 %collective-permute-start.15 = (bf16[32,1152]{1,0:T(8,128)(2,1)S(1)}, bf16[32,1152]{1,0:T(8,128)(2,1)S(1)}, u32[]{:S(2)}, u32[]{:S(2)}) collective-permute-start(bf16[32,1152]{1,0:T(8,128)(2,1)S(1)} %get-tuple-element.42), channel_id=1, source_target_pairs={{0,6},{1,7},{2,4},{3,5},{4,2},{5,3},{6,0},{7,1},{8,14},{9,15},{10,... | collective-permute-start | bytes 221192 | tf_op jit(solution)/shard_map/ppermute | solution.py:25
  63.4 1.6 %collective-permute-start.16 = (bf16[128,1152]{1,0:T(8,128)(2,1)S(1)}, bf16[128,1152]{1,0:T(8,128)(2,1)S(1)}, u32[]{:S(2)}, u32[]{:S(2)}) collective-permute-start(bf16[128,1152]{1,0:T(8,128)(2,1)S(1)} %constant_dynamic-update-slice_fusion.2.near_ref), channel_id=1, source_target_pairs={{0,1},{1,0},{2,3},{3,2},{4,5},{5,4},{6,7},{7,6},{8,9},{9,8},{10,11... | collective-permute-start | bytes 884744 | tf_op jit(solution)/shard_map/ppermute | solution.py:25
  68.7 11.1 %collective-permute-start.17 = (bf16[2,104,768]{2,1,0:T(8,128)(2,1)S(1)}, bf16[2,104,768]{2,1,0:T(8,128)(2,1)S(1)}, u32[]{:S(2)}, u32[]{:S(2)}) collective-permute-start(bf16[2,104,768]{2,1,0:T(8,128)(2,1)S(1)} %get-tuple-element.45), channel_id=1, source_target_pairs={{0,8},{8,0},{16,24},{24,16},{1,9},{9,1},{17,25},{25,17},{2,10},{10... | collective-permute-start | bytes 958472 | tf_op jit(solution)/shard_map/ppermute | solution.py:25
  75.0 11.8 %collective-permute-start.25 = (bf16[2,104,768]{2,1,0:T(8,128)(2,1)S(1)}, bf16[2,104,768]{2,1,0:T(8,128)(2,1)S(1)}, u32[]{:S(2)}, u32[]{:S(2)}) collective-permute-start(bf16[2,104,768]{2,1,0:T(8,128)(2,1)S(1)} %get-tuple-element.57), channel_id=1, source_target_pairs={{0,8},{8,0},{16,24},{24,16},{1,9},{9,1},{17,25},{25,17},{2,10},{10... | collective-permute-start | bytes 958472 | tf_op jit(solution)/shard_map/ppermute | solution.py:25
  83.4 15.7 %collective-permute-start.19 = (bf16[2,104,768]{2,1,0:T(8,128)(2,1)S(1)}, bf16[2,104,768]{2,1,0:T(8,128)(2,1)S(1)}, u32[]{:S(2)}, u32[]{:S(2)}) collective-permute-start(bf16[2,104,768]{2,1,0:T(8,128)(2,1)S(1)} %get-tuple-element.53), channel_id=1, source_target_pairs={{0,8},{8,0},{16,24},{24,16},{1,9},{9,1},{17,25},{25,17},{2,10},{10... | collective-permute-start | bytes 958472 | tf_op jit(solution)/shard_map/ppermute | solution.py:25
  85.5 20.0 %collective-permute-start.18 = (bf16[1,104,768]{2,1,0:T(8,128)(2,1)S(1)}, bf16[1,104,768]{2,1,0:T(8,128)(2,1)S(1)}, u32[]{:S(2)}, u32[]{:S(2)}) collective-permute-start(bf16[1,104,768]{2,1,0:T(8,128)(2,1)S(1)} %fusion.10), channel_id=1, source_target_pairs={{0,16},{8,24},{16,0},{24,8},{1,17},{9,25},{17,1},{25,9},{2,18},{10... | collective-permute-start | bytes 479240 | tf_op jit(solution)/shard_map/ppermute | solution.py:25
  86.9 21.3 %collective-permute-start.26 = (bf16[1,104,768]{2,1,0:T(8,128)(2,1)S(1)}, bf16[1,104,768]{2,1,0:T(8,128)(2,1)S(1)}, u32[]{:S(2)}, u32[]{:S(2)}) collective-permute-start(bf16[1,104,768]{2,1,0:T(8,128)(2,1)S(1)} %fusion.11), channel_id=1, source_target_pairs={{0,16},{8,24},{16,0},{24,8},{1,17},{9,25},{17,1},{25,9},{2,18},{10... | collective-permute-start | bytes 479240 | tf_op jit(solution)/shard_map/ppermute | solution.py:25
  99.3 5.4 %collective-permute-start.20 = (f32[256]{0:T(256)S(1)}, f32[256]{0:T(256)S(1)}, u32[]{:S(2)}, u32[]{:S(2)}) collective-permute-start(f32[256]{0:T(256)S(1)} %convert_reduce_fusion), channel_id=1, source_target_pairs={{0,8},{8,16},{16,24},{24,0},{1,9},{9,17},{17,25},{25,1},{2,10},{10... | collective-permute-start | bytes 3080 | tf_op jit(solution)/shard_map/ppermute | solution.py:21
  99.3 6.0 %collective-permute-start.21 = (f32[256]{0:T(256)S(1)}, f32[256]{0:T(256)S(1)}, u32[]{:S(2)}, u32[]{:S(2)}) collective-permute-start(f32[256]{0:T(256)S(1)} %convert_reduce_fusion), channel_id=1, source_target_pairs={{0,16},{8,24},{16,0},{24,8},{1,17},{9,25},{17,1},{25,9},{2,18},{10... | collective-permute-start | bytes 3080 | tf_op jit(solution)/shard_map/ppermute | solution.py:21
  101.4 3.9 %collective-permute-start.22 = (f32[256]{0:T(256)S(1)}, f32[256]{0:T(256)S(1)}, u32[]{:S(2)}, u32[]{:S(2)}) collective-permute-start(f32[256]{0:T(256)S(1)} %convert_reduce_fusion), channel_id=1, source_target_pairs={{0,24},{8,0},{16,8},{24,16},{1,25},{9,1},{17,9},{25,17},{2,26},{10... | collective-permute-start | bytes 3080 | tf_op jit(solution)/shard_map/ppermute | solution.py:21
  104.7 13.6 %collective-permute-start.29 = (bf16[1,104,768]{2,1,0:T(8,128)(2,1)S(1)}, bf16[1,104,768]{2,1,0:T(8,128)(2,1)S(1)}, u32[]{:S(2)}, u32[]{:S(2)}) collective-permute-start(bf16[1,104,768]{2,1,0:T(8,128)(2,1)S(1)} %fusion.12), channel_id=1, source_target_pairs={{0,16},{8,24},{16,0},{24,8},{1,17},{9,25},{17,1},{25,9},{2,18},{10... | collective-permute-start | bytes 479240 | tf_op jit(solution)/shard_map/ppermute | solution.py:25
  105.7 12.4 %collective-permute-start.23 = (bf16[1,104,384]{2,1,0:T(8,128)(2,1)S(1)}, bf16[1,104,384]{2,1,0:T(8,128)(2,1)S(1)}, u32[]{:S(2)}, u32[]{:S(2)}) collective-permute-start(bf16[1,104,384]{2,1,0:T(8,128)(2,1)S(1)} %fusion.26), channel_id=1, source_target_pairs={{0,16},{8,24},{16,0},{24,8},{1,17},{9,25},{17,1},{25,9},{2,18},{10... | collective-permute-start | bytes 239624 | tf_op jit(solution)/shard_map/ppermute | solution.py:25
  108.3 11.9 %collective-permute-start.27 = (bf16[1,104,384]{2,1,0:T(8,128)(2,1)S(1)}, bf16[1,104,384]{2,1,0:T(8,128)(2,1)S(1)}, u32[]{:S(2)}, u32[]{:S(2)}) collective-permute-start(bf16[1,104,384]{2,1,0:T(8,128)(2,1)S(1)} %fusion.27), channel_id=1, source_target_pairs={{0,16},{8,24},{16,0},{24,8},{1,17},{9,25},{17,1},{25,9},{2,18},{10... | collective-permute-start | bytes 239624 | tf_op jit(solution)/shard_map/ppermute | solution.py:25
  118.2 8.7 %collective-permute-start.24 = (bf16[2,104,384]{2,1,0:T(8,128)(2,1)S(1)}, bf16[2,104,384]{2,1,0:T(8,128)(2,1)S(1)}, u32[]{:S(2)}, u32[]{:S(2)}) collective-permute-start(bf16[2,104,384]{2,1,0:T(8,128)(2,1)S(1)} %pad_maximum_fusion.near_ref), channel_id=1, source_target_pairs={{0,8},{8,0},{16,24},{24,16},{1,9},{9,1},{17,25},{25,17},{2,10},{10... | collective-permute-start | bytes 479240 | tf_op jit(solution)/shard_map/ppermute | solution.py:25
  118.5 5.7 %collective-permute-start.30 = (bf16[1,104,384]{2,1,0:T(8,128)(2,1)S(1)}, bf16[1,104,384]{2,1,0:T(8,128)(2,1)S(1)}, u32[]{:S(2)}, u32[]{:S(2)}) collective-permute-start(bf16[1,104,384]{2,1,0:T(8,128)(2,1)S(1)} %fusion.28), channel_id=1, source_target_pairs={{0,16},{8,24},{16,0},{24,8},{1,17},{9,25},{17,1},{25,9},{2,18},{10... | collective-permute-start | bytes 239624 | tf_op jit(solution)/shard_map/ppermute | solution.py:25
  120.2 9.4 %collective-permute-start.28 = (bf16[2,104,384]{2,1,0:T(8,128)(2,1)S(1)}, bf16[2,104,384]{2,1,0:T(8,128)(2,1)S(1)}, u32[]{:S(2)}, u32[]{:S(2)}) collective-permute-start(bf16[2,104,384]{2,1,0:T(8,128)(2,1)S(1)} %pad_maximum_fusion.1.near_ref), channel_id=1, source_target_pairs={{0,8},{8,0},{16,24},{24,16},{1,9},{9,1},{17,25},{25,17},{2,10},{10... | collective-permute-start | bytes 479240 | tf_op jit(solution)/shard_map/ppermute | solution.py:25
  124.2 8.0 %collective-permute-start.31 = (bf16[2,104,384]{2,1,0:T(8,128)(2,1)S(1)}, bf16[2,104,384]{2,1,0:T(8,128)(2,1)S(1)}, u32[]{:S(2)}, u32[]{:S(2)}) collective-permute-start(bf16[2,104,384]{2,1,0:T(8,128)(2,1)S(1)} %pad_maximum_fusion.2.near_ref), channel_id=1, source_target_pairs={{0,8},{8,0},{16,24},{24,16},{1,9},{9,1},{17,25},{25,17},{2,10},{10... | collective-permute-start | bytes 479240 | tf_op jit(solution)/shard_map/ppermute | solution.py:25
  135.1 1.6 %collective-permute-start.32 = (bf16[4,32,1024]{2,1,0:T(8,128)(2,1)S(1)}, bf16[4,32,1024]{2,1,0:T(8,128)(2,1)S(1)}, u32[]{:S(2)}, u32[]{:S(2)}) collective-permute-start(bf16[4,32,1024]{2,1,0:T(8,128)(2,1)S(1)} %bitcast.176), channel_id=1, source_target_pairs={{0,1},{1,0},{2,3},{3,2},{4,5},{5,4},{6,7},{7,6},{8,9},{9,8},{10,11... | collective-permute-start | bytes 786440 | tf_op jit(solution)/shard_map/ppermute | solution.py:25
  136.8 4.5 %collective-permute-start.33 = (bf16[32,1024]{1,0:T(8,128)(2,1)S(1)}, bf16[32,1024]{1,0:T(8,128)(2,1)S(1)}, u32[]{:S(2)}, u32[]{:S(2)}) collective-permute-start(bf16[32,1024]{1,0:T(8,128)(2,1)S(1)} %get-tuple-element.79), channel_id=1, source_target_pairs={{0,2},{1,3},{2,0},{3,1},{4,6},{5,7},{6,4},{7,5},{8,10},{9,11},{10,... | collective-permute-start | bytes 196616 | tf_op jit(solution)/shard_map/ppermute | solution.py:25
  137.4 5.0 %collective-permute-start.34 = (bf16[32,1024]{1,0:T(8,128)(2,1)S(1)}, bf16[32,1024]{1,0:T(8,128)(2,1)S(1)}, u32[]{:S(2)}, u32[]{:S(2)}) collective-permute-start(bf16[32,1024]{1,0:T(8,128)(2,1)S(1)} %get-tuple-element.81), channel_id=1, source_target_pairs={{0,4},{1,5},{2,6},{3,7},{4,0},{5,1},{6,2},{7,3},{8,12},{9,13},{10,... | collective-permute-start | bytes 196616 | tf_op jit(solution)/shard_map/ppermute | solution.py:25
  138.2 5.2 %collective-permute-start.35 = (bf16[32,1024]{1,0:T(8,128)(2,1)S(1)}, bf16[32,1024]{1,0:T(8,128)(2,1)S(1)}, u32[]{:S(2)}, u32[]{:S(2)}) collective-permute-start(bf16[32,1024]{1,0:T(8,128)(2,1)S(1)} %get-tuple-element.80), channel_id=1, source_target_pairs={{0,6},{1,7},{2,4},{3,5},{4,2},{5,3},{6,0},{7,1},{8,14},{9,15},{10,... | collective-permute-start | bytes 196616 | tf_op jit(solution)/shard_map/ppermute | solution.py:25

commit v4 on v3

--- a/solution.py
+++ b/solution.py
@@ -1,4 +1,5 @@
 import functools
+import math
 
 import jax
 import jax.numpy as jnp
@@ -12,7 +13,6 @@
 TOPK = 8
 NEGATIVE = -1e30
 EPSILON = 1e-06
-DIRECT = ()
 MIB = 1 << 20
 SCOPED = 10 * MIB
 
@@ -113,6 +113,33 @@
     return pltpu.with_memory_space_constraint(array, pltpu.HBM)
 
 
+def fetch_kernel(source_ref, target_ref, sems):
+    pieces = sems.shape[0]
+    step = source_ref.shape[0] // pieces
+    copies = [
+        pltpu.make_async_copy(
+            source_ref.at[pl.ds(i * step, step)], target_ref.at[pl.ds(i * step, step)], sems.at[i]
+        )
+        for i in range(pieces)
+    ]
+    for copy in copies:
+        copy.start()
+    for copy in copies:
+        copy.wait()
+
+
+def fetch(array):
+    return pl.pallas_call(
+        fetch_kernel,
+        out_shape=jax.ShapeDtypeStruct(array.shape, array.dtype),
+        in_specs=[ANY_SPEC],
+        out_specs=VMEM_SPEC,
+        scratch_shapes=[pltpu.SemaphoreType.DMA((math.gcd(array.shape[0], 12),))],
+        compiler_params=pltpu.CompilerParams(vmem_limit_bytes=MIB),
+        cost_estimate=pl.CostEstimate(flops=0, bytes_accessed=4 * array.size, transcendentals=0),
+    )(in_hbm(array))
+
+
 def prompt_part(queries, cache):
     samples = len(queries)
     prompts, heads, _ = queries[0].shape
@@ -156,24 +183,10 @@
 
 def project_kernel(samples, features, place_ref, *refs):
     attended_refs = refs[:samples]
-    weight_ref, residual_ref, gain_ref, mixed_ref, row_ref, order_ref, held_ref, sems = refs[samples:]
+    weight_ref, residual_ref, gain_ref, mixed_ref, row_ref, order_ref = refs[samples:]
     prompts = attended_refs[0].shape[0]
-    pieces = sems.shape[0]
-    depth = weight_ref.shape[0] // pieces
-    copies = []
-    for i in range(pieces):
-        piece = pl.ds(i * depth, depth)
-        copies.append(pltpu.make_async_copy(weight_ref.at[piece], held_ref.at[piece], sems.at[i]))
-        copies[i].start()
     stacked = jnp.concatenate([r[...] for r in attended_refs], axis=0)
-    total = jnp.zeros(order_ref.shape, jnp.float32)
-    for i in range(pieces):
-        copies[i].wait()
-        total = total + jnp.dot(
-            stacked[:, i * depth : (i + 1) * depth],
-            held_ref[i * depth : (i + 1) * depth, :],
-            preferred_element_type=jnp.float32,
-        )
+    total = jnp.dot(stacked, weight_ref[...], preferred_element_type=jnp.float32)
     for k in range(samples):
         s = lax.rem(place_ref[0] - k + samples, samples)
         order_ref[pl.ds(pl.multiple_of(s * prompts, prompts), prompts), :] = total[
@@ -203,21 +216,20 @@
             jax.ShapeDtypeStruct((rows, width), jnp.bfloat16),
             jax.ShapeDtypeStruct((rows, width + HDIM), jnp.bfloat16),
         ],
-        in_specs=[SMEM_SPEC] + [VMEM_SPEC] * samples + [ANY_SPEC] + [VMEM_SPEC] * 2,
+        in_specs=[SMEM_SPEC] + [VMEM_SPEC] * (samples + 3),
         out_specs=[VMEM_SPEC] * 2,
-        scratch_shapes=[
-            pltpu.VMEM((rows, width), jnp.float32),
-            pltpu.VMEM(out_proj.shape, jnp.bfloat16),
-            pltpu.SemaphoreType.DMA((8,)),
-        ],
-        compiler_params=pltpu.CompilerParams(vmem_limit_bytes=SCOPED + 2 * inner * width),
+        scratch_shapes=[pltpu.VMEM((rows, width), jnp.float32)],
+        compiler_params=pltpu.CompilerParams(vmem_limit_bytes=SCOPED),
         cost_estimate=pl.CostEstimate(
             flops=2 * rows * inner * width, bytes_accessed=2 * inner * width, transcendentals=0
         ),
-    )(place, *attended, in_hbm(out_proj), residual, gain)
-
-
-def gate_kernel(features, expert, place_ref, pick_ref, near_ref, far_ref, weight_ref, *refs):
+    )(place, *attended, out_proj, residual, gain)
+
+
+def gate_kernel(
+    features, expert, place_ref, pick_ref, near_ref, far_ref, extra_ref, weight_ref, *refs
+):
+    slots = pick_ref.shape[0]
     keep_refs, give_ref, held_ref, sems = refs[:-3], refs[-3], refs[-2], refs[-1]
     half = near_ref.shape[0]
     samples = 2 * len(keep_refs)
@@ -242,13 +254,16 @@
         out_ref = give_ref.at[m // 2] if m % 2 else keep_refs[m // 2]
         for side in range(2):
             copies[m, side].wait()
-            out_ref[:, side * part : (side + 1) * part] = jnp.dot(
-                chosen, held_ref[m, side], preferred_element_type=jnp.float32
-            ).astype(jnp.bfloat16)
-
-
-def gate_up_parts(pick, near, far, weights, expert, place, samples):
+            columns = slice(side * part, (side + 1) * part)
+            share = jnp.dot(chosen, held_ref[m, side], preferred_element_type=jnp.float32)
+            if out_ref.shape[0] > slots:
+                share = jnp.concatenate([share, extra_ref[:, columns]], axis=0)
+            out_ref[:, columns] = share.astype(jnp.bfloat16)
+
+
+def gate_up_parts(pick, near, far, extra, weights, expert, place, samples):
     slots, rows = pick.shape
+    more = 0 if expert else extra.shape[0]
     _, features, wide = weights.shape
     hidden = wide // 2
     part = hidden // samples
@@ -265,13 +280,15 @@
         )
         shares = jnp.einsum("mn,sgnp->msgp", wanted, shares, preferred_element_type=jnp.float32)
         shares = shares.astype(jnp.bfloat16).reshape(samples, slots, 2 * part)
+        behind = jnp.broadcast_to(extra.astype(jnp.bfloat16)[:more], (samples, more, 2 * part))
+        shares = jnp.concatenate([shares, behind], axis=1)
         return [shares[m] for m in range(0, samples, 2)], shares[1::2]
-    one = jax.ShapeDtypeStruct((slots, 2 * part), jnp.bfloat16)
+    one = jax.ShapeDtypeStruct((slots + more, 2 * part), jnp.bfloat16)
     results = pl.pallas_call(
         functools.partial(gate_kernel, features, expert),
         out_shape=[one] * (samples // 2)
-        + [jax.ShapeDtypeStruct((samples // 2, slots, 2 * part), jnp.bfloat16)],
-        in_specs=[SMEM_SPEC] + [VMEM_SPEC] * 3 + [ANY_SPEC],
+        + [jax.ShapeDtypeStruct((samples // 2, slots + more, 2 * part), jnp.bfloat16)],
+        in_specs=[SMEM_SPEC] + [VMEM_SPEC] * 4 + [ANY_SPEC],
         out_specs=[VMEM_SPEC] * (samples // 2 + 1),
         scratch_shapes=[
             pltpu.VMEM((samples, 2, features, part), jnp.bfloat16),
@@ -281,20 +298,11 @@
         cost_estimate=pl.CostEstimate(
             flops=2 * slots * features * wide, bytes_accessed=2 * features * wide, transcendentals=0
         ),
-    )(place, pick, near, far, in_hbm(weights))
+    )(place, pick, near, far, extra, in_hbm(weights))
     return results[:-1], results[-1]
 
 
-def first_swap(keep, give, samples, direct):
-    if not direct:
-        return swap(give, "sample", samples, 1)
-    shares = [give[m // 2] if m % 2 else keep[m // 2] for m in range(samples)]
-    return [swap(shares[m], "sample", samples, m) for m in range(1, samples)]
-
-
-def reduce_parts(keep, give, arrived, samples, direct):
-    if direct:
-        return sum((a.astype(jnp.float32) for a in arrived), keep[0].astype(jnp.float32))
+def reduce_parts(keep, arrived, samples):
     bits = 1
     while True:
         keep = [a.astype(jnp.float32) + arrived[i].astype(jnp.float32) for i, a in enumerate(keep)]
@@ -307,10 +315,7 @@
         keep = keep[0::2]
 
 
-def gather_parts(act, samples, direct):
-    if direct:
-        acts = [act] + [swap(act, "sample", samples, m) for m in range(1, samples)]
-        return jnp.stack(acts[0::2]), jnp.stack(acts[1::2]), list(range(0, samples, 2))
+def gather_parts(act, samples):
     held, order, bits = [act], [0], samples // 2
     while bits > 1:
         arrived = swap(jnp.stack(held), "sample", samples, bits)
@@ -321,56 +326,71 @@
     return near, swap(near, "sample", samples, 1), order
 
 
-def down_kernel(expert, order, place_ref, near_ref, far_ref, weight_ref, out_ref, held_ref, sems):
-    part = near_ref.shape[2]
-    known = [(m + odd, i, act_ref) for i, m in enumerate(order) for odd, act_ref in enumerate((near_ref, far_ref))]
-    copies = []
-    for n, (m, _, _) in enumerate(known):
-        row = pl.multiple_of(lax.bitwise_xor(place_ref[0], m) * part, HDIM)
-        copies.append(
-            pltpu.make_async_copy(
-                weight_ref.at[expert, pl.ds(row, part)], held_ref.at[n], sems.at[n]
-            )
+def down_kernel(order, place_ref, *refs):
+    pick_ref, weight_ref, near_out_ref, far_out_ref = refs[-4:]
+    experts = weight_ref.shape[0]
+    part = refs[0].shape[2]
+    half = near_out_ref.shape[0]
+    near_sum = far_sum = None
+    for j in range(experts):
+        total = None
+        for n, m in enumerate(order):
+            for odd in range(2):
+                row = pl.multiple_of(lax.bitwise_xor(place_ref[0], m + odd) * part, HDIM)
+                share = jnp.dot(
+                    refs[2 * j + odd][n], weight_ref[j, pl.ds(row, part)], preferred_element_type=jnp.float32
+                )
+                total = share if total is None else total + share
+        finished = total.astype(jnp.bfloat16)
+        given = lax.dot_general(
+            pick_ref[j], finished, (((0,), (0,)), ((), ())), preferred_element_type=jnp.float32
         )
-        copies[n].start()
-    total = None
-    for n, (_, i, act_ref) in enumerate(known):
-        copies[n].wait()
-        share = jnp.dot(act_ref[i], held_ref[n], preferred_element_type=jnp.float32)
-        total = share if total is None else total + share
-    out_ref[...] = total.astype(jnp.bfloat16)
-
-
-def down_rows(near, far, order, weights, expert, place):
-    pairs, slots, part = near.shape
-    _, hidden, width = weights.shape
+        near_sum = given[:half] if near_sum is None else near_sum + given[:half]
+        far_sum = given[half:] if far_sum is None else far_sum + given[half:]
+    near_out_ref[...] = near_sum
+    far_out_ref[...] = far_sum.astype(jnp.bfloat16)
+
+
+def down_rows(acts, order, pick, weights, place):
+    pairs, slots, part = acts[0].shape
+    experts, hidden, width = weights.shape
+    half = pick.shape[2] // 2
+    shapes = [
+        jax.ShapeDtypeStruct((half, width), jnp.float32),
+        jax.ShapeDtypeStruct((half, width), jnp.bfloat16),
+    ]
     if part % HDIM:
         known = jnp.array(order + [m + 1 for m in order], jnp.int32)
         held = jnp.bitwise_xor(place[0], known)[None, :] == jnp.arange(2 * pairs)[:, None]
-        joined = jnp.einsum(
-            "ni,isp->snp",
-            held.astype(jnp.bfloat16),
-            jnp.concatenate([near, far], axis=0),
-            preferred_element_type=jnp.float32,
-        )
-        joined = joined.astype(jnp.bfloat16).reshape(slots, hidden)
-        return jnp.dot(joined, weights[expert], preferred_element_type=jnp.float32).astype(
-            jnp.bfloat16
-        )
+        total = jnp.zeros((2 * half, width), jnp.float32)
+        for j in range(experts):
+            joined = jnp.einsum(
+                "ni,isp->snp",
+                held.astype(jnp.bfloat16),
+                jnp.concatenate(acts[2 * j : 2 * j + 2], axis=0),
+                preferred_element_type=jnp.float32,
+            )
+            joined = joined.astype(jnp.bfloat16).reshape(slots, hidden)
+            finished = jnp.dot(joined, weights[j], preferred_element_type=jnp.float32)
+            total = total + lax.dot_general(
+                pick[j],
+                finished.astype(jnp.bfloat16),
+                (((0,), (0,)), ((), ())),
+                preferred_element_type=jnp.float32,
+            )
+        return total[:half], total[half:].astype(jnp.bfloat16)
     return pl.pallas_call(
-        functools.partial(down_kernel, expert, order),
-        out_shape=jax.ShapeDtypeStruct((slots, width), jnp.bfloat16),
-        in_specs=[SMEM_SPEC] + [VMEM_SPEC] * 2 + [ANY_SPEC],
-        out_specs=VMEM_SPEC,
-        scratch_shapes=[
-            pltpu.VMEM((2 * pairs, part, width), jnp.bfloat16),
-            pltpu.SemaphoreType.DMA((2 * pairs,)),
-        ],
-        compiler_params=pltpu.CompilerParams(vmem_limit_bytes=SCOPED + 2 * hidden * width),
+        functools.partial(down_kernel, order),
+        out_shape=shapes,
+        in_specs=[SMEM_SPEC] + [VMEM_SPEC] * (2 * experts + 1) + [VMEM_SPEC],
+        out_specs=[VMEM_SPEC] * 2,
+        compiler_params=pltpu.CompilerParams(vmem_limit_bytes=SCOPED),
         cost_estimate=pl.CostEstimate(
-            flops=2 * slots * hidden * width, bytes_accessed=2 * hidden * width, transcendentals=0
+            flops=2 * experts * slots * hidden * width,
+            bytes_accessed=2 * experts * hidden * width,
+            transcendentals=0,
         ),
-    )(place, near, far, in_hbm(weights))
+    )(place, *acts, pick, weights)
 
 
 def gather_experts(array, owners):
@@ -401,36 +421,12 @@
     rows = prompts * samples
     per_owner = w_gate_up.shape[0]
     hidden = w_down.shape[1]
-    part = hidden // samples
 
     query = queries.reshape(prompts, heads, HDIM)
     all_queries = [query] + [send(query, "sample", samples, k) for k in range(1, samples)]
 
     gen_out, gen_stat = gen_part(query, gen_kv[:, 0], gen_lengths[:, 0])
-    parts = list(prompt_part(all_queries, prompt_kv))
-    parts = [parts[0]] + [send(parts[k], "sample", samples, -k) for k in range(1, samples)]
-    outs = [gen_out] + [part[:prompts] for part in parts]
-    marks = [(gen_stat[0], gen_stat[1])] + [
-        part_marks(part, prompts, k) for k, part in enumerate(parts)
-    ]
-    highest = functools.reduce(jnp.maximum, [m[0] for m in marks])
-    scales = [jnp.exp(m[0] - highest) for m in marks]
-    total = sum(c * m[1] for c, m in zip(scales, marks))
-    attended = sum(
-        o.astype(jnp.float32) * (c / total)[:, :, None] for o, c in zip(outs, scales)
-    )
-    attended = attended.astype(jnp.bfloat16).reshape(prompts, heads * HDIM)
-    attended = [attended] + [send(attended, "sample", samples, k) for k in range(1, samples)]
-    routes, route_probs, attended[1] = lax.optimization_barrier((routes, route_probs, attended[1]))
-    mixed, row_block = project(
-        attended,
-        out_proj,
-        jnp.swapaxes(residual, 0, 1).reshape(rows, width),
-        norm_gain.reshape(1, width),
-        place,
-    )
-    mixed = jnp.swapaxes(mixed.reshape(samples, prompts, width), 0, 1)
-
+    routes, route_probs, gen_out = lax.optimization_barrier((routes, route_probs, gen_out))
     by_sample = lambda a: jnp.swapaxes(a, 0, 1).reshape(rows, TOPK)
     table = jnp.concatenate(
         [by_sample(routes).astype(jnp.float32), by_sample(route_probs)], axis=1
@@ -457,37 +453,63 @@
     pick = chosen.astype(jnp.bfloat16)
     slot_weight = jnp.sum(jnp.where(chosen, weight[:, None, :], 0.0), axis=2)
 
+    parts = list(prompt_part(all_queries, prompt_kv))
+    parts = [parts[0]] + [send(parts[k], "sample", samples, -k) for k in range(1, samples)]
+    outs = [gen_out] + [part[:prompts] for part in parts]
+    marks = [(gen_stat[0], gen_stat[1])] + [
+        part_marks(part, prompts, k) for k, part in enumerate(parts)
+    ]
+    highest = functools.reduce(jnp.maximum, [m[0] for m in marks])
+    scales = [jnp.exp(m[0] - highest) for m in marks]
+    total = sum(c * m[1] for c, m in zip(scales, marks))
+    attended = sum(
+        o.astype(jnp.float32) * (c / total)[:, :, None] for o, c in zip(outs, scales)
+    )
+    attended = attended.astype(jnp.bfloat16).reshape(prompts, heads * HDIM)
+    out_proj, attended = lax.optimization_barrier((out_proj, attended))
+    out_proj = fetch(out_proj)
+    attended = [attended] + [send(attended, "sample", samples, k) for k in range(1, samples)]
+    mixed, row_block = project(
+        attended,
+        out_proj,
+        jnp.swapaxes(residual, 0, 1).reshape(rows, width),
+        norm_gain.reshape(1, width),
+        place,
+    )
+    mixed = jnp.swapaxes(mixed.reshape(samples, prompts, width), 0, 1)
+
     near, far = gather_experts(row_block, owners)
-    finished = []
-    shares, first_hop = [], []
+    part = hidden // samples
+    square = jnp.concatenate([near[:, width : width + 2], far[:, width : width + 2]], axis=0)
+    square = square.astype(jnp.float32).T.reshape(-1)
+    total_rows = owners * rows
+    extra_rows = -(-2 * total_rows // (16 * part)) * 8
+    extra = jnp.pad(square, (0, extra_rows * 2 * part - square.size)).reshape(extra_rows, 2 * part)
+    sums = []
     for j in range(per_owner):
-        keep, give = gate_up_parts(pick[j], near, far, w_gate_up, j, place, samples)
-        arrived = first_swap(keep, give, samples, j in DIRECT)
-        if 0 < j < per_owner - 1:
-            near, far, shares[j - 1] = lax.optimization_barrier((near, far, shares[j - 1]))
-        shares.append((keep, give, arrived))
-    near, far, shares[-1] = lax.optimization_barrier((near, far, shares[-1]))
-    square = jnp.concatenate([near[:, width : width + 2], far[:, width : width + 2]], axis=0)
-    square = jnp.sum(square.astype(jnp.float32), axis=1)
-    square = square + sum(send(square, "sample", samples, k) for k in range(1, samples))
-    factor = lax.rsqrt(square / (width * samples) + EPSILON)
-    slot_factor = jnp.sum(jnp.where(chosen, factor[None, None, :], 0.0), axis=2)
-
+        keep, give = gate_up_parts(pick[j], near, far, extra, w_gate_up, j, place, samples)
+        arrived = swap(give, "sample", samples, 1)
+        sums.append((keep, arrived))
+    acts = []
     for j in range(per_owner):
-        gate_up = reduce_parts(*shares[j], samples, j in DIRECT)
+        gate_up = reduce_parts(*sums[j], samples)
+        if j == 0:
+            square = gate_up[slots:].reshape(-1)
+            square = square[:total_rows] + square[total_rows : 2 * total_rows]
+            factor = lax.rsqrt(square / (width * samples) + EPSILON)
+            slot_factor = jnp.sum(jnp.where(chosen, factor[None, None, :], 0.0), axis=2)
+            gate_up = gate_up[:slots]
         gate_up = gate_up * slot_factor[j][:, None]
         act = jax.nn.silu(gate_up[:, :part]) * gate_up[:, part:] * slot_weight[j][:, None]
         act = act.astype(jnp.bfloat16)
-        finished.append(down_rows(*gather_parts(act, samples, j in DIRECT), w_down, j, place))
-    returned = sum(
-        lax.dot_general(
-            pick[j], finished[j], (((0,), (0,)), ((), ())), preferred_element_type=jnp.float32
-        )
-        for j in range(per_owner)
-    )
-    returned = returned.reshape(2, owners // 2, rows, width)
-    arrived = swap(returned[1].astype(jnp.bfloat16), "expert", owners, 1)
-    paired = returned[0] + arrived.astype(jnp.float32)
+        act_near, act_far, order = gather_parts(act, samples)
+        acts = acts + [act_near, act_far]
+    w_down, acts[-2] = lax.optimization_barrier((w_down, acts[-2]))
+    w_down = fetch(w_down)
+    kept, given = down_rows(acts, order, pick, w_down, place)
+    kept = kept.reshape(owners // 2, rows, width)
+    arrived = swap(given.reshape(owners // 2, rows, width), "expert", owners, 1)
+    paired = kept + arrived.astype(jnp.float32)
     outgoing = paired.astype(jnp.bfloat16)
     combined = paired[0]
     for b in range(1, owners // 2):

time: 144 us -> 139 us (0.965)
  starting transfers between devices: 50.6 us -> 42.7 us
  waiting for transfers between devices: 53.8 us -> 56.4 us
  Pallas kernels: 26.2 us -> 28.2 us
    ppermute x24, waiting for transfers between devices: 37.2 us -> 45.4 us  [swap(): return lax.ppermute(array, axis, [(i, i ^ bits) for i in range(size)])]
    ppermute x12 -> x9, starting transfers between devices: 22.8 us -> 16.1 us  [send(): lax.ppermute(array, axis, [(i, (i + shift) % size) for i in range(size)])]
    ppermute x12 -> x9, waiting for transfers between devices: 16.6 us -> 11.1 us  [send(): lax.ppermute(array, axis, [(i, (i + shift) % size) for i in range(size)])]
    pallas_call x3, Pallas kernels: 6.66 us -> 12 us  [the longest x2 9.69 us: fetch(): pl.pallas_call(fetch_kernel, out_shape=jax.ShapeDtypeStruct(array.shape,...]
    pallas_call x1, Pallas kernels: 6.5 us -> 3.08 us  [project(): pl.pallas_call(functools.partial(project_kernel, samples, width), out_sha...]
    unnamed x15 -> x16, local copies, waits for them, and re-layouts: 5.34 us -> 4.67 us
  transfers between devices with their start and end apart: 36 -> 33, of which waited for: 18 -> 24; matrix products, arithmetic and copies ran while one was open for 4% -> 4% of each run, Pallas kernels for 13% -> 13%
where the time goes in v4:
time: 139 us
  waiting for transfers between devices  56.4 us (41%)
  starting transfers between devices  42.7 us (31%)
  Pallas kernels  28.2 us (20%)
  local copies, waits for them, and re-layouts  7.79 us (6%)
  other arithmetic  2.78 us (2%)
    ppermute x24, waiting for transfers between devices, swap(): return lax.ppermute(array, axis, [(i, i ^ bits) for i in range(size)])  45.4 us
    ppermute x24, starting transfers between devices, swap(): return lax.ppermute(array, axis, [(i, i ^ bits) for i in range(size)])  26.6 us
    ppermute x9, starting transfers between devices, send(): lax.ppermute(array, axis, [(i, (i + shift) % size) for i in range(size)])  16.1 us
    ppermute x9, waiting for transfers between devices, send(): lax.ppermute(array, axis, [(i, (i + shift) % size) for i in range(size)])  11.1 us
    pallas_call x3, Pallas kernels, gate_up_parts(): pl.pallas_call(functools.partial(gate_kernel, features, expert), out_shap...  10.7 us
    pallas_call x2, Pallas kernels, fetch(): pl.pallas_call(fetch_kernel, out_shape=jax.ShapeDtypeStruct(array.shape,...  9.69 us
    unnamed x16, local copies, waits for them, and re-layouts  4.67 us
    pallas_call x1, Pallas kernels, project(): pl.pallas_call(functools.partial(project_kernel, samples, width), out_sha...  3.08 us
  transfers between devices with their start and end apart: 33, of which 24 were waited for; matrix products, arithmetic and copies ran while one was open for 4% of the time, Pallas kernels for 13%

profile of v4, /device:TPU:0, one launch (start us, length us, event | category | flops | bytes accessed | tf_op | source)
XLA Modules:
  0.0 139.0 jit_solution(12028109316571609078)
XLA Ops:
  0.6 0.9 copy.47
  1.6 3.1 %collective-permute-start = (bf16[8,64,128]{2,1,0:T(8,128)(2,1)S(1)}, bf16[8,64,128]{2,1,0:T(8,128)(2,1)S(1)}, u32[]{:S(2)}, u32[]{:S(2)}) collective-permute-start(bf16[8,64,128]{2,1,0:T(8,128)(2,1)S(1)} %bitcast.167), channel_id=1, source_target_pairs={{0,8},{8,16},{16,24},{24,0},{1,9},{9,17},{17,25},{25,1},{2,10},{10... | collective-permute-start | bytes 393224 | tf_op jit(solution)/shard_map/ppermute | solution.py:21
  4.6 2.6 %collective-permute-start.1 = (bf16[8,64,128]{2,1,0:T(8,128)(2,1)S(1)}, bf16[8,64,128]{2,1,0:T(8,128)(2,1)S(1)}, u32[]{:S(2)}, u32[]{:S(2)}) collective-permute-start(bf16[8,64,128]{2,1,0:T(8,128)(2,1)S(1)} %bitcast.168), channel_id=1, source_target_pairs={{0,16},{8,24},{16,0},{24,8},{1,17},{9,25},{17,1},{25,9},{2,18},{10... | collective-permute-start | bytes 393224 | tf_op jit(solution)/shard_map/ppermute | solution.py:21
  7.2 1.0 copy-done
  8.3 0.7 copy-done.2
  8.9 1.1 shard_map.122
  10.0 0.7 convert_bitcast_fusion
  10.9 0.8 copy.35
  11.8 1.5 %collective-permute-start.10 = (f32[32,16]{0,1:T(8,128)S(1)}, f32[32,16]{0,1:T(8,128)S(1)}, u32[]{:S(2)}, u32[]{:S(2)}) collective-permute-start(f32[32,16]{0,1:T(8,128)S(1)} %constant_dynamic-update-slice_fusion), channel_id=1, source_target_pairs={{0,4},{1,5},{2,6},{3,7},{4,0},{5,1},{6,2},{7,3},{8,12},{9,13},{10,... | collective-permute-start | bytes 6152 | tf_op jit(solution)/shard_map/ppermute | solution.py:25
  13.3 1.4 %collective-permute-start.11 = (f32[32,16]{0,1:T(8,128)S(1)}, f32[32,16]{0,1:T(8,128)S(1)}, u32[]{:S(2)}, u32[]{:S(2)}) collective-permute-start(f32[32,16]{0,1:T(8,128)S(1)} %constant_dynamic-update-slice_fusion), channel_id=1, source_target_pairs={{0,6},{1,7},{2,4},{3,5},{4,2},{5,3},{6,0},{7,1},{8,14},{9,15},{10,... | collective-permute-start | bytes 6152 | tf_op jit(solution)/shard_map/ppermute | solution.py:25
  14.7 0.5 collective-permute-start.9
  15.4 1.3 collective-permute-start.2
  16.8 1.1 collective-permute-done.11
  17.9 0.5 collective-permute-done.9
  18.5 0.9 copy.49
  19.4 0.3 collective-permute-done.12
  19.9 0.5 collective-permute-done.2.refs_3_
  20.4 1.2 copy-done.3
  21.6 1.3 shard_map.123
  23.0 3.6 %collective-permute-start.4 = (bf16[9,64,128]{2,1,0:T(8,128)(2,1)S(1)}, bf16[9,64,128]{2,1,0:T(8,128)(2,1)S(1)}, u32[]{:S(2)}, u32[]{:S(2)}) collective-permute-start(bf16[9,64,128]{2,1,0:T(8,128)(2,1)S(1)} %get-tuple-element.33), channel_id=1, source_target_pairs={{0,16},{8,24},{16,0},{24,8},{1,17},{9,25},{17,1},{25,9},{2,18},{10... | collective-permute-start | bytes 442376 | tf_op jit(solution)/shard_map/ppermute | solution.py:21
  26.8 4.8 %collective-permute-done.5 = bf16[9,64,128]{2,1,0:T(8,128)(2,1)S(1)} collective-permute-done((bf16[9,64,128]{2,1,0:T(8,128)(2,1)S(1)}, bf16[9,64,128]{2,1,0:T(8,128)(2,1)S(1)}, u32[]{:S(2)}, u32[]{:S(2)}) %collective-permute-start.5) | collective-permute-done | bytes 147488 | tf_op jit(solution)/shard_map/ppermute | solution.py:21
  31.7 5.1 %collective-permute-done.4 = bf16[9,64,128]{2,1,0:T(8,128)(2,1)S(1)} collective-permute-done((bf16[9,64,128]{2,1,0:T(8,128)(2,1)S(1)}, bf16[9,64,128]{2,1,0:T(8,128)(2,1)S(1)}, u32[]{:S(2)}, u32[]{:S(2)}) %collective-permute-start.4) | collective-permute-done | bytes 147488 | tf_op jit(solution)/shard_map/ppermute | solution.py:21
  36.9 0.4 fusion.21
  37.4 2.8 %collective-permute-start.6 = (bf16[8,8192]{1,0:T(8,128)(2,1)S(1)}, bf16[8,8192]{1,0:T(8,128)(2,1)S(1)}, u32[]{:S(2)}, u32[]{:S(2)}) collective-permute-start(bf16[8,8192]{1,0:T(8,128)(2,1)S(1)} %bitcast.161), channel_id=1, source_target_pairs={{0,8},{8,16},{16,24},{24,0},{1,9},{9,17},{17,25},{25,1},{2,10},{10... | collective-permute-start | bytes 393224 | tf_op jit(solution)/shard_map/ppermute | solution.py:21
  40.5 2.2 %collective-permute-start.8 = (bf16[8,8192]{1,0:T(8,128)(2,1)S(1)}, bf16[8,8192]{1,0:T(8,128)(2,1)S(1)}, u32[]{:S(2)}, u32[]{:S(2)}) collective-permute-start(bf16[8,8192]{1,0:T(8,128)(2,1)S(1)} %bitcast.163), channel_id=1, source_target_pairs={{0,24},{8,0},{16,8},{24,16},{1,25},{9,1},{17,9},{25,17},{2,26},{10... | collective-permute-start | bytes 393224 | tf_op jit(solution)/shard_map/ppermute | solution.py:21
  42.9 5.9 %shard_map.124.refs_4_ = bf16[8192,1024]{1,0:T(8,128)(2,1)S(1)} custom-call(bf16[8192,1024]{1,0:T(8,128)(2,1)} %source_ref), custom_call_target="tpu_custom_call" | custom-call | bytes 33554432 | tf_op jit(solution)/shard_map/pallas_call | solution.py:132
  48.8 0.7 collective-permute-done.7.refs_2_
  49.5 3.1 %shard_map.125 = (bf16[32,1024]{1,0:T(8,128)(2,1)S(1)}, bf16[32,1152]{1,0:T(8,128)(2,1)S(1)}) custom-call(s32[1]{0:T(128)} %bitcast.place_ref, bf16[8,8192]{1,0:T(8,128)(2,1)S(1)} %bitcast.164, bf16[8,8192]{1,0:T(8,128)(2,1)S(1)} %collective-permute-done.6.refs_1_, bf16[8,8192]{1,0:T(8,128)(2,1)S(1)} %collective-permute-done.7.refs_2_, ...), custom_call_target="tpu_custom_call" | custom-call | flops 536870912 | bytes 16777216 | tf_op jit(solution)/shard_map/pallas_call | solution.py:213
  52.6 0.9 collective-permute-start.13
  53.5 1.1 collective-permute-start.14
  54.6 1.5 %collective-permute-start.15 = (bf16[32,1152]{1,0:T(8,128)(2,1)S(1)}, bf16[32,1152]{1,0:T(8,128)(2,1)S(1)}, u32[]{:S(2)}, u32[]{:S(2)}) collective-permute-start(bf16[32,1152]{1,0:T(8,128)(2,1)S(1)} %get-tuple-element.40), channel_id=1, source_target_pairs={{0,6},{1,7},{2,4},{3,5},{4,2},{5,3},{6,0},{7,1},{8,14},{9,15},{10,... | collective-permute-start | bytes 221192 | tf_op jit(solution)/shard_map/ppermute | solution.py:25
  56.1 0.9 collective-permute-done.13
  56.9 1.4 %collective-permute-done.14 = bf16[32,1152]{1,0:T(8,128)(2,1)S(1)} collective-permute-done((bf16[32,1152]{1,0:T(8,128)(2,1)S(1)}, bf16[32,1152]{1,0:T(8,128)(2,1)S(1)}, u32[]{:S(2)}, u32[]{:S(2)}) %collective-permute-start.14) | collective-permute-done | bytes 73760 | tf_op jit(solution)/shard_map/ppermute | solution.py:25
  58.4 1.5 %collective-permute-done.15 = bf16[32,1152]{1,0:T(8,128)(2,1)S(1)} collective-permute-done((bf16[32,1152]{1,0:T(8,128)(2,1)S(1)}, bf16[32,1152]{1,0:T(8,128)(2,1)S(1)}, u32[]{:S(2)}, u32[]{:S(2)}) %collective-permute-start.15) | collective-permute-done | bytes 73760 | tf_op jit(solution)/shard_map/ppermute | solution.py:25
  60.1 1.4 %collective-permute-done.16.far_ref = bf16[128,1152]{1,0:T(8,128)(2,1)S(1)} collective-permute-done((bf16[128,1152]{1,0:T(8,128)(2,1)S(1)}, bf16[128,1152]{1,0:T(8,128)(2,1)S(1)}, u32[]{:S(2)}, u32[]{:S(2)}) %collective-permute-start.16) | collective-permute-done | bytes 294944 | tf_op jit(solution)/shard_map/ppermute | solution.py:25
  61.7 3.6 %shard_map.128 = (bf16[104,768]{1,0:T(8,128)(2,1)S(1)}, bf16[104,768]{1,0:T(8,128)(2,1)S(1)}, bf16[2,104,768]{2,1,0:T(8,128)(2,1)S(1)}) custom-call(s32[1]{0:T(128)} %bitcast.place_ref, bf16[104,256]{1,0:T(8,128)(2,1)S(1)} %get-tuple-element.74.pick_ref, bf16[128,1152]{1,0:T(8,128)(2,1)S(1)} %constant_dynamic-update-slice_fusion.2.near_ref, ...), custom_call_target="tpu_custom_call" | custom-call | flops 654311424 | bytes 6291456 | tf_op jit(solution)/shard_map/pallas_call | solution.py:287
  65.3 3.3 %collective-permute-start.25 = (bf16[2,104,768]{2,1,0:T(8,128)(2,1)S(1)}, bf16[2,104,768]{2,1,0:T(8,128)(2,1)S(1)}, u32[]{:S(2)}, u32[]{:S(2)}) collective-permute-start(bf16[2,104,768]{2,1,0:T(8,128)(2,1)S(1)} %get-tuple-element.48), channel_id=1, source_target_pairs={{0,8},{8,0},{16,24},{24,16},{1,9},{9,1},{17,25},{25,17},{2,10},{10... | collective-permute-start | bytes 958472 | tf_op jit(solution)/shard_map/ppermute | solution.py:25
  68.6 3.6 %shard_map.126 = (bf16[112,768]{1,0:T(8,128)(2,1)S(1)}, bf16[112,768]{1,0:T(8,128)(2,1)S(1)}, bf16[2,112,768]{2,1,0:T(8,128)(2,1)S(1)}) custom-call(s32[1]{0:T(128)} %bitcast.place_ref, bf16[104,256]{1,0:T(8,128)(2,1)S(1)} %get-tuple-element.76.pick_ref, bf16[128,1152]{1,0:T(8,128)(2,1)S(1)} %constant_dynamic-update-slice_fusion.2.near_ref, ...), custom_call_target="tpu_custom_call" | custom-call | flops 654311424 | bytes 6291456 | tf_op jit(solution)/shard_map/pallas_call | solution.py:287
  72.3 3.6 %shard_map.127 = (bf16[104,768]{1,0:T(8,128)(2,1)S(1)}, bf16[104,768]{1,0:T(8,128)(2,1)S(1)}, bf16[2,104,768]{2,1,0:T(8,128)(2,1)S(1)}) custom-call(s32[1]{0:T(128)} %bitcast.place_ref, bf16[104,256]{1,0:T(8,128)(2,1)S(1)} %get-tuple-element.75.pick_ref, bf16[128,1152]{1,0:T(8,128)(2,1)S(1)} %constant_dynamic-update-slice_fusion.2.near_ref, ...), custom_call_target="tpu_custom_call" | custom-call | flops 654311424 | bytes 6291456 | tf_op jit(solution)/shard_map/pallas_call | solution.py:287
  75.9 2.1 %collective-permute-start.21 = (bf16[2,104,768]{2,1,0:T(8,128)(2,1)S(1)}, bf16[2,104,768]{2,1,0:T(8,128)(2,1)S(1)}, u32[]{:S(2)}, u32[]{:S(2)}) collective-permute-start(bf16[2,104,768]{2,1,0:T(8,128)(2,1)S(1)} %get-tuple-element.45), channel_id=1, source_target_pairs={{0,8},{8,0},{16,24},{24,16},{1,9},{9,1},{17,25},{25,17},{2,10},{10... | collective-permute-start | bytes 958472 | tf_op jit(solution)/shard_map/ppermute | solution.py:25
  78.1 1.7 %collective-permute-start.26 = (bf16[1,104,768]{2,1,0:T(8,128)(2,1)S(1)}, bf16[1,104,768]{2,1,0:T(8,128)(2,1)S(1)}, u32[]{:S(2)}, u32[]{:S(2)}) collective-permute-start(bf16[1,104,768]{2,1,0:T(8,128)(2,1)S(1)} %fusion.10), channel_id=1, source_target_pairs={{0,16},{8,24},{16,0},{24,8},{1,17},{9,25},{17,1},{25,9},{2,18},{10... | collective-permute-start | bytes 479240 | tf_op jit(solution)/shard_map/ppermute | solution.py:25
  79.7 8.0 %collective-permute-done.17 = bf16[2,112,768]{2,1,0:T(8,128)(2,1)S(1)} collective-permute-done((bf16[2,112,768]{2,1,0:T(8,128)(2,1)S(1)}, bf16[2,112,768]{2,1,0:T(8,128)(2,1)S(1)}, u32[]{:S(2)}, u32[]{:S(2)}) %collective-permute-start.17) | collective-permute-done | bytes 344096 | tf_op jit(solution)/shard_map/ppermute | solution.py:25
  87.8 1.3 collective-permute-start.18
  89.0 6.4 %collective-permute-done.21 = bf16[2,104,768]{2,1,0:T(8,128)(2,1)S(1)} collective-permute-done((bf16[2,104,768]{2,1,0:T(8,128)(2,1)S(1)}, bf16[2,104,768]{2,1,0:T(8,128)(2,1)S(1)}, u32[]{:S(2)}, u32[]{:S(2)}) %collective-permute-start.21) | collective-permute-done | bytes 319520 | tf_op jit(solution)/shard_map/ppermute | solution.py:25
  95.4 1.0 collective-permute-start.22
  96.4 9.7 %collective-permute-done.18 = bf16[1,112,768]{2,1,0:T(8,128)(2,1)S(1)} collective-permute-done((bf16[1,112,768]{2,1,0:T(8,128)(2,1)S(1)}, bf16[1,112,768]{2,1,0:T(8,128)(2,1)S(1)}, u32[]{:S(2)}, u32[]{:S(2)}) %collective-permute-start.18) | collective-permute-done | bytes 172064 | tf_op jit(solution)/shard_map/ppermute | solution.py:25
  106.7 2.9 %collective-permute-done.22 = bf16[1,104,768]{2,1,0:T(8,128)(2,1)S(1)} collective-permute-done((bf16[1,104,768]{2,1,0:T(8,128)(2,1)S(1)}, bf16[1,104,768]{2,1,0:T(8,128)(2,1)S(1)}, u32[]{:S(2)}, u32[]{:S(2)}) %collective-permute-start.22) | collective-permute-done | bytes 159776 | tf_op jit(solution)/shard_map/ppermute | solution.py:25
  110.1 3.0 %collective-permute-start.19 = (bf16[1,104,384]{2,1,0:T(8,128)(2,1)S(1)}, bf16[1,104,384]{2,1,0:T(8,128)(2,1)S(1)}, u32[]{:S(2)}, u32[]{:S(2)}) collective-permute-start(bf16[1,104,384]{2,1,0:T(8,128)(2,1)S(1)} %fusion.22), channel_id=1, source_target_pairs={{0,16},{8,24},{16,0},{24,8},{1,17},{9,25},{17,1},{25,9},{2,18},{10... | collective-permute-start | bytes 239624 | tf_op jit(solution)/shard_map/ppermute | solution.py:25
  113.0 2.2 %collective-permute-done.27 = bf16[1,104,384]{2,1,0:T(8,128)(2,1)S(1)} collective-permute-done((bf16[1,104,384]{2,1,0:T(8,128)(2,1)S(1)}, bf16[1,104,384]{2,1,0:T(8,128)(2,1)S(1)}, u32[]{:S(2)}, u32[]{:S(2)}) %collective-permute-start.27) | collective-permute-done | bytes 79904 | tf_op jit(solution)/shard_map/ppermute | solution.py:25
  115.3 2.2 %collective-permute-done.23 = bf16[1,104,384]{2,1,0:T(8,128)(2,1)S(1)} collective-permute-done((bf16[1,104,384]{2,1,0:T(8,128)(2,1)S(1)}, bf16[1,104,384]{2,1,0:T(8,128)(2,1)S(1)}, u32[]{:S(2)}, u32[]{:S(2)}) %collective-permute-start.23) | collective-permute-done | bytes 79904 | tf_op jit(solution)/shard_map/ppermute | solution.py:25
  117.6 0.5 collective-permute-start.24
  118.0 0.4 collective-permute-done.19
  118.5 2.9 %collective-permute-start.20 = (bf16[2,104,384]{2,1,0:T(8,128)(2,1)S(1)}, bf16[2,104,384]{2,1,0:T(8,128)(2,1)S(1)}, u32[]{:S(2)}, u32[]{:S(2)}) collective-permute-start(bf16[2,104,384]{2,1,0:T(8,128)(2,1)S(1)} %pad_maximum_fusion.refs_0_), channel_id=1, source_target_pairs={{0,8},{8,0},{16,24},{24,16},{1,9},{9,1},{17,25},{25,17},{2,10},{10... | collective-permute-start | bytes 479240 | tf_op jit(solution)/shard_map/ppermute | solution.py:25
  121.3 3.8 %shard_map.129.refs_7_ = bf16[3,1536,1024]{2,1,0:T(8,128)(2,1)S(1)} custom-call(bf16[3,1536,1024]{2,1,0:T(8,128)(2,1)} %source_ref.1), custom_call_target="tpu_custom_call" | custom-call | bytes 18874368 | tf_op jit(solution)/shard_map/pallas_call | solution.py:132
  125.1 1.6 %collective-permute-done.20.refs_1_ = bf16[2,104,384]{2,1,0:T(8,128)(2,1)S(1)} collective-permute-done((bf16[2,104,384]{2,1,0:T(8,128)(2,1)S(1)}, bf16[2,104,384]{2,1,0:T(8,128)(2,1)S(1)}, u32[]{:S(2)}, u32[]{:S(2)}) %collective-permute-start.20) | collective-permute-done | bytes 159776 | tf_op jit(solution)/shard_map/ppermute | solution.py:25
  126.7 2.3 %shard_map.130 = (f32[128,1024]{1,0:T(8,128)S(1)}, bf16[128,1024]{1,0:T(8,128)(2,1)S(1)}) custom-call(s32[1]{0:T(128)} %bitcast.place_ref, bf16[2,104,384]{2,1,0:T(8,128)(2,1)S(1)} %pad_maximum_fusion.refs_0_, bf16[2,104,384]{2,1,0:T(8,128)(2,1)S(1)} %collective-permute-done.20.refs_1_, bf16[2,104,384]{2,1,0:T(8,128)(2,1)S(1)} %pad_maximum_fusion.1.refs_2_, ...), custom_call_target="tpu_custom_call" | custom-call | flops 981467136 | bytes 9437184 | tf_op jit(solution)/shard_map/pallas_call | solution.py:382
  129.2 1.5 %collective-permute-done.29 = bf16[4,32,1024]{2,1,0:T(8,128)(2,1)S(1)} collective-permute-done((bf16[4,32,1024]{2,1,0:T(8,128)(2,1)S(1)}, bf16[4,32,1024]{2,1,0:T(8,128)(2,1)S(1)}, u32[]{:S(2)}, u32[]{:S(2)}) %collective-permute-start.29) | collective-permute-done | bytes 262176 | tf_op jit(solution)/shard_map/ppermute | solution.py:25
  130.8 1.6 %collective-permute-start.30 = (bf16[32,1024]{1,0:T(8,128)(2,1)S(1)}, bf16[32,1024]{1,0:T(8,128)(2,1)S(1)}, u32[]{:S(2)}, u32[]{:S(2)}) collective-permute-start(bf16[32,1024]{1,0:T(8,128)(2,1)S(1)} %get-tuple-element.71), channel_id=1, source_target_pairs={{0,2},{1,3},{2,0},{3,1},{4,6},{5,7},{6,4},{7,5},{8,10},{9,11},{10,... | collective-permute-start | bytes 196616 | tf_op jit(solution)/shard_map/ppermute | solution.py:25
  132.4 0.8 collective-permute-start.31
  133.1 1.2 collective-permute-start.32
  134.3 0.7 copy.48
  135.1 2.2 %collective-permute-done.31 = bf16[32,1024]{1,0:T(8,128)(2,1)S(1)} collective-permute-done((bf16[32,1024]{1,0:T(8,128)(2,1)S(1)}, bf16[32,1024]{1,0:T(8,128)(2,1)S(1)}, u32[]{:S(2)}, u32[]{:S(2)}) %collective-permute-start.31) | collective-permute-done | bytes 65568 | tf_op jit(solution)/shard_map/ppermute | solution.py:25
  137.3 0.9 collective-permute-done.32
  138.3 0.7 copy.38
  (87 shorter events, 3.8 us)
Async XLA Ops:
  1.6 18.4 %collective-permute-start = (bf16[8,64,128]{2,1,0:T(8,128)(2,1)S(1)}, bf16[8,64,128]{2,1,0:T(8,128)(2,1)S(1)}, u32[]{:S(2)}, u32[]{:S(2)}) collective-permute-start(bf16[8,64,128]{2,1,0:T(8,128)(2,1)S(1)} %bitcast.167), channel_id=1, source_target_pairs={{0,8},{8,16},{16,24},{24,0},{1,9},{9,17},{17,25},{25,1},{2,10},{10... | collective-permute-start | bytes 393224 | tf_op jit(solution)/shard_map/ppermute | solution.py:21
  4.6 15.3 %collective-permute-start.1 = (bf16[8,64,128]{2,1,0:T(8,128)(2,1)S(1)}, bf16[8,64,128]{2,1,0:T(8,128)(2,1)S(1)}, u32[]{:S(2)}, u32[]{:S(2)}) collective-permute-start(bf16[8,64,128]{2,1,0:T(8,128)(2,1)S(1)} %bitcast.168), channel_id=1, source_target_pairs={{0,16},{8,24},{16,0},{24,8},{1,17},{9,25},{17,1},{25,9},{2,18},{10... | collective-permute-start | bytes 393224 | tf_op jit(solution)/shard_map/ppermute | solution.py:21
  7.2 1.0 copy-start
  8.3 0.7 copy-start.2
  11.8 3.7 %collective-permute-start.10 = (f32[32,16]{0,1:T(8,128)S(1)}, f32[32,16]{0,1:T(8,128)S(1)}, u32[]{:S(2)}, u32[]{:S(2)}) collective-permute-start(f32[32,16]{0,1:T(8,128)S(1)} %constant_dynamic-update-slice_fusion), channel_id=1, source_target_pairs={{0,4},{1,5},{2,6},{3,7},{4,0},{5,1},{6,2},{7,3},{8,12},{9,13},{10,... | collective-permute-start | bytes 6152 | tf_op jit(solution)/shard_map/ppermute | solution.py:25
  13.3 4.5 %collective-permute-start.11 = (f32[32,16]{0,1:T(8,128)S(1)}, f32[32,16]{0,1:T(8,128)S(1)}, u32[]{:S(2)}, u32[]{:S(2)}) collective-permute-start(f32[32,16]{0,1:T(8,128)S(1)} %constant_dynamic-update-slice_fusion), channel_id=1, source_target_pairs={{0,6},{1,7},{2,4},{3,5},{4,2},{5,3},{6,0},{7,1},{8,14},{9,15},{10,... | collective-permute-start | bytes 6152 | tf_op jit(solution)/shard_map/ppermute | solution.py:25
  14.7 3.7 %collective-permute-start.9 = (f32[32,16]{0,1:T(8,128)S(1)}, f32[32,16]{0,1:T(8,128)S(1)}, u32[]{:S(2)}, u32[]{:S(2)}) collective-permute-start(f32[32,16]{0,1:T(8,128)S(1)} %constant_dynamic-update-slice_fusion), channel_id=1, source_target_pairs={{0,2},{1,3},{2,0},{3,1},{4,6},{5,7},{6,4},{7,5},{8,10},{9,11},{10,... | collective-permute-start | bytes 6152 | tf_op jit(solution)/shard_map/ppermute | solution.py:25
  15.4 5.0 %collective-permute-start.2 = (bf16[8,64,128]{2,1,0:T(8,128)(2,1)S(1)}, bf16[8,64,128]{2,1,0:T(8,128)(2,1)S(1)}, u32[]{:S(2)}, u32[]{:S(2)}) collective-permute-start(bf16[8,64,128]{2,1,0:T(8,128)(2,1)S(1)} %bitcast.170), channel_id=1, source_target_pairs={{0,24},{8,0},{16,8},{24,16},{1,25},{9,1},{17,9},{25,17},{2,26},{10... | collective-permute-start | bytes 393224 | tf_op jit(solution)/shard_map/ppermute | solution.py:21
  18.5 1.2 collective-permute-start.12
  20.4 1.2 copy-start.3
  22.9 8.7 %collective-permute-start.5 = (bf16[9,64,128]{2,1,0:T(8,128)(2,1)S(1)}, bf16[9,64,128]{2,1,0:T(8,128)(2,1)S(1)}, u32[]{:S(2)}, u32[]{:S(2)}) collective-permute-start(bf16[9,64,128]{2,1,0:T(8,128)(2,1)S(1)} %get-tuple-element.34), channel_id=1, source_target_pairs={{0,8},{8,16},{16,24},{24,0},{1,9},{9,17},{17,25},{25,1},{2,10},{10... | collective-permute-start | bytes 442376 | tf_op jit(solution)/shard_map/ppermute | solution.py:21
  23.0 13.7 %collective-permute-start.4 = (bf16[9,64,128]{2,1,0:T(8,128)(2,1)S(1)}, bf16[9,64,128]{2,1,0:T(8,128)(2,1)S(1)}, u32[]{:S(2)}, u32[]{:S(2)}) collective-permute-start(bf16[9,64,128]{2,1,0:T(8,128)(2,1)S(1)} %get-tuple-element.33), channel_id=1, source_target_pairs={{0,16},{8,24},{16,0},{24,8},{1,17},{9,25},{17,1},{25,9},{2,18},{10... | collective-permute-start | bytes 442376 | tf_op jit(solution)/shard_map/ppermute | solution.py:21
  26.7 10.1 %collective-permute-start.3 = (bf16[9,64,128]{2,1,0:T(8,128)(2,1)S(1)}, bf16[9,64,128]{2,1,0:T(8,128)(2,1)S(1)}, u32[]{:S(2)}, u32[]{:S(2)}) collective-permute-start(bf16[9,64,128]{2,1,0:T(8,128)(2,1)S(1)} %get-tuple-element.32), channel_id=1, source_target_pairs={{0,24},{8,0},{16,8},{24,16},{1,25},{9,1},{17,9},{25,17},{2,26},{10... | collective-permute-start | bytes 442376 | tf_op jit(solution)/shard_map/ppermute | solution.py:21
  37.4 11.3 %collective-permute-start.6 = (bf16[8,8192]{1,0:T(8,128)(2,1)S(1)}, bf16[8,8192]{1,0:T(8,128)(2,1)S(1)}, u32[]{:S(2)}, u32[]{:S(2)}) collective-permute-start(bf16[8,8192]{1,0:T(8,128)(2,1)S(1)} %bitcast.161), channel_id=1, source_target_pairs={{0,8},{8,16},{16,24},{24,0},{1,9},{9,17},{17,25},{25,1},{2,10},{10... | collective-permute-start | bytes 393224 | tf_op jit(solution)/shard_map/ppermute | solution.py:21
  40.2 9.3 %collective-permute-start.7 = (bf16[8,8192]{1,0:T(8,128)(2,1)S(1)}, bf16[8,8192]{1,0:T(8,128)(2,1)S(1)}, u32[]{:S(2)}, u32[]{:S(2)}) collective-permute-start(bf16[8,8192]{1,0:T(8,128)(2,1)S(1)} %bitcast.162), channel_id=1, source_target_pairs={{0,16},{8,24},{16,0},{24,8},{1,17},{9,25},{17,1},{25,9},{2,18},{10... | collective-permute-start | bytes 393224 | tf_op jit(solution)/shard_map/ppermute | solution.py:21
  40.5 9.0 %collective-permute-start.8 = (bf16[8,8192]{1,0:T(8,128)(2,1)S(1)}, bf16[8,8192]{1,0:T(8,128)(2,1)S(1)}, u32[]{:S(2)}, u32[]{:S(2)}) collective-permute-start(bf16[8,8192]{1,0:T(8,128)(2,1)S(1)} %bitcast.163), channel_id=1, source_target_pairs={{0,24},{8,0},{16,8},{24,16},{1,25},{9,1},{17,9},{25,17},{2,26},{10... | collective-permute-start | bytes 393224 | tf_op jit(solution)/shard_map/ppermute | solution.py:21
  42.9 6.6 %copy-start.1 = (f32[1024]{0:T(1024)S(1)}, f32[1024]{0:T(1024)}, u32[]{:S(2)}) copy-start(f32[1024]{0:T(1024)} %param.17) | copy-start | bytes 12292
  52.6 4.4 %collective-permute-start.13 = (bf16[32,1152]{1,0:T(8,128)(2,1)S(1)}, bf16[32,1152]{1,0:T(8,128)(2,1)S(1)}, u32[]{:S(2)}, u32[]{:S(2)}) collective-permute-start(bf16[32,1152]{1,0:T(8,128)(2,1)S(1)} %get-tuple-element.40), channel_id=1, source_target_pairs={{0,2},{1,3},{2,0},{3,1},{4,6},{5,7},{6,4},{7,5},{8,10},{9,11},{10,... | collective-permute-start | bytes 221192 | tf_op jit(solution)/shard_map/ppermute | solution.py:25
  53.5 4.8 %collective-permute-start.14 = (bf16[32,1152]{1,0:T(8,128)(2,1)S(1)}, bf16[32,1152]{1,0:T(8,128)(2,1)S(1)}, u32[]{:S(2)}, u32[]{:S(2)}) collective-permute-start(bf16[32,1152]{1,0:T(8,128)(2,1)S(1)} %get-tuple-element.40), channel_id=1, source_target_pairs={{0,4},{1,5},{2,6},{3,7},{4,0},{5,1},{6,2},{7,3},{8,12},{9,13},{10,... | collective-permute-start | bytes 221192 | tf_op jit(solution)/shard_map/ppermute | solution.py:25
  54.6 5.3 %collective-permute-start.15 = (bf16[32,1152]{1,0:T(8,128)(2,1)S(1)}, bf16[32,1152]{1,0:T(8,128)(2,1)S(1)}, u32[]{:S(2)}, u32[]{:S(2)}) collective-permute-start(bf16[32,1152]{1,0:T(8,128)(2,1)S(1)} %get-tuple-element.40), channel_id=1, source_target_pairs={{0,6},{1,7},{2,4},{3,5},{4,2},{5,3},{6,0},{7,1},{8,14},{9,15},{10,... | collective-permute-start | bytes 221192 | tf_op jit(solution)/shard_map/ppermute | solution.py:25
  59.9 1.6 %collective-permute-start.16 = (bf16[128,1152]{1,0:T(8,128)(2,1)S(1)}, bf16[128,1152]{1,0:T(8,128)(2,1)S(1)}, u32[]{:S(2)}, u32[]{:S(2)}) collective-permute-start(bf16[128,1152]{1,0:T(8,128)(2,1)S(1)} %constant_dynamic-update-slice_fusion.2.near_ref), channel_id=1, source_target_pairs={{0,1},{1,0},{2,3},{3,2},{4,5},{5,4},{6,7},{7,6},{8,9},{9,8},{10,11... | collective-permute-start | bytes 884744 | tf_op jit(solution)/shard_map/ppermute | solution.py:25
  65.3 12.8 %collective-permute-start.25 = (bf16[2,104,768]{2,1,0:T(8,128)(2,1)S(1)}, bf16[2,104,768]{2,1,0:T(8,128)(2,1)S(1)}, u32[]{:S(2)}, u32[]{:S(2)}) collective-permute-start(bf16[2,104,768]{2,1,0:T(8,128)(2,1)S(1)} %get-tuple-element.48), channel_id=1, source_target_pairs={{0,8},{8,0},{16,24},{24,16},{1,9},{9,1},{17,25},{25,17},{2,10},{10... | collective-permute-start | bytes 958472 | tf_op jit(solution)/shard_map/ppermute | solution.py:25
  72.2 15.5 %collective-permute-start.17 = (bf16[2,112,768]{2,1,0:T(8,128)(2,1)S(1)}, bf16[2,112,768]{2,1,0:T(8,128)(2,1)S(1)}, u32[]{:S(2)}, u32[]{:S(2)}) collective-permute-start(bf16[2,112,768]{2,1,0:T(8,128)(2,1)S(1)} %get-tuple-element.42), channel_id=1, source_target_pairs={{0,8},{8,0},{16,24},{24,16},{1,9},{9,1},{17,25},{25,17},{2,10},{10... | collective-permute-start | bytes 1032200 | tf_op jit(solution)/shard_map/ppermute | solution.py:25
  75.9 19.5 %collective-permute-start.21 = (bf16[2,104,768]{2,1,0:T(8,128)(2,1)S(1)}, bf16[2,104,768]{2,1,0:T(8,128)(2,1)S(1)}, u32[]{:S(2)}, u32[]{:S(2)}) collective-permute-start(bf16[2,104,768]{2,1,0:T(8,128)(2,1)S(1)} %get-tuple-element.45), channel_id=1, source_target_pairs={{0,8},{8,0},{16,24},{24,16},{1,9},{9,1},{17,25},{25,17},{2,10},{10... | collective-permute-start | bytes 958472 | tf_op jit(solution)/shard_map/ppermute | solution.py:25
  78.1 28.3 %collective-permute-start.26 = (bf16[1,104,768]{2,1,0:T(8,128)(2,1)S(1)}, bf16[1,104,768]{2,1,0:T(8,128)(2,1)S(1)}, u32[]{:S(2)}, u32[]{:S(2)}) collective-permute-start(bf16[1,104,768]{2,1,0:T(8,128)(2,1)S(1)} %fusion.10), channel_id=1, source_target_pairs={{0,16},{8,24},{16,0},{24,8},{1,17},{9,25},{17,1},{25,9},{2,18},{10... | collective-permute-start | bytes 479240 | tf_op jit(solution)/shard_map/ppermute | solution.py:25
  87.8 18.3 %collective-permute-start.18 = (bf16[1,112,768]{2,1,0:T(8,128)(2,1)S(1)}, bf16[1,112,768]{2,1,0:T(8,128)(2,1)S(1)}, u32[]{:S(2)}, u32[]{:S(2)}) collective-permute-start(bf16[1,112,768]{2,1,0:T(8,128)(2,1)S(1)} %fusion.8), channel_id=1, source_target_pairs={{0,16},{8,24},{16,0},{24,8},{1,17},{9,25},{17,1},{25,9},{2,18},{10... | collective-permute-start | bytes 516104 | tf_op jit(solution)/shard_map/ppermute | solution.py:25
  95.4 14.2 %collective-permute-start.22 = (bf16[1,104,768]{2,1,0:T(8,128)(2,1)S(1)}, bf16[1,104,768]{2,1,0:T(8,128)(2,1)S(1)}, u32[]{:S(2)}, u32[]{:S(2)}) collective-permute-start(bf16[1,104,768]{2,1,0:T(8,128)(2,1)S(1)} %fusion.9), channel_id=1, source_target_pairs={{0,16},{8,24},{16,0},{24,8},{1,17},{9,25},{17,1},{25,9},{2,18},{10... | collective-permute-start | bytes 479240 | tf_op jit(solution)/shard_map/ppermute | solution.py:25
  106.6 8.6 %collective-permute-start.27 = (bf16[1,104,384]{2,1,0:T(8,128)(2,1)S(1)}, bf16[1,104,384]{2,1,0:T(8,128)(2,1)S(1)}, u32[]{:S(2)}, u32[]{:S(2)}) collective-permute-start(bf16[1,104,384]{2,1,0:T(8,128)(2,1)S(1)} %fusion.24), channel_id=1, source_target_pairs={{0,16},{8,24},{16,0},{24,8},{1,17},{9,25},{17,1},{25,9},{2,18},{10... | collective-permute-start | bytes 239624 | tf_op jit(solution)/shard_map/ppermute | solution.py:25
  109.8 7.7 %collective-permute-start.23 = (bf16[1,104,384]{2,1,0:T(8,128)(2,1)S(1)}, bf16[1,104,384]{2,1,0:T(8,128)(2,1)S(1)}, u32[]{:S(2)}, u32[]{:S(2)}) collective-permute-start(bf16[1,104,384]{2,1,0:T(8,128)(2,1)S(1)} %fusion.23), channel_id=1, source_target_pairs={{0,16},{8,24},{16,0},{24,8},{1,17},{9,25},{17,1},{25,9},{2,18},{10... | collective-permute-start | bytes 239624 | tf_op jit(solution)/shard_map/ppermute | solution.py:25
  110.1 8.4 %collective-permute-start.19 = (bf16[1,104,384]{2,1,0:T(8,128)(2,1)S(1)}, bf16[1,104,384]{2,1,0:T(8,128)(2,1)S(1)}, u32[]{:S(2)}, u32[]{:S(2)}) collective-permute-start(bf16[1,104,384]{2,1,0:T(8,128)(2,1)S(1)} %fusion.22), channel_id=1, source_target_pairs={{0,16},{8,24},{16,0},{24,8},{1,17},{9,25},{17,1},{25,9},{2,18},{10... | collective-permute-start | bytes 239624 | tf_op jit(solution)/shard_map/ppermute | solution.py:25
  115.2 9.9 %collective-permute-start.28 = (bf16[2,104,384]{2,1,0:T(8,128)(2,1)S(1)}, bf16[2,104,384]{2,1,0:T(8,128)(2,1)S(1)}, u32[]{:S(2)}, u32[]{:S(2)}) collective-permute-start(bf16[2,104,384]{2,1,0:T(8,128)(2,1)S(1)} %pad_maximum_fusion.2.refs_4_), channel_id=1, source_target_pairs={{0,8},{8,0},{16,24},{24,16},{1,9},{9,1},{17,25},{25,17},{2,10},{10... | collective-permute-start | bytes 479240 | tf_op jit(solution)/shard_map/ppermute | solution.py:25
  117.6 7.6 %collective-permute-start.24 = (bf16[2,104,384]{2,1,0:T(8,128)(2,1)S(1)}, bf16[2,104,384]{2,1,0:T(8,128)(2,1)S(1)}, u32[]{:S(2)}, u32[]{:S(2)}) collective-permute-start(bf16[2,104,384]{2,1,0:T(8,128)(2,1)S(1)} %pad_maximum_fusion.1.refs_2_), channel_id=1, source_target_pairs={{0,8},{8,0},{16,24},{24,16},{1,9},{9,1},{17,25},{25,17},{2,10},{10... | collective-permute-start | bytes 479240 | tf_op jit(solution)/shard_map/ppermute | solution.py:25
  118.5 8.3 %collective-permute-start.20 = (bf16[2,104,384]{2,1,0:T(8,128)(2,1)S(1)}, bf16[2,104,384]{2,1,0:T(8,128)(2,1)S(1)}, u32[]{:S(2)}, u32[]{:S(2)}) collective-permute-start(bf16[2,104,384]{2,1,0:T(8,128)(2,1)S(1)} %pad_maximum_fusion.refs_0_), channel_id=1, source_target_pairs={{0,8},{8,0},{16,24},{24,16},{1,9},{9,1},{17,25},{25,17},{2,10},{10... | collective-permute-start | bytes 479240 | tf_op jit(solution)/shard_map/ppermute | solution.py:25
  129.1 1.6 %collective-permute-start.29 = (bf16[4,32,1024]{2,1,0:T(8,128)(2,1)S(1)}, bf16[4,32,1024]{2,1,0:T(8,128)(2,1)S(1)}, u32[]{:S(2)}, u32[]{:S(2)}) collective-permute-start(bf16[4,32,1024]{2,1,0:T(8,128)(2,1)S(1)} %bitcast.176), channel_id=1, source_target_pairs={{0,1},{1,0},{2,3},{3,2},{4,5},{5,4},{6,7},{7,6},{8,9},{9,8},{10,11... | collective-permute-start | bytes 786440 | tf_op jit(solution)/shard_map/ppermute | solution.py:25
  130.8 4.3 %collective-permute-start.30 = (bf16[32,1024]{1,0:T(8,128)(2,1)S(1)}, bf16[32,1024]{1,0:T(8,128)(2,1)S(1)}, u32[]{:S(2)}, u32[]{:S(2)}) collective-permute-start(bf16[32,1024]{1,0:T(8,128)(2,1)S(1)} %get-tuple-element.71), channel_id=1, source_target_pairs={{0,2},{1,3},{2,0},{3,1},{4,6},{5,7},{6,4},{7,5},{8,10},{9,11},{10,... | collective-permute-start | bytes 196616 | tf_op jit(solution)/shard_map/ppermute | solution.py:25
  132.4 5.0 %collective-permute-start.31 = (bf16[32,1024]{1,0:T(8,128)(2,1)S(1)}, bf16[32,1024]{1,0:T(8,128)(2,1)S(1)}, u32[]{:S(2)}, u32[]{:S(2)}) collective-permute-start(bf16[32,1024]{1,0:T(8,128)(2,1)S(1)} %get-tuple-element.73), channel_id=1, source_target_pairs={{0,4},{1,5},{2,6},{3,7},{4,0},{5,1},{6,2},{7,3},{8,12},{9,13},{10,... | collective-permute-start | bytes 196616 | tf_op jit(solution)/shard_map/ppermute | solution.py:25
  133.1 5.2 %collective-permute-start.32 = (bf16[32,1024]{1,0:T(8,128)(2,1)S(1)}, bf16[32,1024]{1,0:T(8,128)(2,1)S(1)}, u32[]{:S(2)}, u32[]{:S(2)}) collective-permute-start(bf16[32,1024]{1,0:T(8,128)(2,1)S(1)} %get-tuple-element.72), channel_id=1, source_target_pairs={{0,6},{1,7},{2,4},{3,5},{4,2},{5,3},{6,0},{7,1},{8,14},{9,15},{10,... | collective-permute-start | bytes 196616 | tf_op jit(solution)/shard_map/ppermute | solution.py:25

commit v5 on v4

--- a/solution.py
+++ b/solution.py
@@ -13,6 +13,7 @@
 TOPK = 8
 NEGATIVE = -1e30
 EPSILON = 1e-06
+CARRIER = 0
 MIB = 1 << 20
 SCOPED = 10 * MIB
 
@@ -263,7 +264,7 @@
 
 def gate_up_parts(pick, near, far, extra, weights, expert, place, samples):
     slots, rows = pick.shape
-    more = 0 if expert else extra.shape[0]
+    more = extra.shape[0] if expert == CARRIER else 0
     _, features, wide = weights.shape
     hidden = wide // 2
     part = hidden // samples
@@ -302,16 +303,17 @@
     return results[:-1], results[-1]
 
 
-def reduce_parts(keep, arrived, samples):
+def reduce_parts(keep, arrived, samples, after):
     bits = 1
     while True:
         keep = [a.astype(jnp.float32) + arrived[i].astype(jnp.float32) for i, a in enumerate(keep)]
         bits *= 2
         if bits == samples:
             return keep[0]
-        arrived = swap(
-            jnp.stack([a.astype(jnp.bfloat16) for a in keep[1::2]]), "sample", samples, bits
-        )
+        give = jnp.stack([a.astype(jnp.bfloat16) for a in keep[1::2]])
+        if after is not None:
+            give, _ = lax.optimization_barrier((give, after))
+        arrived = swap(give, "sample", samples, bits)
         keep = keep[0::2]
 
 
@@ -426,7 +428,10 @@
     all_queries = [query] + [send(query, "sample", samples, k) for k in range(1, samples)]
 
     gen_out, gen_stat = gen_part(query, gen_kv[:, 0], gen_lengths[:, 0])
-    routes, route_probs, gen_out = lax.optimization_barrier((routes, route_probs, gen_out))
+    prompt_kv, _ = lax.optimization_barrier((prompt_kv, gen_out))
+    parts = list(prompt_part(all_queries, fetch(prompt_kv)))
+    parts = [parts[0]] + [send(parts[k], "sample", samples, -k) for k in range(1, samples)]
+    routes, route_probs, parts[-1] = lax.optimization_barrier((routes, route_probs, parts[-1]))
     by_sample = lambda a: jnp.swapaxes(a, 0, 1).reshape(rows, TOPK)
     table = jnp.concatenate(
         [by_sample(routes).astype(jnp.float32), by_sample(route_probs)], axis=1
@@ -453,8 +458,6 @@
     pick = chosen.astype(jnp.bfloat16)
     slot_weight = jnp.sum(jnp.where(chosen, weight[:, None, :], 0.0), axis=2)
 
-    parts = list(prompt_part(all_queries, prompt_kv))
-    parts = [parts[0]] + [send(parts[k], "sample", samples, -k) for k in range(1, samples)]
     outs = [gen_out] + [part[:prompts] for part in parts]
     marks = [(gen_stat[0], gen_stat[1])] + [
         part_marks(part, prompts, k) for k, part in enumerate(parts)
@@ -466,7 +469,9 @@
         o.astype(jnp.float32) * (c / total)[:, :, None] for o, c in zip(outs, scales)
     )
     attended = attended.astype(jnp.bfloat16).reshape(prompts, heads * HDIM)
-    out_proj, attended = lax.optimization_barrier((out_proj, attended))
+    out_proj, _, pick, chosen, slot_weight = lax.optimization_barrier(
+        (out_proj, attended, pick, chosen, slot_weight)
+    )
     out_proj = fetch(out_proj)
     attended = [attended] + [send(attended, "sample", samples, k) for k in range(1, samples)]
     mixed, row_block = project(
@@ -485,15 +490,15 @@
     total_rows = owners * rows
     extra_rows = -(-2 * total_rows // (16 * part)) * 8
     extra = jnp.pad(square, (0, extra_rows * 2 * part - square.size)).reshape(extra_rows, 2 * part)
-    sums = []
-    for j in range(per_owner):
+    sums = {}
+    for j in reversed(range(per_owner)):
         keep, give = gate_up_parts(pick[j], near, far, extra, w_gate_up, j, place, samples)
         arrived = swap(give, "sample", samples, 1)
-        sums.append((keep, arrived))
-    acts = []
-    for j in range(per_owner):
-        gate_up = reduce_parts(*sums[j], samples)
-        if j == 0:
+        sums[j] = keep, arrived
+    acts = [None] * (2 * per_owner)
+    for j in [CARRIER] + [j for j in range(per_owner) if j != CARRIER]:
+        gate_up = reduce_parts(*sums[j], samples, first_act if j == 1 else None)
+        if j == CARRIER:
             square = gate_up[slots:].reshape(-1)
             square = square[:total_rows] + square[total_rows : 2 * total_rows]
             factor = lax.rsqrt(square / (width * samples) + EPSILON)
@@ -502,8 +507,9 @@
         gate_up = gate_up * slot_factor[j][:, None]
         act = jax.nn.silu(gate_up[:, :part]) * gate_up[:, part:] * slot_weight[j][:, None]
         act = act.astype(jnp.bfloat16)
+        first_act = act if j == 0 else first_act
         act_near, act_far, order = gather_parts(act, samples)
-        acts = acts + [act_near, act_far]
+        acts[2 * j : 2 * j + 2] = act_near, act_far
     w_down, acts[-2] = lax.optimization_barrier((w_down, acts[-2]))
     w_down = fetch(w_down)
     kept, given = down_rows(acts, order, pick, w_down, place)

time: 139 us -> 138 us (level)
    ppermute x9, waiting for transfers between devices: 11.1 us -> 8.37 us  [send(): lax.ppermute(array, axis, [(i, (i + shift) % size) for i in range(size)])]
    ppermute x24, waiting for transfers between devices: 45.4 us -> 47.2 us  [swap(): return lax.ppermute(array, axis, [(i, i ^ bits) for i in range(size)])]
    unnamed x16 -> x14, local copies, waits for them, and re-layouts: 4.67 us -> 3.45 us
    pallas_call x2 -> x3, Pallas kernels: 9.69 us -> 10.9 us  [fetch(): pl.pallas_call(fetch_kernel, out_shape=jax.ShapeDtypeStruct(array.shape,...]
  transfers between devices with their start and end apart: 33 -> 33, of which waited for: 24 -> 21; matrix products, arithmetic and copies ran while one was open for 4% -> 4% of each run, Pallas kernels for 13% -> 14%
where the time goes in v5:
time: 138 us
  waiting for transfers between devices  55.6 us (40%)
  starting transfers between devices  42.5 us (31%)
  Pallas kernels  29.4 us (21%)
  local copies, waits for them, and re-layouts  6.58 us (5%)
  other arithmetic  2.89 us (2%)
    ppermute x24, waiting for transfers between devices, swap(): return lax.ppermute(array, axis, [(i, i ^ bits) for i in range(size)])  47.2 us
    ppermute x24, starting transfers between devices, swap(): return lax.ppermute(array, axis, [(i, i ^ bits) for i in range(size)])  25.8 us
    ppermute x9, starting transfers between devices, send(): lax.ppermute(array, axis, [(i, (i + shift) % size) for i in range(size)])  16.7 us
    pallas_call x3, Pallas kernels, fetch(): pl.pallas_call(fetch_kernel, out_shape=jax.ShapeDtypeStruct(array.shape,...  10.9 us
    pallas_call x3, Pallas kernels, gate_up_parts(): pl.pallas_call(functools.partial(gate_kernel, features, expert), out_shap...  10.7 us
    ppermute x9, waiting for transfers between devices, send(): lax.ppermute(array, axis, [(i, (i + shift) % size) for i in range(size)])  8.37 us
    unnamed x14, local copies, waits for them, and re-layouts  3.45 us
    pallas_call x1, Pallas kernels, project(): pl.pallas_call(functools.partial(project_kernel, samples, width), out_sha...  3.09 us
  transfers between devices with their start and end apart: 33, of which 21 were waited for; matrix products, arithmetic and copies ran while one was open for 4% of the time, Pallas kernels for 14%

profile of v5, /device:TPU:0, one launch (start us, length us, event | category | flops | bytes accessed | tf_op | source)
XLA Modules:
  0.0 138.1 jit_solution(5166182966761127357)
XLA Ops:
  0.6 0.9 copy.47
  1.6 3.1 %collective-permute-start = (bf16[8,64,128]{2,1,0:T(8,128)(2,1)S(1)}, bf16[8,64,128]{2,1,0:T(8,128)(2,1)S(1)}, u32[]{:S(2)}, u32[]{:S(2)}) collective-permute-start(bf16[8,64,128]{2,1,0:T(8,128)(2,1)S(1)} %bitcast.167), channel_id=1, source_target_pairs={{0,8},{8,16},{16,24},{24,0},{1,9},{9,17},{17,25},{25,1},{2,10},{10... | collective-permute-start | bytes 393224 | tf_op jit(solution)/shard_map/ppermute | solution.py:22
  4.6 2.6 %collective-permute-start.1 = (bf16[8,64,128]{2,1,0:T(8,128)(2,1)S(1)}, bf16[8,64,128]{2,1,0:T(8,128)(2,1)S(1)}, u32[]{:S(2)}, u32[]{:S(2)}) collective-permute-start(bf16[8,64,128]{2,1,0:T(8,128)(2,1)S(1)} %bitcast.168), channel_id=1, source_target_pairs={{0,16},{8,24},{16,0},{24,8},{1,17},{9,25},{17,1},{25,9},{2,18},{10... | collective-permute-start | bytes 393224 | tf_op jit(solution)/shard_map/ppermute | solution.py:22
  7.2 1.3 collective-permute-start.2
  8.6 1.0 copy-done
  9.6 0.7 copy-done.2
  10.3 1.1 shard_map.122
  11.3 1.2 shard_map.123.refs_4_
  12.6 0.9 copy.49
  13.5 2.4 %collective-permute-done.1.refs_2_ = bf16[8,64,128]{2,1,0:T(8,128)(2,1)S(1)} collective-permute-done((bf16[8,64,128]{2,1,0:T(8,128)(2,1)S(1)}, bf16[8,64,128]{2,1,0:T(8,128)(2,1)S(1)}, u32[]{:S(2)}, u32[]{:S(2)}) %collective-permute-start.1) | collective-permute-done | bytes 131104 | tf_op jit(solution)/shard_map/ppermute | solution.py:22
  15.9 1.3 shard_map.124
  17.2 3.3 %collective-permute-start.5 = (bf16[9,64,128]{2,1,0:T(8,128)(2,1)S(1)}, bf16[9,64,128]{2,1,0:T(8,128)(2,1)S(1)}, u32[]{:S(2)}, u32[]{:S(2)}) collective-permute-start(bf16[9,64,128]{2,1,0:T(8,128)(2,1)S(1)} %get-tuple-element.38), channel_id=1, source_target_pairs={{0,8},{8,16},{16,24},{24,0},{1,9},{9,17},{17,25},{25,1},{2,10},{10... | collective-permute-start | bytes 442376 | tf_op jit(solution)/shard_map/ppermute | solution.py:22
  20.5 1.6 %collective-permute-start.4 = (bf16[9,64,128]{2,1,0:T(8,128)(2,1)S(1)}, bf16[9,64,128]{2,1,0:T(8,128)(2,1)S(1)}, u32[]{:S(2)}, u32[]{:S(2)}) collective-permute-start(bf16[9,64,128]{2,1,0:T(8,128)(2,1)S(1)} %get-tuple-element.37), channel_id=1, source_target_pairs={{0,16},{8,24},{16,0},{24,8},{1,17},{9,25},{17,1},{25,9},{2,18},{10... | collective-permute-start | bytes 442376 | tf_op jit(solution)/shard_map/ppermute | solution.py:22
  22.1 0.8 collective-permute-start.3
  22.9 3.1 %collective-permute-done.5 = bf16[9,64,128]{2,1,0:T(8,128)(2,1)S(1)} collective-permute-done((bf16[9,64,128]{2,1,0:T(8,128)(2,1)S(1)}, bf16[9,64,128]{2,1,0:T(8,128)(2,1)S(1)}, u32[]{:S(2)}, u32[]{:S(2)}) %collective-permute-start.5) | collective-permute-done | bytes 147488 | tf_op jit(solution)/shard_map/ppermute | solution.py:22
  26.0 0.7 convert_bitcast_fusion
  26.9 0.8 copy.33
  27.8 1.5 %collective-permute-start.10 = (f32[32,16]{0,1:T(8,128)S(1)}, f32[32,16]{0,1:T(8,128)S(1)}, u32[]{:S(2)}, u32[]{:S(2)}) collective-permute-start(f32[32,16]{0,1:T(8,128)S(1)} %constant_dynamic-update-slice_fusion), channel_id=1, source_target_pairs={{0,4},{1,5},{2,6},{3,7},{4,0},{5,1},{6,2},{7,3},{8,12},{9,13},{10,... | collective-permute-start | bytes 6152 | tf_op jit(solution)/shard_map/ppermute | solution.py:26
  29.3 1.4 %collective-permute-start.11 = (f32[32,16]{0,1:T(8,128)S(1)}, f32[32,16]{0,1:T(8,128)S(1)}, u32[]{:S(2)}, u32[]{:S(2)}) collective-permute-start(f32[32,16]{0,1:T(8,128)S(1)} %constant_dynamic-update-slice_fusion), channel_id=1, source_target_pairs={{0,6},{1,7},{2,4},{3,5},{4,2},{5,3},{6,0},{7,1},{8,14},{9,15},{10,... | collective-permute-start | bytes 6152 | tf_op jit(solution)/shard_map/ppermute | solution.py:26
  30.8 0.5 collective-permute-start.9
  31.6 2.3 %collective-permute-done.11 = f32[32,16]{0,1:T(8,128)S(1)} collective-permute-done((f32[32,16]{0,1:T(8,128)S(1)}, f32[32,16]{0,1:T(8,128)S(1)}, u32[]{:S(2)}, u32[]{:S(2)}) %collective-permute-start.11) | collective-permute-done | bytes 2080 | tf_op jit(solution)/shard_map/ppermute | solution.py:26
  33.9 0.5 collective-permute-done.9
  34.5 0.4 fusion.21
  35.0 1.2 collective-permute-start.6
  36.2 1.6 %collective-permute-start.7 = (bf16[8,8192]{1,0:T(8,128)(2,1)S(1)}, bf16[8,8192]{1,0:T(8,128)(2,1)S(1)}, u32[]{:S(2)}, u32[]{:S(2)}) collective-permute-start(bf16[8,8192]{1,0:T(8,128)(2,1)S(1)} %bitcast.162), channel_id=1, source_target_pairs={{0,16},{8,24},{16,0},{24,8},{1,17},{9,25},{17,1},{25,9},{2,18},{10... | collective-permute-start | bytes 393224 | tf_op jit(solution)/shard_map/ppermute | solution.py:22
  37.9 1.1 collective-permute-start.8
  39.8 5.9 %shard_map.125.refs_4_ = bf16[8192,1024]{1,0:T(8,128)(2,1)S(1)} custom-call(bf16[8192,1024]{1,0:T(8,128)(2,1)} %source_ref.1), custom_call_target="tpu_custom_call" | custom-call | bytes 33554432 | tf_op jit(solution)/shard_map/pallas_call | solution.py:133
  45.7 2.9 %collective-permute-done.7.refs_2_ = bf16[8,8192]{1,0:T(8,128)(2,1)S(1)} collective-permute-done((bf16[8,8192]{1,0:T(8,128)(2,1)S(1)}, bf16[8,8192]{1,0:T(8,128)(2,1)S(1)}, u32[]{:S(2)}, u32[]{:S(2)}) %collective-permute-start.7) | collective-permute-done | bytes 131104 | tf_op jit(solution)/shard_map/ppermute | solution.py:22
  48.5 3.1 %shard_map.126 = (bf16[32,1024]{1,0:T(8,128)(2,1)S(1)}, bf16[32,1152]{1,0:T(8,128)(2,1)S(1)}) custom-call(s32[1]{0:T(128)} %bitcast.place_ref, bf16[8,8192]{1,0:T(8,128)(2,1)S(1)} %bitcast.164, bf16[8,8192]{1,0:T(8,128)(2,1)S(1)} %collective-permute-done.6.refs_1_, bf16[8,8192]{1,0:T(8,128)(2,1)S(1)} %collective-permute-done.7.refs_2_, ...), custom_call_target="tpu_custom_call" | custom-call | flops 536870912 | bytes 16777216 | tf_op jit(solution)/shard_map/pallas_call | solution.py:214
  51.6 0.9 collective-permute-start.13
  52.6 1.0 collective-permute-start.14
  53.6 1.5 %collective-permute-start.15 = (bf16[32,1152]{1,0:T(8,128)(2,1)S(1)}, bf16[32,1152]{1,0:T(8,128)(2,1)S(1)}, u32[]{:S(2)}, u32[]{:S(2)}) collective-permute-start(bf16[32,1152]{1,0:T(8,128)(2,1)S(1)} %get-tuple-element.45), channel_id=1, source_target_pairs={{0,6},{1,7},{2,4},{3,5},{4,2},{5,3},{6,0},{7,1},{8,14},{9,15},{10,... | collective-permute-start | bytes 221192 | tf_op jit(solution)/shard_map/ppermute | solution.py:26
  55.1 0.9 collective-permute-done.13
  56.1 1.3 collective-permute-done.14
  57.4 1.5 %collective-permute-done.15 = bf16[32,1152]{1,0:T(8,128)(2,1)S(1)} collective-permute-done((bf16[32,1152]{1,0:T(8,128)(2,1)S(1)}, bf16[32,1152]{1,0:T(8,128)(2,1)S(1)}, u32[]{:S(2)}, u32[]{:S(2)}) %collective-permute-start.15) | collective-permute-done | bytes 73760 | tf_op jit(solution)/shard_map/ppermute | solution.py:26
  59.1 1.5 %collective-permute-done.16.far_ref = bf16[128,1152]{1,0:T(8,128)(2,1)S(1)} collective-permute-done((bf16[128,1152]{1,0:T(8,128)(2,1)S(1)}, bf16[128,1152]{1,0:T(8,128)(2,1)S(1)}, u32[]{:S(2)}, u32[]{:S(2)}) %collective-permute-start.16) | collective-permute-done | bytes 294944 | tf_op jit(solution)/shard_map/ppermute | solution.py:26
  60.7 3.6 %shard_map.129 = (bf16[104,768]{1,0:T(8,128)(2,1)S(1)}, bf16[104,768]{1,0:T(8,128)(2,1)S(1)}, bf16[2,104,768]{2,1,0:T(8,128)(2,1)S(1)}) custom-call(s32[1]{0:T(128)} %bitcast.place_ref, bf16[104,256]{1,0:T(8,128)(2,1)S(1)} %get-tuple-element.80.pick_ref, bf16[128,1152]{1,0:T(8,128)(2,1)S(1)} %constant_dynamic-update-slice_fusion.2.near_ref, ...), custom_call_target="tpu_custom_call" | custom-call | flops 654311424 | bytes 6291456 | tf_op jit(solution)/shard_map/pallas_call | solution.py:288
  64.3 3.4 %collective-permute-start.25 = (bf16[2,104,768]{2,1,0:T(8,128)(2,1)S(1)}, bf16[2,104,768]{2,1,0:T(8,128)(2,1)S(1)}, u32[]{:S(2)}, u32[]{:S(2)}) collective-permute-start(bf16[2,104,768]{2,1,0:T(8,128)(2,1)S(1)} %get-tuple-element.56), channel_id=1, source_target_pairs={{0,8},{8,0},{16,24},{24,16},{1,9},{9,1},{17,25},{25,17},{2,10},{10... | collective-permute-start | bytes 958472 | tf_op jit(solution)/shard_map/ppermute | solution.py:26
  67.6 3.6 %shard_map.127 = (bf16[112,768]{1,0:T(8,128)(2,1)S(1)}, bf16[112,768]{1,0:T(8,128)(2,1)S(1)}, bf16[2,112,768]{2,1,0:T(8,128)(2,1)S(1)}) custom-call(s32[1]{0:T(128)} %bitcast.place_ref, bf16[104,256]{1,0:T(8,128)(2,1)S(1)} %get-tuple-element.82.pick_ref, bf16[128,1152]{1,0:T(8,128)(2,1)S(1)} %constant_dynamic-update-slice_fusion.2.near_ref, ...), custom_call_target="tpu_custom_call" | custom-call | flops 654311424 | bytes 6291456 | tf_op jit(solution)/shard_map/pallas_call | solution.py:288
  71.3 3.6 %shard_map.128 = (bf16[104,768]{1,0:T(8,128)(2,1)S(1)}, bf16[104,768]{1,0:T(8,128)(2,1)S(1)}, bf16[2,104,768]{2,1,0:T(8,128)(2,1)S(1)}) custom-call(s32[1]{0:T(128)} %bitcast.place_ref, bf16[104,256]{1,0:T(8,128)(2,1)S(1)} %get-tuple-element.81.pick_ref, bf16[128,1152]{1,0:T(8,128)(2,1)S(1)} %constant_dynamic-update-slice_fusion.2.near_ref, ...), custom_call_target="tpu_custom_call" | custom-call | flops 654311424 | bytes 6291456 | tf_op jit(solution)/shard_map/pallas_call | solution.py:288
  74.9 2.1 %collective-permute-start.21 = (bf16[2,104,768]{2,1,0:T(8,128)(2,1)S(1)}, bf16[2,104,768]{2,1,0:T(8,128)(2,1)S(1)}, u32[]{:S(2)}, u32[]{:S(2)}) collective-permute-start(bf16[2,104,768]{2,1,0:T(8,128)(2,1)S(1)} %get-tuple-element.52), channel_id=1, source_target_pairs={{0,8},{8,0},{16,24},{24,16},{1,9},{9,1},{17,25},{25,17},{2,10},{10... | collective-permute-start | bytes 958472 | tf_op jit(solution)/shard_map/ppermute | solution.py:26
  77.4 9.3 %collective-permute-done.17 = bf16[2,112,768]{2,1,0:T(8,128)(2,1)S(1)} collective-permute-done((bf16[2,112,768]{2,1,0:T(8,128)(2,1)S(1)}, bf16[2,112,768]{2,1,0:T(8,128)(2,1)S(1)}, u32[]{:S(2)}, u32[]{:S(2)}) %collective-permute-start.17) | collective-permute-done | bytes 344096 | tf_op jit(solution)/shard_map/ppermute | solution.py:26
  86.9 6.9 %collective-permute-done.21 = bf16[2,104,768]{2,1,0:T(8,128)(2,1)S(1)} collective-permute-done((bf16[2,104,768]{2,1,0:T(8,128)(2,1)S(1)}, bf16[2,104,768]{2,1,0:T(8,128)(2,1)S(1)}, u32[]{:S(2)}, u32[]{:S(2)}) %collective-permute-start.21) | collective-permute-done | bytes 319520 | tf_op jit(solution)/shard_map/ppermute | solution.py:26
  93.8 6.2 %collective-permute-done.18 = bf16[1,112,768]{2,1,0:T(8,128)(2,1)S(1)} collective-permute-done((bf16[1,112,768]{2,1,0:T(8,128)(2,1)S(1)}, bf16[1,112,768]{2,1,0:T(8,128)(2,1)S(1)}, u32[]{:S(2)}, u32[]{:S(2)}) %collective-permute-start.18) | collective-permute-done | bytes 172064 | tf_op jit(solution)/shard_map/ppermute | solution.py:26
  100.7 3.0 %collective-permute-start.22 = (bf16[1,104,768]{2,1,0:T(8,128)(2,1)S(1)}, bf16[1,104,768]{2,1,0:T(8,128)(2,1)S(1)}, u32[]{:S(2)}, u32[]{:S(2)}) collective-permute-start(bf16[1,104,768]{2,1,0:T(8,128)(2,1)S(1)} %fusion.9), channel_id=1, source_target_pairs={{0,16},{8,24},{16,0},{24,8},{1,17},{9,25},{17,1},{25,9},{2,18},{10... | collective-permute-start | bytes 479240 | tf_op jit(solution)/shard_map/ppermute | solution.py:26
  103.9 3.6 %collective-permute-done.27 = bf16[1,104,384]{2,1,0:T(8,128)(2,1)S(1)} collective-permute-done((bf16[1,104,384]{2,1,0:T(8,128)(2,1)S(1)}, bf16[1,104,384]{2,1,0:T(8,128)(2,1)S(1)}, u32[]{:S(2)}, u32[]{:S(2)}) %collective-permute-start.27) | collective-permute-done | bytes 79904 | tf_op jit(solution)/shard_map/ppermute | solution.py:26
  107.5 3.2 %collective-permute-start.28 = (bf16[2,104,384]{2,1,0:T(8,128)(2,1)S(1)}, bf16[2,104,384]{2,1,0:T(8,128)(2,1)S(1)}, u32[]{:S(2)}, u32[]{:S(2)}) collective-permute-start(bf16[2,104,384]{2,1,0:T(8,128)(2,1)S(1)} %pad_maximum_fusion.2.refs_4_), channel_id=1, source_target_pairs={{0,8},{8,0},{16,24},{24,16},{1,9},{9,1},{17,25},{25,17},{2,10},{10... | collective-permute-start | bytes 479240 | tf_op jit(solution)/shard_map/ppermute | solution.py:26
  110.7 3.7 %collective-permute-done.22 = bf16[1,104,768]{2,1,0:T(8,128)(2,1)S(1)} collective-permute-done((bf16[1,104,768]{2,1,0:T(8,128)(2,1)S(1)}, bf16[1,104,768]{2,1,0:T(8,128)(2,1)S(1)}, u32[]{:S(2)}, u32[]{:S(2)}) %collective-permute-start.22) | collective-permute-done | bytes 159776 | tf_op jit(solution)/shard_map/ppermute | solution.py:26
  114.5 0.4 collective-permute-start.23
  115.0 1.0 collective-permute-done.19
  116.0 1.8 %collective-permute-start.20 = (bf16[2,104,384]{2,1,0:T(8,128)(2,1)S(1)}, bf16[2,104,384]{2,1,0:T(8,128)(2,1)S(1)}, u32[]{:S(2)}, u32[]{:S(2)}) collective-permute-start(bf16[2,104,384]{2,1,0:T(8,128)(2,1)S(1)} %pad_maximum_fusion.refs_0_), channel_id=1, source_target_pairs={{0,8},{8,0},{16,24},{24,16},{1,9},{9,1},{17,25},{25,17},{2,10},{10... | collective-permute-start | bytes 479240 | tf_op jit(solution)/shard_map/ppermute | solution.py:26
  117.8 3.0 %collective-permute-done.23 = bf16[1,104,384]{2,1,0:T(8,128)(2,1)S(1)} collective-permute-done((bf16[1,104,384]{2,1,0:T(8,128)(2,1)S(1)}, bf16[1,104,384]{2,1,0:T(8,128)(2,1)S(1)}, u32[]{:S(2)}, u32[]{:S(2)}) %collective-permute-start.23) | collective-permute-done | bytes 79904 | tf_op jit(solution)/shard_map/ppermute | solution.py:26
  120.9 0.5 collective-permute-start.24
  121.4 3.8 %shard_map.130.refs_7_ = bf16[3,1536,1024]{2,1,0:T(8,128)(2,1)S(1)} custom-call(bf16[3,1536,1024]{2,1,0:T(8,128)(2,1)} %source_ref.2), custom_call_target="tpu_custom_call" | custom-call | bytes 18874368 | tf_op jit(solution)/shard_map/pallas_call | solution.py:133
  125.2 1.0 collective-permute-done.24.refs_3_
  126.2 2.3 %shard_map.131 = (f32[128,1024]{1,0:T(8,128)S(1)}, bf16[128,1024]{1,0:T(8,128)(2,1)S(1)}) custom-call(s32[1]{0:T(128)} %bitcast.place_ref, bf16[2,104,384]{2,1,0:T(8,128)(2,1)S(1)} %pad_maximum_fusion.refs_0_, bf16[2,104,384]{2,1,0:T(8,128)(2,1)S(1)} %collective-permute-done.20.refs_1_, bf16[2,104,384]{2,1,0:T(8,128)(2,1)S(1)} %pad_maximum_fusion.1.refs_2_, ...), custom_call_target="tpu_custom_call" | custom-call | flops 981467136 | bytes 9437184 | tf_op jit(solution)/shard_map/pallas_call | solution.py:384
  128.6 1.5 %collective-permute-done.29 = bf16[4,32,1024]{2,1,0:T(8,128)(2,1)S(1)} collective-permute-done((bf16[4,32,1024]{2,1,0:T(8,128)(2,1)S(1)}, bf16[4,32,1024]{2,1,0:T(8,128)(2,1)S(1)}, u32[]{:S(2)}, u32[]{:S(2)}) %collective-permute-start.29) | collective-permute-done | bytes 262176 | tf_op jit(solution)/shard_map/ppermute | solution.py:26
  130.2 1.5 %collective-permute-start.30 = (bf16[32,1024]{1,0:T(8,128)(2,1)S(1)}, bf16[32,1024]{1,0:T(8,128)(2,1)S(1)}, u32[]{:S(2)}, u32[]{:S(2)}) collective-permute-start(bf16[32,1024]{1,0:T(8,128)(2,1)S(1)} %get-tuple-element.77), channel_id=1, source_target_pairs={{0,2},{1,3},{2,0},{3,1},{4,6},{5,7},{6,4},{7,5},{8,10},{9,11},{10,... | collective-permute-start | bytes 196616 | tf_op jit(solution)/shard_map/ppermute | solution.py:26
  131.7 0.5 collective-permute-start.31
  132.2 1.6 %collective-permute-start.32 = (bf16[32,1024]{1,0:T(8,128)(2,1)S(1)}, bf16[32,1024]{1,0:T(8,128)(2,1)S(1)}, u32[]{:S(2)}, u32[]{:S(2)}) collective-permute-start(bf16[32,1024]{1,0:T(8,128)(2,1)S(1)} %get-tuple-element.78), channel_id=1, source_target_pairs={{0,6},{1,7},{2,4},{3,5},{4,2},{5,3},{6,0},{7,1},{8,14},{9,15},{10,... | collective-permute-start | bytes 196616 | tf_op jit(solution)/shard_map/ppermute | solution.py:26
  133.8 0.7 copy.48
  134.6 2.1 %collective-permute-done.31 = bf16[32,1024]{1,0:T(8,128)(2,1)S(1)} collective-permute-done((bf16[32,1024]{1,0:T(8,128)(2,1)S(1)}, bf16[32,1024]{1,0:T(8,128)(2,1)S(1)}, u32[]{:S(2)}, u32[]{:S(2)}) %collective-permute-start.31) | collective-permute-done | bytes 65568 | tf_op jit(solution)/shard_map/ppermute | solution.py:26
  136.7 0.7 collective-permute-done.32
  137.4 0.7 copy.38
  (87 shorter events, 3.7 us)
Async XLA Ops:
  1.6 11.9 %collective-permute-start = (bf16[8,64,128]{2,1,0:T(8,128)(2,1)S(1)}, bf16[8,64,128]{2,1,0:T(8,128)(2,1)S(1)}, u32[]{:S(2)}, u32[]{:S(2)}) collective-permute-start(bf16[8,64,128]{2,1,0:T(8,128)(2,1)S(1)} %bitcast.167), channel_id=1, source_target_pairs={{0,8},{8,16},{16,24},{24,0},{1,9},{9,17},{17,25},{25,1},{2,10},{10... | collective-permute-start | bytes 393224 | tf_op jit(solution)/shard_map/ppermute | solution.py:22
  4.6 11.2 %collective-permute-start.1 = (bf16[8,64,128]{2,1,0:T(8,128)(2,1)S(1)}, bf16[8,64,128]{2,1,0:T(8,128)(2,1)S(1)}, u32[]{:S(2)}, u32[]{:S(2)}) collective-permute-start(bf16[8,64,128]{2,1,0:T(8,128)(2,1)S(1)} %bitcast.168), channel_id=1, source_target_pairs={{0,16},{8,24},{16,0},{24,8},{1,17},{9,25},{17,1},{25,9},{2,18},{10... | collective-permute-start | bytes 393224 | tf_op jit(solution)/shard_map/ppermute | solution.py:22
  7.2 8.6 %collective-permute-start.2 = (bf16[8,64,128]{2,1,0:T(8,128)(2,1)S(1)}, bf16[8,64,128]{2,1,0:T(8,128)(2,1)S(1)}, u32[]{:S(2)}, u32[]{:S(2)}) collective-permute-start(bf16[8,64,128]{2,1,0:T(8,128)(2,1)S(1)} %bitcast.169), channel_id=1, source_target_pairs={{0,24},{8,0},{16,8},{24,16},{1,25},{9,1},{17,9},{25,17},{2,26},{10... | collective-permute-start | bytes 393224 | tf_op jit(solution)/shard_map/ppermute | solution.py:22
  8.6 1.0 copy-start
  9.6 0.7 copy-start.2
  17.2 8.9 %collective-permute-start.5 = (bf16[9,64,128]{2,1,0:T(8,128)(2,1)S(1)}, bf16[9,64,128]{2,1,0:T(8,128)(2,1)S(1)}, u32[]{:S(2)}, u32[]{:S(2)}) collective-permute-start(bf16[9,64,128]{2,1,0:T(8,128)(2,1)S(1)} %get-tuple-element.38), channel_id=1, source_target_pairs={{0,8},{8,16},{16,24},{24,0},{1,9},{9,17},{17,25},{25,1},{2,10},{10... | collective-permute-start | bytes 442376 | tf_op jit(solution)/shard_map/ppermute | solution.py:22
  20.5 10.8 %collective-permute-start.4 = (bf16[9,64,128]{2,1,0:T(8,128)(2,1)S(1)}, bf16[9,64,128]{2,1,0:T(8,128)(2,1)S(1)}, u32[]{:S(2)}, u32[]{:S(2)}) collective-permute-start(bf16[9,64,128]{2,1,0:T(8,128)(2,1)S(1)} %get-tuple-element.37), channel_id=1, source_target_pairs={{0,16},{8,24},{16,0},{24,8},{1,17},{9,25},{17,1},{25,9},{2,18},{10... | collective-permute-start | bytes 442376 | tf_op jit(solution)/shard_map/ppermute | solution.py:22
  22.1 9.2 %collective-permute-start.3 = (bf16[9,64,128]{2,1,0:T(8,128)(2,1)S(1)}, bf16[9,64,128]{2,1,0:T(8,128)(2,1)S(1)}, u32[]{:S(2)}, u32[]{:S(2)}) collective-permute-start(bf16[9,64,128]{2,1,0:T(8,128)(2,1)S(1)} %get-tuple-element.36), channel_id=1, source_target_pairs={{0,24},{8,0},{16,8},{24,16},{1,25},{9,1},{17,9},{25,17},{2,26},{10... | collective-permute-start | bytes 442376 | tf_op jit(solution)/shard_map/ppermute | solution.py:22
  27.8 3.7 %collective-permute-start.10 = (f32[32,16]{0,1:T(8,128)S(1)}, f32[32,16]{0,1:T(8,128)S(1)}, u32[]{:S(2)}, u32[]{:S(2)}) collective-permute-start(f32[32,16]{0,1:T(8,128)S(1)} %constant_dynamic-update-slice_fusion), channel_id=1, source_target_pairs={{0,4},{1,5},{2,6},{3,7},{4,0},{5,1},{6,2},{7,3},{8,12},{9,13},{10,... | collective-permute-start | bytes 6152 | tf_op jit(solution)/shard_map/ppermute | solution.py:26
  29.3 4.5 %collective-permute-start.11 = (f32[32,16]{0,1:T(8,128)S(1)}, f32[32,16]{0,1:T(8,128)S(1)}, u32[]{:S(2)}, u32[]{:S(2)}) collective-permute-start(f32[32,16]{0,1:T(8,128)S(1)} %constant_dynamic-update-slice_fusion), channel_id=1, source_target_pairs={{0,6},{1,7},{2,4},{3,5},{4,2},{5,3},{6,0},{7,1},{8,14},{9,15},{10,... | collective-permute-start | bytes 6152 | tf_op jit(solution)/shard_map/ppermute | solution.py:26
  30.8 3.7 %collective-permute-start.9 = (f32[32,16]{0,1:T(8,128)S(1)}, f32[32,16]{0,1:T(8,128)S(1)}, u32[]{:S(2)}, u32[]{:S(2)}) collective-permute-start(f32[32,16]{0,1:T(8,128)S(1)} %constant_dynamic-update-slice_fusion), channel_id=1, source_target_pairs={{0,2},{1,3},{2,0},{3,1},{4,6},{5,7},{6,4},{7,5},{8,10},{9,11},{10,... | collective-permute-start | bytes 6152 | tf_op jit(solution)/shard_map/ppermute | solution.py:26
  34.5 4.5 %collective-permute-start.12 = (f32[128,16]{0,1:T(8,128)S(1)}, f32[128,16]{0,1:T(8,128)S(1)}, u32[]{:S(2)}, u32[]{:S(2)}) collective-permute-start(f32[128,16]{0,1:T(8,128)S(1)} %pad_maximum_fusion.3), channel_id=1, source_target_pairs={{0,1},{1,0},{2,3},{3,2},{4,5},{5,4},{6,7},{7,6},{8,9},{9,8},{10,11... | collective-permute-start | bytes 24584 | tf_op jit(solution)/shard_map/ppermute | solution.py:26
  35.0 10.6 %collective-permute-start.6 = (bf16[8,8192]{1,0:T(8,128)(2,1)S(1)}, bf16[8,8192]{1,0:T(8,128)(2,1)S(1)}, u32[]{:S(2)}, u32[]{:S(2)}) collective-permute-start(bf16[8,8192]{1,0:T(8,128)(2,1)S(1)} %bitcast.161), channel_id=1, source_target_pairs={{0,8},{8,16},{16,24},{24,0},{1,9},{9,17},{17,25},{25,1},{2,10},{10... | collective-permute-start | bytes 393224 | tf_op jit(solution)/shard_map/ppermute | solution.py:22
  36.2 12.3 %collective-permute-start.7 = (bf16[8,8192]{1,0:T(8,128)(2,1)S(1)}, bf16[8,8192]{1,0:T(8,128)(2,1)S(1)}, u32[]{:S(2)}, u32[]{:S(2)}) collective-permute-start(bf16[8,8192]{1,0:T(8,128)(2,1)S(1)} %bitcast.162), channel_id=1, source_target_pairs={{0,16},{8,24},{16,0},{24,8},{1,17},{9,25},{17,1},{25,9},{2,18},{10... | collective-permute-start | bytes 393224 | tf_op jit(solution)/shard_map/ppermute | solution.py:22
  37.9 10.7 %collective-permute-start.8 = (bf16[8,8192]{1,0:T(8,128)(2,1)S(1)}, bf16[8,8192]{1,0:T(8,128)(2,1)S(1)}, u32[]{:S(2)}, u32[]{:S(2)}) collective-permute-start(bf16[8,8192]{1,0:T(8,128)(2,1)S(1)} %bitcast.163), channel_id=1, source_target_pairs={{0,24},{8,0},{16,8},{24,16},{1,25},{9,1},{17,9},{25,17},{2,26},{10... | collective-permute-start | bytes 393224 | tf_op jit(solution)/shard_map/ppermute | solution.py:22
  39.7 8.8 %copy-start.1 = (f32[1024]{0:T(1024)S(1)}, f32[1024]{0:T(1024)}, u32[]{:S(2)}) copy-start(f32[1024]{0:T(1024)} %param.17) | copy-start | bytes 12292
  51.6 4.4 %collective-permute-start.13 = (bf16[32,1152]{1,0:T(8,128)(2,1)S(1)}, bf16[32,1152]{1,0:T(8,128)(2,1)S(1)}, u32[]{:S(2)}, u32[]{:S(2)}) collective-permute-start(bf16[32,1152]{1,0:T(8,128)(2,1)S(1)} %get-tuple-element.45), channel_id=1, source_target_pairs={{0,2},{1,3},{2,0},{3,1},{4,6},{5,7},{6,4},{7,5},{8,10},{9,11},{10,... | collective-permute-start | bytes 221192 | tf_op jit(solution)/shard_map/ppermute | solution.py:26
  52.6 4.8 %collective-permute-start.14 = (bf16[32,1152]{1,0:T(8,128)(2,1)S(1)}, bf16[32,1152]{1,0:T(8,128)(2,1)S(1)}, u32[]{:S(2)}, u32[]{:S(2)}) collective-permute-start(bf16[32,1152]{1,0:T(8,128)(2,1)S(1)} %get-tuple-element.45), channel_id=1, source_target_pairs={{0,4},{1,5},{2,6},{3,7},{4,0},{5,1},{6,2},{7,3},{8,12},{9,13},{10,... | collective-permute-start | bytes 221192 | tf_op jit(solution)/shard_map/ppermute | solution.py:26
  53.6 5.3 %collective-permute-start.15 = (bf16[32,1152]{1,0:T(8,128)(2,1)S(1)}, bf16[32,1152]{1,0:T(8,128)(2,1)S(1)}, u32[]{:S(2)}, u32[]{:S(2)}) collective-permute-start(bf16[32,1152]{1,0:T(8,128)(2,1)S(1)} %get-tuple-element.45), channel_id=1, source_target_pairs={{0,6},{1,7},{2,4},{3,5},{4,2},{5,3},{6,0},{7,1},{8,14},{9,15},{10,... | collective-permute-start | bytes 221192 | tf_op jit(solution)/shard_map/ppermute | solution.py:26
  58.9 1.6 %collective-permute-start.16 = (bf16[128,1152]{1,0:T(8,128)(2,1)S(1)}, bf16[128,1152]{1,0:T(8,128)(2,1)S(1)}, u32[]{:S(2)}, u32[]{:S(2)}) collective-permute-start(bf16[128,1152]{1,0:T(8,128)(2,1)S(1)} %constant_dynamic-update-slice_fusion.2.near_ref), channel_id=1, source_target_pairs={{0,1},{1,0},{2,3},{3,2},{4,5},{5,4},{6,7},{7,6},{8,9},{9,8},{10,11... | collective-permute-start | bytes 884744 | tf_op jit(solution)/shard_map/ppermute | solution.py:26
  64.3 12.7 %collective-permute-start.25 = (bf16[2,104,768]{2,1,0:T(8,128)(2,1)S(1)}, bf16[2,104,768]{2,1,0:T(8,128)(2,1)S(1)}, u32[]{:S(2)}, u32[]{:S(2)}) collective-permute-start(bf16[2,104,768]{2,1,0:T(8,128)(2,1)S(1)} %get-tuple-element.56), channel_id=1, source_target_pairs={{0,8},{8,0},{16,24},{24,16},{1,9},{9,1},{17,25},{25,17},{2,10},{10... | collective-permute-start | bytes 958472 | tf_op jit(solution)/shard_map/ppermute | solution.py:26
  71.2 15.5 %collective-permute-start.17 = (bf16[2,112,768]{2,1,0:T(8,128)(2,1)S(1)}, bf16[2,112,768]{2,1,0:T(8,128)(2,1)S(1)}, u32[]{:S(2)}, u32[]{:S(2)}) collective-permute-start(bf16[2,112,768]{2,1,0:T(8,128)(2,1)S(1)} %get-tuple-element.47), channel_id=1, source_target_pairs={{0,8},{8,0},{16,24},{24,16},{1,9},{9,1},{17,25},{25,17},{2,10},{10... | collective-permute-start | bytes 1032200 | tf_op jit(solution)/shard_map/ppermute | solution.py:26
  74.9 18.9 %collective-permute-start.21 = (bf16[2,104,768]{2,1,0:T(8,128)(2,1)S(1)}, bf16[2,104,768]{2,1,0:T(8,128)(2,1)S(1)}, u32[]{:S(2)}, u32[]{:S(2)}) collective-permute-start(bf16[2,104,768]{2,1,0:T(8,128)(2,1)S(1)} %get-tuple-element.52), channel_id=1, source_target_pairs={{0,8},{8,0},{16,24},{24,16},{1,9},{9,1},{17,25},{25,17},{2,10},{10... | collective-permute-start | bytes 958472 | tf_op jit(solution)/shard_map/ppermute | solution.py:26
  77.0 23.3 %collective-permute-start.26 = (bf16[1,104,768]{2,1,0:T(8,128)(2,1)S(1)}, bf16[1,104,768]{2,1,0:T(8,128)(2,1)S(1)}, u32[]{:S(2)}, u32[]{:S(2)}) collective-permute-start(bf16[1,104,768]{2,1,0:T(8,128)(2,1)S(1)} %fusion.10), channel_id=1, source_target_pairs={{0,16},{8,24},{16,0},{24,8},{1,17},{9,25},{17,1},{25,9},{2,18},{10... | collective-permute-start | bytes 479240 | tf_op jit(solution)/shard_map/ppermute | solution.py:26
  86.8 13.3 %collective-permute-start.18 = (bf16[1,112,768]{2,1,0:T(8,128)(2,1)S(1)}, bf16[1,112,768]{2,1,0:T(8,128)(2,1)S(1)}, u32[]{:S(2)}, u32[]{:S(2)}) collective-permute-start(bf16[1,112,768]{2,1,0:T(8,128)(2,1)S(1)} %fusion.7), channel_id=1, source_target_pairs={{0,16},{8,24},{16,0},{24,8},{1,17},{9,25},{17,1},{25,9},{2,18},{10... | collective-permute-start | bytes 516104 | tf_op jit(solution)/shard_map/ppermute | solution.py:26
  100.5 6.9 %collective-permute-start.27 = (bf16[1,104,384]{2,1,0:T(8,128)(2,1)S(1)}, bf16[1,104,384]{2,1,0:T(8,128)(2,1)S(1)}, u32[]{:S(2)}, u32[]{:S(2)}) collective-permute-start(bf16[1,104,384]{2,1,0:T(8,128)(2,1)S(1)} %fusion.23), channel_id=1, source_target_pairs={{0,16},{8,24},{16,0},{24,8},{1,17},{9,25},{17,1},{25,9},{2,18},{10... | collective-permute-start | bytes 239624 | tf_op jit(solution)/shard_map/ppermute | solution.py:26
  100.7 13.6 %collective-permute-start.22 = (bf16[1,104,768]{2,1,0:T(8,128)(2,1)S(1)}, bf16[1,104,768]{2,1,0:T(8,128)(2,1)S(1)}, u32[]{:S(2)}, u32[]{:S(2)}) collective-permute-start(bf16[1,104,768]{2,1,0:T(8,128)(2,1)S(1)} %fusion.9), channel_id=1, source_target_pairs={{0,16},{8,24},{16,0},{24,8},{1,17},{9,25},{17,1},{25,9},{2,18},{10... | collective-permute-start | bytes 479240 | tf_op jit(solution)/shard_map/ppermute | solution.py:26
  103.8 12.2 %collective-permute-start.19 = (bf16[1,104,384]{2,1,0:T(8,128)(2,1)S(1)}, bf16[1,104,384]{2,1,0:T(8,128)(2,1)S(1)}, u32[]{:S(2)}, u32[]{:S(2)}) collective-permute-start(bf16[1,104,384]{2,1,0:T(8,128)(2,1)S(1)} %fusion.53), channel_id=1, source_target_pairs={{0,16},{8,24},{16,0},{24,8},{1,17},{9,25},{17,1},{25,9},{2,18},{10... | collective-permute-start | bytes 239624 | tf_op jit(solution)/shard_map/ppermute | solution.py:26
  107.5 17.7 %collective-permute-start.28 = (bf16[2,104,384]{2,1,0:T(8,128)(2,1)S(1)}, bf16[2,104,384]{2,1,0:T(8,128)(2,1)S(1)}, u32[]{:S(2)}, u32[]{:S(2)}) collective-permute-start(bf16[2,104,384]{2,1,0:T(8,128)(2,1)S(1)} %pad_maximum_fusion.2.refs_4_), channel_id=1, source_target_pairs={{0,8},{8,0},{16,24},{24,16},{1,9},{9,1},{17,25},{25,17},{2,10},{10... | collective-permute-start | bytes 479240 | tf_op jit(solution)/shard_map/ppermute | solution.py:26
  114.5 6.3 %collective-permute-start.23 = (bf16[1,104,384]{2,1,0:T(8,128)(2,1)S(1)}, bf16[1,104,384]{2,1,0:T(8,128)(2,1)S(1)}, u32[]{:S(2)}, u32[]{:S(2)}) collective-permute-start(bf16[1,104,384]{2,1,0:T(8,128)(2,1)S(1)} %fusion.22), channel_id=1, source_target_pairs={{0,16},{8,24},{16,0},{24,8},{1,17},{9,25},{17,1},{25,9},{2,18},{10... | collective-permute-start | bytes 239624 | tf_op jit(solution)/shard_map/ppermute | solution.py:26
  116.0 9.2 %collective-permute-start.20 = (bf16[2,104,384]{2,1,0:T(8,128)(2,1)S(1)}, bf16[2,104,384]{2,1,0:T(8,128)(2,1)S(1)}, u32[]{:S(2)}, u32[]{:S(2)}) collective-permute-start(bf16[2,104,384]{2,1,0:T(8,128)(2,1)S(1)} %pad_maximum_fusion.refs_0_), channel_id=1, source_target_pairs={{0,8},{8,0},{16,24},{24,16},{1,9},{9,1},{17,25},{25,17},{2,10},{10... | collective-permute-start | bytes 479240 | tf_op jit(solution)/shard_map/ppermute | solution.py:26
  120.9 5.3 %collective-permute-start.24 = (bf16[2,104,384]{2,1,0:T(8,128)(2,1)S(1)}, bf16[2,104,384]{2,1,0:T(8,128)(2,1)S(1)}, u32[]{:S(2)}, u32[]{:S(2)}) collective-permute-start(bf16[2,104,384]{2,1,0:T(8,128)(2,1)S(1)} %pad_maximum_fusion.1.refs_2_), channel_id=1, source_target_pairs={{0,8},{8,0},{16,24},{24,16},{1,9},{9,1},{17,25},{25,17},{2,10},{10... | collective-permute-start | bytes 479240 | tf_op jit(solution)/shard_map/ppermute | solution.py:26
  128.5 1.6 %collective-permute-start.29 = (bf16[4,32,1024]{2,1,0:T(8,128)(2,1)S(1)}, bf16[4,32,1024]{2,1,0:T(8,128)(2,1)S(1)}, u32[]{:S(2)}, u32[]{:S(2)}) collective-permute-start(bf16[4,32,1024]{2,1,0:T(8,128)(2,1)S(1)} %bitcast.176), channel_id=1, source_target_pairs={{0,1},{1,0},{2,3},{3,2},{4,5},{5,4},{6,7},{7,6},{8,9},{9,8},{10,11... | collective-permute-start | bytes 786440 | tf_op jit(solution)/shard_map/ppermute | solution.py:26
  130.2 4.3 %collective-permute-start.30 = (bf16[32,1024]{1,0:T(8,128)(2,1)S(1)}, bf16[32,1024]{1,0:T(8,128)(2,1)S(1)}, u32[]{:S(2)}, u32[]{:S(2)}) collective-permute-start(bf16[32,1024]{1,0:T(8,128)(2,1)S(1)} %get-tuple-element.77), channel_id=1, source_target_pairs={{0,2},{1,3},{2,0},{3,1},{4,6},{5,7},{6,4},{7,5},{8,10},{9,11},{10,... | collective-permute-start | bytes 196616 | tf_op jit(solution)/shard_map/ppermute | solution.py:26
  131.7 5.0 %collective-permute-start.31 = (bf16[32,1024]{1,0:T(8,128)(2,1)S(1)}, bf16[32,1024]{1,0:T(8,128)(2,1)S(1)}, u32[]{:S(2)}, u32[]{:S(2)}) collective-permute-start(bf16[32,1024]{1,0:T(8,128)(2,1)S(1)} %get-tuple-element.79), channel_id=1, source_target_pairs={{0,4},{1,5},{2,6},{3,7},{4,0},{5,1},{6,2},{7,3},{8,12},{9,13},{10,... | collective-permute-start | bytes 196616 | tf_op jit(solution)/shard_map/ppermute | solution.py:26
  132.2 5.2 %collective-permute-start.32 = (bf16[32,1024]{1,0:T(8,128)(2,1)S(1)}, bf16[32,1024]{1,0:T(8,128)(2,1)S(1)}, u32[]{:S(2)}, u32[]{:S(2)}) collective-permute-start(bf16[32,1024]{1,0:T(8,128)(2,1)S(1)} %get-tuple-element.78), channel_id=1, source_target_pairs={{0,6},{1,7},{2,4},{3,5},{4,2},{5,3},{6,0},{7,1},{8,14},{9,15},{10,... | collective-permute-start | bytes 196616 | tf_op jit(solution)/shard_map/ppermute | solution.py:26

commit v6 on v5

--- a/solution.py
+++ b/solution.py
@@ -260,6 +260,63 @@
             if out_ref.shape[0] > slots:
                 share = jnp.concatenate([share, extra_ref[:, columns]], axis=0)
             out_ref[:, columns] = share.astype(jnp.bfloat16)
+
+
+def held_gate_kernel(features, place_ref, pick_ref, near_ref, far_ref, weight_ref, *out_refs):
+    keep_refs, give_ref = out_refs[:-1], out_refs[-1]
+    half = near_ref.shape[0]
+    samples = 2 * len(keep_refs)
+    hidden = weight_ref.shape[1] // 2
+    part = hidden // samples
+    pick = pick_ref[...]
+    chosen = jnp.dot(
+        pick[:, :half], near_ref[:, :features], preferred_element_type=jnp.float32
+    ) + jnp.dot(pick[:, half:], far_ref[:, :features], preferred_element_type=jnp.float32)
+    chosen = chosen.astype(jnp.bfloat16)
+    for m in range(samples):
+        out_ref = give_ref.at[m // 2] if m % 2 else keep_refs[m // 2]
+        column = lax.bitwise_xor(place_ref[0], m) * part
+        for side in range(2):
+            columns = pl.ds(pl.multiple_of(side * hidden + column, HDIM), part)
+            out_ref[:, side * part : (side + 1) * part] = jnp.dot(
+                chosen, weight_ref[:, columns], preferred_element_type=jnp.float32
+            ).astype(jnp.bfloat16)
+
+
+def held_gate_up_parts(pick, near, far, weights, place, samples):
+    slots = pick.shape[0]
+    features, wide = weights.shape
+    part = wide // 2 // samples
+    one = jax.ShapeDtypeStruct((slots, 2 * part), jnp.bfloat16)
+    results = pl.pallas_call(
+        functools.partial(held_gate_kernel, features),
+        out_shape=[one] * (samples // 2)
+        + [jax.ShapeDtypeStruct((samples // 2, slots, 2 * part), jnp.bfloat16)],
+        in_specs=[SMEM_SPEC] + [VMEM_SPEC] * 4,
+        out_specs=[VMEM_SPEC] * (samples // 2 + 1),
+        compiler_params=pltpu.CompilerParams(vmem_limit_bytes=SCOPED),
+        cost_estimate=pl.CostEstimate(
+            flops=2 * slots * features * wide, bytes_accessed=2 * features * wide, transcendentals=0
+        ),
+    )(place, pick, near, far, weights)
+    return list(results[:-1]), results[-1]
+
+
+def fetch_one(array, index):
+    def kernel(source_ref, target_ref, sem):
+        copy = pltpu.make_async_copy(source_ref.at[index], target_ref, sem)
+        copy.start()
+        copy.wait()
+
+    return pl.pallas_call(
+        kernel,
+        out_shape=jax.ShapeDtypeStruct(array.shape[1:], array.dtype),
+        in_specs=[ANY_SPEC],
+        out_specs=VMEM_SPEC,
+        scratch_shapes=[pltpu.SemaphoreType.DMA],
+        compiler_params=pltpu.CompilerParams(vmem_limit_bytes=MIB),
+        cost_estimate=pl.CostEstimate(flops=0, bytes_accessed=4 * array[0].size, transcendentals=0),
+    )(in_hbm(array))
 
 
 def gate_up_parts(pick, near, far, extra, weights, expert, place, samples):
@@ -492,7 +549,12 @@
     extra = jnp.pad(square, (0, extra_rows * 2 * part - square.size)).reshape(extra_rows, 2 * part)
     sums = {}
     for j in reversed(range(per_owner)):
-        keep, give = gate_up_parts(pick[j], near, far, extra, w_gate_up, j, place, samples)
+        if j == 1 and part % HDIM == 0:
+            source, _ = lax.optimization_barrier((w_gate_up, row_block))
+            held = fetch_one(source, j)
+            keep, give = held_gate_up_parts(pick[j], near, far, held, place, samples)
+        else:
+            keep, give = gate_up_parts(pick[j], near, far, extra, w_gate_up, j, place, samples)
         arrived = swap(give, "sample", samples, 1)
         sums[j] = keep, arrived
     acts = [None] * (2 * per_owner)

time: 138 us -> 138 us (level)
    pallas_call x0 -> x2, Pallas kernels: none -> 4.18 us  [the longest x1 2.8 us: fetch_one(): pl.pallas_call(kernel, out_shape=jax.ShapeDtypeStruct(array.shape[1:], ar...]
    pallas_call x3 -> x2, Pallas kernels: 10.7 us -> 7.16 us  [gate_up_parts(): pl.pallas_call(functools.partial(gate_kernel, features, expert), out_shap...]
  transfers between devices with their start and end apart: 33 -> 33, of which waited for: 21 -> 20; matrix products, arithmetic and copies ran while one was open for 4% -> 4% of each run, Pallas kernels for 14% -> 14%
where the time goes in v6:
time: 138 us
  waiting for transfers between devices  55.3 us (40%)
  starting transfers between devices  42.1 us (31%)
  Pallas kernels  30 us (22%)
  local copies, waits for them, and re-layouts  6.58 us (5%)
  other arithmetic  2.87 us (2%)
    ppermute x24, waiting for transfers between devices, swap(): return lax.ppermute(array, axis, [(i, i ^ bits) for i in range(size)])  46.9 us
    ppermute x24, starting transfers between devices, swap(): return lax.ppermute(array, axis, [(i, i ^ bits) for i in range(size)])  25.4 us
    ppermute x9, starting transfers between devices, send(): lax.ppermute(array, axis, [(i, (i + shift) % size) for i in range(size)])  16.7 us
    pallas_call x3, Pallas kernels, fetch(): pl.pallas_call(fetch_kernel, out_shape=jax.ShapeDtypeStruct(array.shape,...  10.9 us
    ppermute x9, waiting for transfers between devices, send(): lax.ppermute(array, axis, [(i, (i + shift) % size) for i in range(size)])  8.37 us
    pallas_call x2, Pallas kernels, gate_up_parts(): pl.pallas_call(functools.partial(gate_kernel, features, expert), out_shap...  7.16 us
    unnamed x14, local copies, waits for them, and re-layouts  3.45 us
    pallas_call x1, Pallas kernels, project(): pl.pallas_call(functools.partial(project_kernel, samples, width), out_sha...  3.09 us
  transfers between devices with their start and end apart: 33, of which 20 were waited for; matrix products, arithmetic and copies ran while one was open for 4% of the time, Pallas kernels for 14%

profile of v6, /device:TPU:0, one launch (start us, length us, event | category | flops | bytes accessed | tf_op | source)
XLA Modules:
  0.0 138.0 jit_solution(3383986879669605410)
XLA Ops:
  0.6 0.9 copy.47
  1.6 3.1 %collective-permute-start = (bf16[8,64,128]{2,1,0:T(8,128)(2,1)S(1)}, bf16[8,64,128]{2,1,0:T(8,128)(2,1)S(1)}, u32[]{:S(2)}, u32[]{:S(2)}) collective-permute-start(bf16[8,64,128]{2,1,0:T(8,128)(2,1)S(1)} %bitcast.167), channel_id=1, source_target_pairs={{0,8},{8,16},{16,24},{24,0},{1,9},{9,17},{17,25},{25,1},{2,10},{10... | collective-permute-start | bytes 393224 | tf_op jit(solution)/shard_map/ppermute | solution.py:22
  4.6 2.6 %collective-permute-start.1 = (bf16[8,64,128]{2,1,0:T(8,128)(2,1)S(1)}, bf16[8,64,128]{2,1,0:T(8,128)(2,1)S(1)}, u32[]{:S(2)}, u32[]{:S(2)}) collective-permute-start(bf16[8,64,128]{2,1,0:T(8,128)(2,1)S(1)} %bitcast.168), channel_id=1, source_target_pairs={{0,16},{8,24},{16,0},{24,8},{1,17},{9,25},{17,1},{25,9},{2,18},{10... | collective-permute-start | bytes 393224 | tf_op jit(solution)/shard_map/ppermute | solution.py:22
  7.2 1.3 collective-permute-start.2
  8.6 1.0 copy-done
  9.6 0.7 copy-done.2
  10.3 1.1 shard_map.122
  11.3 1.2 shard_map.123.refs_4_
  12.6 0.9 copy.49
  13.5 2.4 %collective-permute-done.1.refs_2_ = bf16[8,64,128]{2,1,0:T(8,128)(2,1)S(1)} collective-permute-done((bf16[8,64,128]{2,1,0:T(8,128)(2,1)S(1)}, bf16[8,64,128]{2,1,0:T(8,128)(2,1)S(1)}, u32[]{:S(2)}, u32[]{:S(2)}) %collective-permute-start.1) | collective-permute-done | bytes 131104 | tf_op jit(solution)/shard_map/ppermute | solution.py:22
  15.9 1.3 shard_map.124
  17.2 3.3 %collective-permute-start.5 = (bf16[9,64,128]{2,1,0:T(8,128)(2,1)S(1)}, bf16[9,64,128]{2,1,0:T(8,128)(2,1)S(1)}, u32[]{:S(2)}, u32[]{:S(2)}) collective-permute-start(bf16[9,64,128]{2,1,0:T(8,128)(2,1)S(1)} %get-tuple-element.39), channel_id=1, source_target_pairs={{0,8},{8,16},{16,24},{24,0},{1,9},{9,17},{17,25},{25,1},{2,10},{10... | collective-permute-start | bytes 442376 | tf_op jit(solution)/shard_map/ppermute | solution.py:22
  20.5 1.6 %collective-permute-start.4 = (bf16[9,64,128]{2,1,0:T(8,128)(2,1)S(1)}, bf16[9,64,128]{2,1,0:T(8,128)(2,1)S(1)}, u32[]{:S(2)}, u32[]{:S(2)}) collective-permute-start(bf16[9,64,128]{2,1,0:T(8,128)(2,1)S(1)} %get-tuple-element.38), channel_id=1, source_target_pairs={{0,16},{8,24},{16,0},{24,8},{1,17},{9,25},{17,1},{25,9},{2,18},{10... | collective-permute-start | bytes 442376 | tf_op jit(solution)/shard_map/ppermute | solution.py:22
  22.1 0.8 collective-permute-start.3
  22.9 3.1 %collective-permute-done.5 = bf16[9,64,128]{2,1,0:T(8,128)(2,1)S(1)} collective-permute-done((bf16[9,64,128]{2,1,0:T(8,128)(2,1)S(1)}, bf16[9,64,128]{2,1,0:T(8,128)(2,1)S(1)}, u32[]{:S(2)}, u32[]{:S(2)}) %collective-permute-start.5) | collective-permute-done | bytes 147488 | tf_op jit(solution)/shard_map/ppermute | solution.py:22
  26.0 0.7 convert_bitcast_fusion
  26.9 0.8 copy.33
  27.8 1.5 %collective-permute-start.9 = (f32[32,16]{0,1:T(8,128)S(1)}, f32[32,16]{0,1:T(8,128)S(1)}, u32[]{:S(2)}, u32[]{:S(2)}) collective-permute-start(f32[32,16]{0,1:T(8,128)S(1)} %constant_dynamic-update-slice_fusion), channel_id=1, source_target_pairs={{0,2},{1,3},{2,0},{3,1},{4,6},{5,7},{6,4},{7,5},{8,10},{9,11},{10,... | collective-permute-start | bytes 6152 | tf_op jit(solution)/shard_map/ppermute | solution.py:26
  29.3 1.5 %collective-permute-start.10 = (f32[32,16]{0,1:T(8,128)S(1)}, f32[32,16]{0,1:T(8,128)S(1)}, u32[]{:S(2)}, u32[]{:S(2)}) collective-permute-start(f32[32,16]{0,1:T(8,128)S(1)} %constant_dynamic-update-slice_fusion), channel_id=1, source_target_pairs={{0,4},{1,5},{2,6},{3,7},{4,0},{5,1},{6,2},{7,3},{8,12},{9,13},{10,... | collective-permute-start | bytes 6152 | tf_op jit(solution)/shard_map/ppermute | solution.py:26
  30.8 0.5 collective-permute-start.11
  31.6 1.4 %collective-permute-done.10 = f32[32,16]{0,1:T(8,128)S(1)} collective-permute-done((f32[32,16]{0,1:T(8,128)S(1)}, f32[32,16]{0,1:T(8,128)S(1)}, u32[]{:S(2)}, u32[]{:S(2)}) %collective-permute-start.10) | collective-permute-done | bytes 2080 | tf_op jit(solution)/shard_map/ppermute | solution.py:26
  33.0 2.4 %collective-permute-done.11 = f32[32,16]{0,1:T(8,128)S(1)} collective-permute-done((f32[32,16]{0,1:T(8,128)S(1)}, f32[32,16]{0,1:T(8,128)S(1)}, u32[]{:S(2)}, u32[]{:S(2)}) %collective-permute-start.11) | collective-permute-done | bytes 2080 | tf_op jit(solution)/shard_map/ppermute | solution.py:26
  35.5 0.4 fusion.21
  36.0 1.2 collective-permute-start.6
  37.2 0.6 collective-permute-start.7
  37.9 2.1 %collective-permute-start.8 = (bf16[8,8192]{1,0:T(8,128)(2,1)S(1)}, bf16[8,8192]{1,0:T(8,128)(2,1)S(1)}, u32[]{:S(2)}, u32[]{:S(2)}) collective-permute-start(bf16[8,8192]{1,0:T(8,128)(2,1)S(1)} %bitcast.163), channel_id=1, source_target_pairs={{0,24},{8,0},{16,8},{24,16},{1,25},{9,1},{17,9},{25,17},{2,26},{10... | collective-permute-start | bytes 393224 | tf_op jit(solution)/shard_map/ppermute | solution.py:22
  40.7 5.9 %shard_map.125.refs_4_ = bf16[8192,1024]{1,0:T(8,128)(2,1)S(1)} custom-call(bf16[8192,1024]{1,0:T(8,128)(2,1)} %source_ref.1), custom_call_target="tpu_custom_call" | custom-call | bytes 33554432 | tf_op jit(solution)/shard_map/pallas_call | solution.py:133
  46.6 2.9 %collective-permute-done.7.refs_2_ = bf16[8,8192]{1,0:T(8,128)(2,1)S(1)} collective-permute-done((bf16[8,8192]{1,0:T(8,128)(2,1)S(1)}, bf16[8,8192]{1,0:T(8,128)(2,1)S(1)}, u32[]{:S(2)}, u32[]{:S(2)}) %collective-permute-start.7) | collective-permute-done | bytes 131104 | tf_op jit(solution)/shard_map/ppermute | solution.py:22
  49.5 3.1 %shard_map.126 = (bf16[32,1024]{1,0:T(8,128)(2,1)S(1)}, bf16[32,1152]{1,0:T(8,128)(2,1)S(1)}) custom-call(s32[1]{0:T(128)} %bitcast.place_ref, bf16[8,8192]{1,0:T(8,128)(2,1)S(1)} %bitcast.164, bf16[8,8192]{1,0:T(8,128)(2,1)S(1)} %collective-permute-done.6.refs_1_, bf16[8,8192]{1,0:T(8,128)(2,1)S(1)} %collective-permute-done.7.refs_2_, ...), custom_call_target="tpu_custom_call" | custom-call | flops 536870912 | bytes 16777216 | tf_op jit(solution)/shard_map/pallas_call | solution.py:214
  52.6 0.6 collective-permute-start.13
  53.1 0.4 collective-permute-start.14
  53.6 2.5 %collective-permute-start.15 = (bf16[32,1152]{1,0:T(8,128)(2,1)S(1)}, bf16[32,1152]{1,0:T(8,128)(2,1)S(1)}, u32[]{:S(2)}, u32[]{:S(2)}) collective-permute-start(bf16[32,1152]{1,0:T(8,128)(2,1)S(1)} %get-tuple-element.46), channel_id=1, source_target_pairs={{0,6},{1,7},{2,4},{3,5},{4,2},{5,3},{6,0},{7,1},{8,14},{9,15},{10,... | collective-permute-start | bytes 221192 | tf_op jit(solution)/shard_map/ppermute | solution.py:26
  56.1 1.4 %collective-permute-done.13 = bf16[32,1152]{1,0:T(8,128)(2,1)S(1)} collective-permute-done((bf16[32,1152]{1,0:T(8,128)(2,1)S(1)}, bf16[32,1152]{1,0:T(8,128)(2,1)S(1)}, u32[]{:S(2)}, u32[]{:S(2)}) %collective-permute-start.13) | collective-permute-done | bytes 73760 | tf_op jit(solution)/shard_map/ppermute | solution.py:26
  57.5 1.4 %collective-permute-done.14 = bf16[32,1152]{1,0:T(8,128)(2,1)S(1)} collective-permute-done((bf16[32,1152]{1,0:T(8,128)(2,1)S(1)}, bf16[32,1152]{1,0:T(8,128)(2,1)S(1)}, u32[]{:S(2)}, u32[]{:S(2)}) %collective-permute-start.14) | collective-permute-done | bytes 73760 | tf_op jit(solution)/shard_map/ppermute | solution.py:26
  59.2 1.5 %collective-permute-done.16.far_ref = bf16[128,1152]{1,0:T(8,128)(2,1)S(1)} collective-permute-done((bf16[128,1152]{1,0:T(8,128)(2,1)S(1)}, bf16[128,1152]{1,0:T(8,128)(2,1)S(1)}, u32[]{:S(2)}, u32[]{:S(2)}) %collective-permute-start.16) | collective-permute-done | bytes 294944 | tf_op jit(solution)/shard_map/ppermute | solution.py:26
  60.8 3.6 %shard_map.130 = (bf16[104,768]{1,0:T(8,128)(2,1)S(1)}, bf16[104,768]{1,0:T(8,128)(2,1)S(1)}, bf16[2,104,768]{2,1,0:T(8,128)(2,1)S(1)}) custom-call(s32[1]{0:T(128)} %bitcast.place_ref, bf16[104,256]{1,0:T(8,128)(2,1)S(1)} %get-tuple-element.82.pick_ref, bf16[128,1152]{1,0:T(8,128)(2,1)S(1)} %constant_dynamic-update-slice_fusion.2.near_ref, ...), custom_call_target="tpu_custom_call" | custom-call | flops 654311424 | bytes 6291456 | tf_op jit(solution)/shard_map/pallas_call | solution.py:345
  64.3 3.4 %collective-permute-start.25 = (bf16[2,104,768]{2,1,0:T(8,128)(2,1)S(1)}, bf16[2,104,768]{2,1,0:T(8,128)(2,1)S(1)}, u32[]{:S(2)}, u32[]{:S(2)}) collective-permute-start(bf16[2,104,768]{2,1,0:T(8,128)(2,1)S(1)} %get-tuple-element.58), channel_id=1, source_target_pairs={{0,8},{8,0},{16,24},{24,16},{1,9},{9,1},{17,25},{25,17},{2,10},{10... | collective-permute-start | bytes 958472 | tf_op jit(solution)/shard_map/ppermute | solution.py:26
  67.7 3.6 %shard_map.127 = (bf16[112,768]{1,0:T(8,128)(2,1)S(1)}, bf16[112,768]{1,0:T(8,128)(2,1)S(1)}, bf16[2,112,768]{2,1,0:T(8,128)(2,1)S(1)}) custom-call(s32[1]{0:T(128)} %bitcast.place_ref, bf16[104,256]{1,0:T(8,128)(2,1)S(1)} %get-tuple-element.84.pick_ref, bf16[128,1152]{1,0:T(8,128)(2,1)S(1)} %constant_dynamic-update-slice_fusion.2.near_ref, ...), custom_call_target="tpu_custom_call" | custom-call | flops 654311424 | bytes 6291456 | tf_op jit(solution)/shard_map/pallas_call | solution.py:345
  71.4 2.8 %shard_map.128.weight_ref = bf16[1024,3072]{1,0:T(8,128)(2,1)S(1)} custom-call(bf16[3,1024,3072]{2,1,0:T(8,128)(2,1)} %weight_ref.3), custom_call_target="tpu_custom_call" | custom-call | bytes 12582912 | tf_op jit(solution)/shard_map/pallas_call | solution.py:311
  74.2 1.4 %shard_map.129 = (bf16[104,768]{1,0:T(8,128)(2,1)S(1)}, bf16[104,768]{1,0:T(8,128)(2,1)S(1)}, bf16[2,104,768]{2,1,0:T(8,128)(2,1)S(1)}) custom-call(s32[1]{0:T(128)} %bitcast.place_ref, bf16[104,256]{1,0:T(8,128)(2,1)S(1)} %get-tuple-element.83.pick_ref, bf16[128,1152]{1,0:T(8,128)(2,1)S(1)} %constant_dynamic-update-slice_fusion.2.near_ref, ...), custom_call_target="tpu_custom_call" | custom-call | flops 654311424 | bytes 6291456 | tf_op jit(solution)/shard_map/pallas_call | solution.py:291
  75.6 2.1 %collective-permute-start.21 = (bf16[2,104,768]{2,1,0:T(8,128)(2,1)S(1)}, bf16[2,104,768]{2,1,0:T(8,128)(2,1)S(1)}, u32[]{:S(2)}, u32[]{:S(2)}) collective-permute-start(bf16[2,104,768]{2,1,0:T(8,128)(2,1)S(1)} %get-tuple-element.54), channel_id=1, source_target_pairs={{0,8},{8,0},{16,24},{24,16},{1,9},{9,1},{17,25},{25,17},{2,10},{10... | collective-permute-start | bytes 958472 | tf_op jit(solution)/shard_map/ppermute | solution.py:26
  78.0 8.8 %collective-permute-done.17 = bf16[2,112,768]{2,1,0:T(8,128)(2,1)S(1)} collective-permute-done((bf16[2,112,768]{2,1,0:T(8,128)(2,1)S(1)}, bf16[2,112,768]{2,1,0:T(8,128)(2,1)S(1)}, u32[]{:S(2)}, u32[]{:S(2)}) %collective-permute-start.17) | collective-permute-done | bytes 344096 | tf_op jit(solution)/shard_map/ppermute | solution.py:26
  87.0 6.9 %collective-permute-done.21 = bf16[2,104,768]{2,1,0:T(8,128)(2,1)S(1)} collective-permute-done((bf16[2,104,768]{2,1,0:T(8,128)(2,1)S(1)}, bf16[2,104,768]{2,1,0:T(8,128)(2,1)S(1)}, u32[]{:S(2)}, u32[]{:S(2)}) %collective-permute-start.21) | collective-permute-done | bytes 319520 | tf_op jit(solution)/shard_map/ppermute | solution.py:26
  93.9 6.2 %collective-permute-done.18 = bf16[1,112,768]{2,1,0:T(8,128)(2,1)S(1)} collective-permute-done((bf16[1,112,768]{2,1,0:T(8,128)(2,1)S(1)}, bf16[1,112,768]{2,1,0:T(8,128)(2,1)S(1)}, u32[]{:S(2)}, u32[]{:S(2)}) %collective-permute-start.18) | collective-permute-done | bytes 172064 | tf_op jit(solution)/shard_map/ppermute | solution.py:26
  100.7 2.9 %collective-permute-start.22 = (bf16[1,104,768]{2,1,0:T(8,128)(2,1)S(1)}, bf16[1,104,768]{2,1,0:T(8,128)(2,1)S(1)}, u32[]{:S(2)}, u32[]{:S(2)}) collective-permute-start(bf16[1,104,768]{2,1,0:T(8,128)(2,1)S(1)} %fusion.9), channel_id=1, source_target_pairs={{0,16},{8,24},{16,0},{24,8},{1,17},{9,25},{17,1},{25,9},{2,18},{10... | collective-permute-start | bytes 479240 | tf_op jit(solution)/shard_map/ppermute | solution.py:26
  103.9 3.5 %collective-permute-done.19 = bf16[1,104,384]{2,1,0:T(8,128)(2,1)S(1)} collective-permute-done((bf16[1,104,384]{2,1,0:T(8,128)(2,1)S(1)}, bf16[1,104,384]{2,1,0:T(8,128)(2,1)S(1)}, u32[]{:S(2)}, u32[]{:S(2)}) %collective-permute-start.19) | collective-permute-done | bytes 79904 | tf_op jit(solution)/shard_map/ppermute | solution.py:26
  107.5 3.1 %collective-permute-start.20 = (bf16[2,104,384]{2,1,0:T(8,128)(2,1)S(1)}, bf16[2,104,384]{2,1,0:T(8,128)(2,1)S(1)}, u32[]{:S(2)}, u32[]{:S(2)}) collective-permute-start(bf16[2,104,384]{2,1,0:T(8,128)(2,1)S(1)} %pad_maximum_fusion.refs_0_), channel_id=1, source_target_pairs={{0,8},{8,0},{16,24},{24,16},{1,9},{9,1},{17,25},{25,17},{2,10},{10... | collective-permute-start | bytes 479240 | tf_op jit(solution)/shard_map/ppermute | solution.py:26
  110.6 3.8 %collective-permute-done.22 = bf16[1,104,768]{2,1,0:T(8,128)(2,1)S(1)} collective-permute-done((bf16[1,104,768]{2,1,0:T(8,128)(2,1)S(1)}, bf16[1,104,768]{2,1,0:T(8,128)(2,1)S(1)}, u32[]{:S(2)}, u32[]{:S(2)}) %collective-permute-start.22) | collective-permute-done | bytes 159776 | tf_op jit(solution)/shard_map/ppermute | solution.py:26
  114.9 1.1 collective-permute-done.27
  116.0 1.8 %collective-permute-start.28 = (bf16[2,104,384]{2,1,0:T(8,128)(2,1)S(1)}, bf16[2,104,384]{2,1,0:T(8,128)(2,1)S(1)}, u32[]{:S(2)}, u32[]{:S(2)}) collective-permute-start(bf16[2,104,384]{2,1,0:T(8,128)(2,1)S(1)} %pad_maximum_fusion.2.refs_4_), channel_id=1, source_target_pairs={{0,8},{8,0},{16,24},{24,16},{1,9},{9,1},{17,25},{25,17},{2,10},{10... | collective-permute-start | bytes 479240 | tf_op jit(solution)/shard_map/ppermute | solution.py:26
  117.8 3.0 %collective-permute-done.23 = bf16[1,104,384]{2,1,0:T(8,128)(2,1)S(1)} collective-permute-done((bf16[1,104,384]{2,1,0:T(8,128)(2,1)S(1)}, bf16[1,104,384]{2,1,0:T(8,128)(2,1)S(1)}, u32[]{:S(2)}, u32[]{:S(2)}) %collective-permute-start.23) | collective-permute-done | bytes 79904 | tf_op jit(solution)/shard_map/ppermute | solution.py:26
  120.8 0.4 collective-permute-start.24
  121.2 3.8 %shard_map.131.refs_7_ = bf16[3,1536,1024]{2,1,0:T(8,128)(2,1)S(1)} custom-call(bf16[3,1536,1024]{2,1,0:T(8,128)(2,1)} %source_ref.3), custom_call_target="tpu_custom_call" | custom-call | bytes 18874368 | tf_op jit(solution)/shard_map/pallas_call | solution.py:133
  125.0 1.1 collective-permute-done.24.refs_3_
  126.2 2.3 %shard_map.132 = (f32[128,1024]{1,0:T(8,128)S(1)}, bf16[128,1024]{1,0:T(8,128)(2,1)S(1)}) custom-call(s32[1]{0:T(128)} %bitcast.place_ref, bf16[2,104,384]{2,1,0:T(8,128)(2,1)S(1)} %pad_maximum_fusion.refs_0_, bf16[2,104,384]{2,1,0:T(8,128)(2,1)S(1)} %collective-permute-done.20.refs_1_, bf16[2,104,384]{2,1,0:T(8,128)(2,1)S(1)} %pad_maximum_fusion.1.refs_2_, ...), custom_call_target="tpu_custom_call" | custom-call | flops 981467136 | bytes 9437184 | tf_op jit(solution)/shard_map/pallas_call | solution.py:441
  128.6 1.5 %collective-permute-done.29 = bf16[4,32,1024]{2,1,0:T(8,128)(2,1)S(1)} collective-permute-done((bf16[4,32,1024]{2,1,0:T(8,128)(2,1)S(1)}, bf16[4,32,1024]{2,1,0:T(8,128)(2,1)S(1)}, u32[]{:S(2)}, u32[]{:S(2)}) %collective-permute-start.29) | collective-permute-done | bytes 262176 | tf_op jit(solution)/shard_map/ppermute | solution.py:26
  130.2 2.3 %collective-permute-start.32 = (bf16[32,1024]{1,0:T(8,128)(2,1)S(1)}, bf16[32,1024]{1,0:T(8,128)(2,1)S(1)}, u32[]{:S(2)}, u32[]{:S(2)}) collective-permute-start(bf16[32,1024]{1,0:T(8,128)(2,1)S(1)} %get-tuple-element.80), channel_id=1, source_target_pairs={{0,6},{1,7},{2,4},{3,5},{4,2},{5,3},{6,0},{7,1},{8,14},{9,15},{10,... | collective-permute-start | bytes 196616 | tf_op jit(solution)/shard_map/ppermute | solution.py:26
  132.5 0.5 collective-permute-start.31
  133.0 0.7 collective-permute-start.30
  133.7 0.7 copy.48
  134.4 1.0 collective-permute-done.32
  135.5 1.4 collective-permute-done.31
  136.8 0.4 collective-permute-done.30
  137.3 0.7 copy.38
  (88 shorter events, 4.0 us)
Async XLA Ops:
  1.6 11.9 %collective-permute-start = (bf16[8,64,128]{2,1,0:T(8,128)(2,1)S(1)}, bf16[8,64,128]{2,1,0:T(8,128)(2,1)S(1)}, u32[]{:S(2)}, u32[]{:S(2)}) collective-permute-start(bf16[8,64,128]{2,1,0:T(8,128)(2,1)S(1)} %bitcast.167), channel_id=1, source_target_pairs={{0,8},{8,16},{16,24},{24,0},{1,9},{9,17},{17,25},{25,1},{2,10},{10... | collective-permute-start | bytes 393224 | tf_op jit(solution)/shard_map/ppermute | solution.py:22
  4.6 11.2 %collective-permute-start.1 = (bf16[8,64,128]{2,1,0:T(8,128)(2,1)S(1)}, bf16[8,64,128]{2,1,0:T(8,128)(2,1)S(1)}, u32[]{:S(2)}, u32[]{:S(2)}) collective-permute-start(bf16[8,64,128]{2,1,0:T(8,128)(2,1)S(1)} %bitcast.168), channel_id=1, source_target_pairs={{0,16},{8,24},{16,0},{24,8},{1,17},{9,25},{17,1},{25,9},{2,18},{10... | collective-permute-start | bytes 393224 | tf_op jit(solution)/shard_map/ppermute | solution.py:22
  7.2 8.6 %collective-permute-start.2 = (bf16[8,64,128]{2,1,0:T(8,128)(2,1)S(1)}, bf16[8,64,128]{2,1,0:T(8,128)(2,1)S(1)}, u32[]{:S(2)}, u32[]{:S(2)}) collective-permute-start(bf16[8,64,128]{2,1,0:T(8,128)(2,1)S(1)} %bitcast.169), channel_id=1, source_target_pairs={{0,24},{8,0},{16,8},{24,16},{1,25},{9,1},{17,9},{25,17},{2,26},{10... | collective-permute-start | bytes 393224 | tf_op jit(solution)/shard_map/ppermute | solution.py:22
  8.6 1.0 copy-start
  9.6 0.7 copy-start.2
  17.2 8.9 %collective-permute-start.5 = (bf16[9,64,128]{2,1,0:T(8,128)(2,1)S(1)}, bf16[9,64,128]{2,1,0:T(8,128)(2,1)S(1)}, u32[]{:S(2)}, u32[]{:S(2)}) collective-permute-start(bf16[9,64,128]{2,1,0:T(8,128)(2,1)S(1)} %get-tuple-element.39), channel_id=1, source_target_pairs={{0,8},{8,16},{16,24},{24,0},{1,9},{9,17},{17,25},{25,1},{2,10},{10... | collective-permute-start | bytes 442376 | tf_op jit(solution)/shard_map/ppermute | solution.py:22
  20.5 10.8 %collective-permute-start.4 = (bf16[9,64,128]{2,1,0:T(8,128)(2,1)S(1)}, bf16[9,64,128]{2,1,0:T(8,128)(2,1)S(1)}, u32[]{:S(2)}, u32[]{:S(2)}) collective-permute-start(bf16[9,64,128]{2,1,0:T(8,128)(2,1)S(1)} %get-tuple-element.38), channel_id=1, source_target_pairs={{0,16},{8,24},{16,0},{24,8},{1,17},{9,25},{17,1},{25,9},{2,18},{10... | collective-permute-start | bytes 442376 | tf_op jit(solution)/shard_map/ppermute | solution.py:22
  22.1 9.2 %collective-permute-start.3 = (bf16[9,64,128]{2,1,0:T(8,128)(2,1)S(1)}, bf16[9,64,128]{2,1,0:T(8,128)(2,1)S(1)}, u32[]{:S(2)}, u32[]{:S(2)}) collective-permute-start(bf16[9,64,128]{2,1,0:T(8,128)(2,1)S(1)} %get-tuple-element.37), channel_id=1, source_target_pairs={{0,24},{8,0},{16,8},{24,16},{1,25},{9,1},{17,9},{25,17},{2,26},{10... | collective-permute-start | bytes 442376 | tf_op jit(solution)/shard_map/ppermute | solution.py:22
  27.8 3.7 %collective-permute-start.9 = (f32[32,16]{0,1:T(8,128)S(1)}, f32[32,16]{0,1:T(8,128)S(1)}, u32[]{:S(2)}, u32[]{:S(2)}) collective-permute-start(f32[32,16]{0,1:T(8,128)S(1)} %constant_dynamic-update-slice_fusion), channel_id=1, source_target_pairs={{0,2},{1,3},{2,0},{3,1},{4,6},{5,7},{6,4},{7,5},{8,10},{9,11},{10,... | collective-permute-start | bytes 6152 | tf_op jit(solution)/shard_map/ppermute | solution.py:26
  29.3 3.7 %collective-permute-start.10 = (f32[32,16]{0,1:T(8,128)S(1)}, f32[32,16]{0,1:T(8,128)S(1)}, u32[]{:S(2)}, u32[]{:S(2)}) collective-permute-start(f32[32,16]{0,1:T(8,128)S(1)} %constant_dynamic-update-slice_fusion), channel_id=1, source_target_pairs={{0,4},{1,5},{2,6},{3,7},{4,0},{5,1},{6,2},{7,3},{8,12},{9,13},{10,... | collective-permute-start | bytes 6152 | tf_op jit(solution)/shard_map/ppermute | solution.py:26
  30.8 4.5 %collective-permute-start.11 = (f32[32,16]{0,1:T(8,128)S(1)}, f32[32,16]{0,1:T(8,128)S(1)}, u32[]{:S(2)}, u32[]{:S(2)}) collective-permute-start(f32[32,16]{0,1:T(8,128)S(1)} %constant_dynamic-update-slice_fusion), channel_id=1, source_target_pairs={{0,6},{1,7},{2,4},{3,5},{4,2},{5,3},{6,0},{7,1},{8,14},{9,15},{10,... | collective-permute-start | bytes 6152 | tf_op jit(solution)/shard_map/ppermute | solution.py:26
  35.5 4.5 %collective-permute-start.12 = (f32[128,16]{0,1:T(8,128)S(1)}, f32[128,16]{0,1:T(8,128)S(1)}, u32[]{:S(2)}, u32[]{:S(2)}) collective-permute-start(f32[128,16]{0,1:T(8,128)S(1)} %pad_maximum_fusion.3), channel_id=1, source_target_pairs={{0,1},{1,0},{2,3},{3,2},{4,5},{5,4},{6,7},{7,6},{8,9},{9,8},{10,11... | collective-permute-start | bytes 24584 | tf_op jit(solution)/shard_map/ppermute | solution.py:26
  36.0 10.6 %collective-permute-start.6 = (bf16[8,8192]{1,0:T(8,128)(2,1)S(1)}, bf16[8,8192]{1,0:T(8,128)(2,1)S(1)}, u32[]{:S(2)}, u32[]{:S(2)}) collective-permute-start(bf16[8,8192]{1,0:T(8,128)(2,1)S(1)} %bitcast.161), channel_id=1, source_target_pairs={{0,8},{8,16},{16,24},{24,0},{1,9},{9,17},{17,25},{25,1},{2,10},{10... | collective-permute-start | bytes 393224 | tf_op jit(solution)/shard_map/ppermute | solution.py:22
  37.2 12.3 %collective-permute-start.7 = (bf16[8,8192]{1,0:T(8,128)(2,1)S(1)}, bf16[8,8192]{1,0:T(8,128)(2,1)S(1)}, u32[]{:S(2)}, u32[]{:S(2)}) collective-permute-start(bf16[8,8192]{1,0:T(8,128)(2,1)S(1)} %bitcast.162), channel_id=1, source_target_pairs={{0,16},{8,24},{16,0},{24,8},{1,17},{9,25},{17,1},{25,9},{2,18},{10... | collective-permute-start | bytes 393224 | tf_op jit(solution)/shard_map/ppermute | solution.py:22
  37.9 11.6 %collective-permute-start.8 = (bf16[8,8192]{1,0:T(8,128)(2,1)S(1)}, bf16[8,8192]{1,0:T(8,128)(2,1)S(1)}, u32[]{:S(2)}, u32[]{:S(2)}) collective-permute-start(bf16[8,8192]{1,0:T(8,128)(2,1)S(1)} %bitcast.163), channel_id=1, source_target_pairs={{0,24},{8,0},{16,8},{24,16},{1,25},{9,1},{17,9},{25,17},{2,26},{10... | collective-permute-start | bytes 393224 | tf_op jit(solution)/shard_map/ppermute | solution.py:22
  40.7 8.8 %copy-start.1 = (f32[1024]{0:T(1024)S(1)}, f32[1024]{0:T(1024)}, u32[]{:S(2)}) copy-start(f32[1024]{0:T(1024)} %param.17) | copy-start | bytes 12292
  52.6 4.9 %collective-permute-start.13 = (bf16[32,1152]{1,0:T(8,128)(2,1)S(1)}, bf16[32,1152]{1,0:T(8,128)(2,1)S(1)}, u32[]{:S(2)}, u32[]{:S(2)}) collective-permute-start(bf16[32,1152]{1,0:T(8,128)(2,1)S(1)} %get-tuple-element.46), channel_id=1, source_target_pairs={{0,2},{1,3},{2,0},{3,1},{4,6},{5,7},{6,4},{7,5},{8,10},{9,11},{10,... | collective-permute-start | bytes 221192 | tf_op jit(solution)/shard_map/ppermute | solution.py:26
  53.1 5.8 %collective-permute-start.14 = (bf16[32,1152]{1,0:T(8,128)(2,1)S(1)}, bf16[32,1152]{1,0:T(8,128)(2,1)S(1)}, u32[]{:S(2)}, u32[]{:S(2)}) collective-permute-start(bf16[32,1152]{1,0:T(8,128)(2,1)S(1)} %get-tuple-element.46), channel_id=1, source_target_pairs={{0,4},{1,5},{2,6},{3,7},{4,0},{5,1},{6,2},{7,3},{8,12},{9,13},{10,... | collective-permute-start | bytes 221192 | tf_op jit(solution)/shard_map/ppermute | solution.py:26
  53.6 5.4 %collective-permute-start.15 = (bf16[32,1152]{1,0:T(8,128)(2,1)S(1)}, bf16[32,1152]{1,0:T(8,128)(2,1)S(1)}, u32[]{:S(2)}, u32[]{:S(2)}) collective-permute-start(bf16[32,1152]{1,0:T(8,128)(2,1)S(1)} %get-tuple-element.46), channel_id=1, source_target_pairs={{0,6},{1,7},{2,4},{3,5},{4,2},{5,3},{6,0},{7,1},{8,14},{9,15},{10,... | collective-permute-start | bytes 221192 | tf_op jit(solution)/shard_map/ppermute | solution.py:26
  59.0 1.6 %collective-permute-start.16 = (bf16[128,1152]{1,0:T(8,128)(2,1)S(1)}, bf16[128,1152]{1,0:T(8,128)(2,1)S(1)}, u32[]{:S(2)}, u32[]{:S(2)}) collective-permute-start(bf16[128,1152]{1,0:T(8,128)(2,1)S(1)} %constant_dynamic-update-slice_fusion.2.near_ref), channel_id=1, source_target_pairs={{0,1},{1,0},{2,3},{3,2},{4,5},{5,4},{6,7},{7,6},{8,9},{9,8},{10,11... | collective-permute-start | bytes 884744 | tf_op jit(solution)/shard_map/ppermute | solution.py:26
  64.3 13.3 %collective-permute-start.25 = (bf16[2,104,768]{2,1,0:T(8,128)(2,1)S(1)}, bf16[2,104,768]{2,1,0:T(8,128)(2,1)S(1)}, u32[]{:S(2)}, u32[]{:S(2)}) collective-permute-start(bf16[2,104,768]{2,1,0:T(8,128)(2,1)S(1)} %get-tuple-element.58), channel_id=1, source_target_pairs={{0,8},{8,0},{16,24},{24,16},{1,9},{9,1},{17,25},{25,17},{2,10},{10... | collective-permute-start | bytes 958472 | tf_op jit(solution)/shard_map/ppermute | solution.py:26
  71.3 15.5 %collective-permute-start.17 = (bf16[2,112,768]{2,1,0:T(8,128)(2,1)S(1)}, bf16[2,112,768]{2,1,0:T(8,128)(2,1)S(1)}, u32[]{:S(2)}, u32[]{:S(2)}) collective-permute-start(bf16[2,112,768]{2,1,0:T(8,128)(2,1)S(1)} %get-tuple-element.48), channel_id=1, source_target_pairs={{0,8},{8,0},{16,24},{24,16},{1,9},{9,1},{17,25},{25,17},{2,10},{10... | collective-permute-start | bytes 1032200 | tf_op jit(solution)/shard_map/ppermute | solution.py:26
  75.6 18.3 %collective-permute-start.21 = (bf16[2,104,768]{2,1,0:T(8,128)(2,1)S(1)}, bf16[2,104,768]{2,1,0:T(8,128)(2,1)S(1)}, u32[]{:S(2)}, u32[]{:S(2)}) collective-permute-start(bf16[2,104,768]{2,1,0:T(8,128)(2,1)S(1)} %get-tuple-element.54), channel_id=1, source_target_pairs={{0,8},{8,0},{16,24},{24,16},{1,9},{9,1},{17,25},{25,17},{2,10},{10... | collective-permute-start | bytes 958472 | tf_op jit(solution)/shard_map/ppermute | solution.py:26
  77.7 25.9 %collective-permute-start.26 = (bf16[1,104,768]{2,1,0:T(8,128)(2,1)S(1)}, bf16[1,104,768]{2,1,0:T(8,128)(2,1)S(1)}, u32[]{:S(2)}, u32[]{:S(2)}) collective-permute-start(bf16[1,104,768]{2,1,0:T(8,128)(2,1)S(1)} %fusion.10), channel_id=1, source_target_pairs={{0,16},{8,24},{16,0},{24,8},{1,17},{9,25},{17,1},{25,9},{2,18},{10... | collective-permute-start | bytes 479240 | tf_op jit(solution)/shard_map/ppermute | solution.py:26
  86.9 13.3 %collective-permute-start.18 = (bf16[1,112,768]{2,1,0:T(8,128)(2,1)S(1)}, bf16[1,112,768]{2,1,0:T(8,128)(2,1)S(1)}, u32[]{:S(2)}, u32[]{:S(2)}) collective-permute-start(bf16[1,112,768]{2,1,0:T(8,128)(2,1)S(1)} %fusion.7), channel_id=1, source_target_pairs={{0,16},{8,24},{16,0},{24,8},{1,17},{9,25},{17,1},{25,9},{2,18},{10... | collective-permute-start | bytes 516104 | tf_op jit(solution)/shard_map/ppermute | solution.py:26
  100.6 6.8 %collective-permute-start.19 = (bf16[1,104,384]{2,1,0:T(8,128)(2,1)S(1)}, bf16[1,104,384]{2,1,0:T(8,128)(2,1)S(1)}, u32[]{:S(2)}, u32[]{:S(2)}) collective-permute-start(bf16[1,104,384]{2,1,0:T(8,128)(2,1)S(1)} %fusion.53), channel_id=1, source_target_pairs={{0,16},{8,24},{16,0},{24,8},{1,17},{9,25},{17,1},{25,9},{2,18},{10... | collective-permute-start | bytes 239624 | tf_op jit(solution)/shard_map/ppermute | solution.py:26
  100.7 13.7 %collective-permute-start.22 = (bf16[1,104,768]{2,1,0:T(8,128)(2,1)S(1)}, bf16[1,104,768]{2,1,0:T(8,128)(2,1)S(1)}, u32[]{:S(2)}, u32[]{:S(2)}) collective-permute-start(bf16[1,104,768]{2,1,0:T(8,128)(2,1)S(1)} %fusion.9), channel_id=1, source_target_pairs={{0,16},{8,24},{16,0},{24,8},{1,17},{9,25},{17,1},{25,9},{2,18},{10... | collective-permute-start | bytes 479240 | tf_op jit(solution)/shard_map/ppermute | solution.py:26
  103.8 12.2 %collective-permute-start.27 = (bf16[1,104,384]{2,1,0:T(8,128)(2,1)S(1)}, bf16[1,104,384]{2,1,0:T(8,128)(2,1)S(1)}, u32[]{:S(2)}, u32[]{:S(2)}) collective-permute-start(bf16[1,104,384]{2,1,0:T(8,128)(2,1)S(1)} %fusion.23), channel_id=1, source_target_pairs={{0,16},{8,24},{16,0},{24,8},{1,17},{9,25},{17,1},{25,9},{2,18},{10... | collective-permute-start | bytes 239624 | tf_op jit(solution)/shard_map/ppermute | solution.py:26
  107.5 17.5 %collective-permute-start.20 = (bf16[2,104,384]{2,1,0:T(8,128)(2,1)S(1)}, bf16[2,104,384]{2,1,0:T(8,128)(2,1)S(1)}, u32[]{:S(2)}, u32[]{:S(2)}) collective-permute-start(bf16[2,104,384]{2,1,0:T(8,128)(2,1)S(1)} %pad_maximum_fusion.refs_0_), channel_id=1, source_target_pairs={{0,8},{8,0},{16,24},{24,16},{1,9},{9,1},{17,25},{25,17},{2,10},{10... | collective-permute-start | bytes 479240 | tf_op jit(solution)/shard_map/ppermute | solution.py:26
  114.6 6.2 %collective-permute-start.23 = (bf16[1,104,384]{2,1,0:T(8,128)(2,1)S(1)}, bf16[1,104,384]{2,1,0:T(8,128)(2,1)S(1)}, u32[]{:S(2)}, u32[]{:S(2)}) collective-permute-start(bf16[1,104,384]{2,1,0:T(8,128)(2,1)S(1)} %fusion.22), channel_id=1, source_target_pairs={{0,16},{8,24},{16,0},{24,8},{1,17},{9,25},{17,1},{25,9},{2,18},{10... | collective-permute-start | bytes 239624 | tf_op jit(solution)/shard_map/ppermute | solution.py:26
  116.0 9.0 %collective-permute-start.28 = (bf16[2,104,384]{2,1,0:T(8,128)(2,1)S(1)}, bf16[2,104,384]{2,1,0:T(8,128)(2,1)S(1)}, u32[]{:S(2)}, u32[]{:S(2)}) collective-permute-start(bf16[2,104,384]{2,1,0:T(8,128)(2,1)S(1)} %pad_maximum_fusion.2.refs_4_), channel_id=1, source_target_pairs={{0,8},{8,0},{16,24},{24,16},{1,9},{9,1},{17,25},{25,17},{2,10},{10... | collective-permute-start | bytes 479240 | tf_op jit(solution)/shard_map/ppermute | solution.py:26
  120.8 5.3 %collective-permute-start.24 = (bf16[2,104,384]{2,1,0:T(8,128)(2,1)S(1)}, bf16[2,104,384]{2,1,0:T(8,128)(2,1)S(1)}, u32[]{:S(2)}, u32[]{:S(2)}) collective-permute-start(bf16[2,104,384]{2,1,0:T(8,128)(2,1)S(1)} %pad_maximum_fusion.1.refs_2_), channel_id=1, source_target_pairs={{0,8},{8,0},{16,24},{24,16},{1,9},{9,1},{17,25},{25,17},{2,10},{10... | collective-permute-start | bytes 479240 | tf_op jit(solution)/shard_map/ppermute | solution.py:26
  128.5 1.6 %collective-permute-start.29 = (bf16[4,32,1024]{2,1,0:T(8,128)(2,1)S(1)}, bf16[4,32,1024]{2,1,0:T(8,128)(2,1)S(1)}, u32[]{:S(2)}, u32[]{:S(2)}) collective-permute-start(bf16[4,32,1024]{2,1,0:T(8,128)(2,1)S(1)} %bitcast.176), channel_id=1, source_target_pairs={{0,1},{1,0},{2,3},{3,2},{4,5},{5,4},{6,7},{7,6},{8,9},{9,8},{10,11... | collective-permute-start | bytes 786440 | tf_op jit(solution)/shard_map/ppermute | solution.py:26
  130.2 5.3 %collective-permute-start.32 = (bf16[32,1024]{1,0:T(8,128)(2,1)S(1)}, bf16[32,1024]{1,0:T(8,128)(2,1)S(1)}, u32[]{:S(2)}, u32[]{:S(2)}) collective-permute-start(bf16[32,1024]{1,0:T(8,128)(2,1)S(1)} %get-tuple-element.80), channel_id=1, source_target_pairs={{0,6},{1,7},{2,4},{3,5},{4,2},{5,3},{6,0},{7,1},{8,14},{9,15},{10,... | collective-permute-start | bytes 196616 | tf_op jit(solution)/shard_map/ppermute | solution.py:26
  132.5 4.4 %collective-permute-start.31 = (bf16[32,1024]{1,0:T(8,128)(2,1)S(1)}, bf16[32,1024]{1,0:T(8,128)(2,1)S(1)}, u32[]{:S(2)}, u32[]{:S(2)}) collective-permute-start(bf16[32,1024]{1,0:T(8,128)(2,1)S(1)} %get-tuple-element.81), channel_id=1, source_target_pairs={{0,4},{1,5},{2,6},{3,7},{4,0},{5,1},{6,2},{7,3},{8,12},{9,13},{10,... | collective-permute-start | bytes 196616 | tf_op jit(solution)/shard_map/ppermute | solution.py:26
  133.0 4.3 %collective-permute-start.30 = (bf16[32,1024]{1,0:T(8,128)(2,1)S(1)}, bf16[32,1024]{1,0:T(8,128)(2,1)S(1)}, u32[]{:S(2)}, u32[]{:S(2)}) collective-permute-start(bf16[32,1024]{1,0:T(8,128)(2,1)S(1)} %get-tuple-element.79), channel_id=1, source_target_pairs={{0,2},{1,3},{2,0},{3,1},{4,6},{5,7},{6,4},{7,5},{8,10},{9,11},{10,... | collective-permute-start | bytes 196616 | tf_op jit(solution)/shard_map/ppermute | solution.py:26
